TPU v7x, 128 devices: a whole 4x4x4 slice. The times are simulated.
128 devices in a mesh: ctx: 32 (over x, z, core), exp: 4 (over y).
Axes of the slice: x: 4, y: 4, z: 4, core: 2. Of those that a mesh axis runs over, the one named last changes fastest.
Arguments:
- tokens: bfloat16 [65536, 1280], P('ctx'), may hold values from -40 to 40
- slot_weight: bfloat16 [1280, 256], replicated, may hold values from -0.5 to 0.5
- w_in: bfloat16 [128, 1280, 2560], P(('ctx', 'exp')), may hold values from -0.15625 to 0.15625
- w_out: bfloat16 [128, 2560, 1280], P(('ctx', 'exp')), may hold values from -0.125 to 0.125
- cotangent: bfloat16 [65536, 1280], P(('ctx', 'exp')), may hold values from -24 to 24
Outputs:
- mixed_out: bfloat16 [65536, 1280], P(('ctx', 'exp'))
- token_grad: bfloat16 [65536, 1280], P(('ctx', 'exp'))
All inputs are finite; a program needn't handle non-finite values.
Results may differ from a plain program's by a relative error of at most 0.034.
Values may be sent and summed in bfloat16 or wider, within the bound.
No kernel may reach another device: no remote copies, remote signals or barrier semaphores. Data moves between devices by JAX's collectives and lax.ppermute only.
A program may use at most 128 MiB of HBM per device.

v0:
```python
import jax
import jax.numpy as jnp
from jax import lax
from jax.sharding import PartitionSpec as P


def inner_rows(left_rows, right_rows):
    return lax.dot_general(
        left_rows, right_rows, (((1,), (1,)), ((), ())), preferred_element_type=jnp.float32
    )


def inner_cols(left_rows, right_rows):
    return lax.dot_general(
        left_rows, right_rows, (((0,), (0,)), ((), ())), preferred_element_type=jnp.float32
    )


def shards(tokens, slot_weight, w_in, w_out, cotangent):
    ctx_count = lax.axis_size("ctx")
    exp_count = lax.axis_size("exp")
    ctx_index = lax.axis_index("ctx")
    exp_index = lax.axis_index("exp")
    model_width = tokens.shape[1]
    row_count = cotangent.shape[0]
    grouped = slot_weight.reshape(model_width, ctx_count, exp_count, 2)
    quarter_weight = lax.dynamic_index_in_dim(grouped, exp_index, 2, keepdims=False).reshape(
        model_width, 2 * ctx_count
    )
    logits = jnp.dot(tokens, quarter_weight, preferred_element_type=jnp.float32)
    local_max = jnp.max(logits, axis=0)
    shifted = jnp.exp(logits - local_max[None, :])
    local_totals = jnp.sum(shifted, axis=0)
    shifted_low = shifted.astype(jnp.bfloat16)
    highest = lax.pmax(local_max, "ctx")
    rescale = jnp.exp(local_max - highest)
    totals = lax.psum(local_totals * rescale, "ctx")
    columns = shifted_low
    own_sum = lax.psum_scatter(
        inner_cols(columns, tokens) * rescale[:, None], "ctx", scatter_dimension=0, tiled=True
    )
    own_totals = lax.dynamic_slice_in_dim(totals, 2 * ctx_index, 2, 0)
    slot_exact = own_sum / own_totals[:, None]
    slot_low = slot_exact.astype(jnp.bfloat16)
    preact = jnp.dot(slot_low, w_in[0], preferred_element_type=jnp.float32)
    hidden = jax.nn.gelu(preact).astype(jnp.bfloat16)
    slot_out = jnp.dot(hidden, w_out[0], preferred_element_type=jnp.float32).astype(jnp.bfloat16)
    all_out = lax.all_gather(slot_out, ("ctx", "exp"), axis=0, tiled=True)
    own_rows = lax.dynamic_slice_in_dim(tokens, exp_index * row_count, row_count, 0)
    comb_logits = jnp.dot(own_rows, slot_weight, preferred_element_type=jnp.float32)
    combine = jax.nn.softmax(comb_logits, axis=1)
    combine_low = combine.astype(jnp.bfloat16)
    mixed_out = jnp.dot(combine_low, all_out, preferred_element_type=jnp.float32).astype(
        jnp.bfloat16
    )
    comb_grad = inner_rows(cotangent, all_out)
    logit_comb = combine * (comb_grad - jnp.sum(combine * comb_grad, axis=1, keepdims=True))
    columns = combine_low
    out_grad = lax.psum_scatter(
        inner_cols(columns, cotangent), ("ctx", "exp"), scatter_dimension=0, tiled=True
    )
    hid_grad = inner_rows(out_grad.astype(jnp.bfloat16), w_out[0])
    pullback = jax.vjp(jax.nn.gelu, preact)[1]
    pre_grad = pullback(hid_grad)[0].astype(jnp.bfloat16)
    in_grad = inner_rows(pre_grad, w_in[0])
    own_product = jnp.sum(slot_exact * in_grad, axis=1)
    dispatch = jnp.exp(logits - highest[None, :]) / totals[None, :]
    dispatch_low = dispatch.astype(jnp.bfloat16)
    every_grad, every_product = (
        lax.all_gather(in_grad, ("ctx", "exp"), axis=0, tiled=True),
        lax.all_gather(own_product, ("ctx", "exp"), axis=0, tiled=True),
    )
    grad_groups = every_grad.reshape(ctx_count, exp_count, 2, model_width)
    quarter_grad = lax.dynamic_index_in_dim(grad_groups, exp_index, 1, keepdims=False).reshape(
        2 * ctx_count, model_width
    )
    product_groups = every_product.reshape(ctx_count, exp_count, 2)
    quarter_product = lax.dynamic_index_in_dim(
        product_groups, exp_index, 1, keepdims=False
    ).reshape(2 * ctx_count)
    quarter_low = quarter_grad.astype(jnp.bfloat16)
    logit_disp = (dispatch * (inner_rows(tokens, quarter_low) - quarter_product[None, :])).astype(
        jnp.bfloat16
    )
    sent_grad, sent_weight = (
        lax.all_to_all(logit_disp, "exp", split_axis=0, concat_axis=1, tiled=True),
        lax.all_to_all(dispatch_low, "exp", split_axis=0, concat_axis=1, tiled=True),
    )
    order_weight = grouped.transpose(0, 2, 1, 3).reshape(model_width, 2 * ctx_count * exp_count)
    order_grad = (
        grad_groups.transpose(1, 0, 2, 3)
        .reshape(2 * ctx_count * exp_count, model_width)
        .astype(jnp.bfloat16)
    )
    token_part = inner_rows(sent_grad, order_weight) + jnp.dot(
        sent_weight, order_grad, preferred_element_type=jnp.float32
    )
    token_grad = token_part + inner_rows(logit_comb.astype(jnp.bfloat16), slot_weight)
    return (mixed_out, token_grad.astype(jnp.bfloat16))


def solution(mesh):
    placed = (
        P("ctx", None),
        P(),
        P(("ctx", "exp"), None, None),
        P(("ctx", "exp"), None, None),
        P(("ctx", "exp"), None),
    )
    return jax.shard_map(
        shards,
        mesh=mesh,
        in_specs=placed,
        out_specs=(P(("ctx", "exp"), None), P(("ctx", "exp"), None)),
        check_vma=False,
    )
```

profile of v0, /device:TPU:1, one launch (start us, length us, event | category | flops | bytes accessed | tf_op | source)
XLA Modules:
  0.0 473.3 jit_solution(18211418442804663479)
XLA Ops:
  9.8 4.3 fusion.75
  14.2 64.8 %pmax.7 = f32[64]{0:T(128)S(1)} all-reduce(f32[64]{0:T(128)S(1)} %get-tuple-element.4), channel_id=1, replica_groups=mesh['ctx'=32,'exp'=4] {'ctx'}, use_global_device_ids=true, to_apply=%region_3.4 | all-reduce | flops 64 | bytes 512 | tf_op jit(solution)/shard_map/pmax | solution.py:35
  79.2 4.3 convolution_multiply_fusion
  83.6 67.1 %psum.7 = f32[64]{0:T(128)S(1)} all-reduce(f32[64]{0:T(128)S(1)} %get-tuple-element.2), channel_id=1, replica_groups=mesh['ctx'=32,'exp'=4] {'ctx'}, use_global_device_ids=true, to_apply=%region_6.7 | all-reduce | flops 64 | bytes 512 | tf_op jit(solution)/shard_map/psum | solution.py:37
  150.6 1.9 fusion.76
  154.4 68.9 %all-reduce.8 = bf16[256,1280]{1,0:T(8,128)(2,1)} all-reduce(f32[256,1280]{1,0:T(8,128)} %fusion.27), channel_id=3, replica_groups=mesh['ctx'=32,'exp'=4] {'ctx','exp'}, use_global_device_ids=true, to_apply=%region_7.8.clone | all-reduce | flops 327680 | bytes 1966080
  224.6 2.4 copy.14
  227.0 2.7 reshape.45
  230.5 3.9 fusion.6
  234.3 8.5 %multiply_reduce_fusion.1 = (f32[2]{0:T(128)S(1)}, bf16[2,1280]{1,0:T(2,128)(2,1)S(1)}) fusion(f32[2]{0:T(128)S(1)} %dynamic_slice.20, f32[64,1280]{1,0:T(8,128)} %all-reduce.7.cloned.1.call-done, u32[]{:T(128)S(6)} %multiply.5, bf16[1,1280,2560]{2,1,0:T(8,128)(2,1)} %param.7, f32[2,2560]{1,0:T(2,128)S(1)} %fusion.6, bf16[1,2560,1280]{2,1,0:T(8,128)(2,1)} %param.8, ...), kind=kOutput, calls=%fused_computation.55 | convolution fusion | flops 26327038 | bytes 13148184 | tf_op jit(solution)/shard_map/dot_general | solution.py:8
  242.8 57.8 %all-gather.1 = bf16[128,2,1280]{2,1,0:T(2,128)(2,1)S(1)} all-gather(bf16[1,2,1280]{2,1,0:T(2,128)(2,1)S(1)} %bitcast.82), channel_id=1, replica_groups=mesh['ctx'=32,'exp'=4] {'ctx','exp'}, dimensions={0}, use_global_device_ids=true | all-gather | bytes 660480 | tf_op jit(solution)/shard_map/all_gather | solution.py:70
  302.0 3.8 fusion.14
  306.4 65.1 %all-reduce.1 = f32[32,4,2]{2,1,0:T(4,128)S(1)} all-reduce(f32[32,4,2]{2,1,0:T(4,128)S(1)} %reshape.44), channel_id=1, replica_groups=mesh['ctx'=32,'exp'=4] {'ctx','exp'}, use_global_device_ids=true, to_apply=%add | all-reduce | flops 256 | bytes 2048
  371.6 4.2 fusion.10
  376.5 3.4 all-to-all-start
  379.9 2.7 convert_element_type.67
  382.6 63.2 %all-gather = bf16[128,2,1280]{2,1,0:T(2,128)(2,1)} all-gather(bf16[1,2,1280]{2,1,0:T(2,128)(2,1)S(1)} %fusion.14), channel_id=1, replica_groups=mesh['ctx'=32,'exp'=4] {'ctx','exp'}, dimensions={0}, use_global_device_ids=true | all-gather | bytes 660480 | tf_op jit(solution)/shard_map/all_gather | solution.py:48
  445.9 2.7 reshape.49
  450.2 2.7 convolution_convert_fusion
  452.9 3.4 all-to-all-start.1
  456.3 3.1 fusion.79
  459.5 2.7 all-to-all-done.1
  462.2 2.5 convolution_add_fusion.1
  464.7 1.7 fusion.8
  (34 shorter events, 10.5 us)
Async XLA Ops:
  7.2 145.5 %copy-start = (bf16[512,1280]{1,0:T(8,128)(2,1)S(1)}, bf16[512,1280]{1,0:T(8,128)(2,1)}, u32[]{:S(2)}) copy-start(bf16[512,1280]{1,0:T(8,128)(2,1)} %param.9) | copy-start | bytes 3932164
  7.2 223.3 %all-reduce.7.cloned.1.call-start = ((), (), s32[]{:S(2)}) async-start(), calls=%async_computation.2 | async-start | bytes 655360
  8.9 0.8 copy-start.2
  9.8 140.8 %copy-start.1 = (bf16[1280,256]{1,0:T(8,128)(2,1)S(1)}, bf16[1280,256]{1,0:T(8,128)(2,1)}, u32[]{:S(2)}) copy-start(bf16[1280,256]{1,0:T(8,128)(2,1)} %param.6) | copy-start | bytes 1966084
  83.5 139.8 %copy-start.3 = (u32[128]{0:T(128)S(1)}, u32[128]{0:T(128)}, u32[]{:S(2)}) copy-start(u32[128]{0:T(128)} %constant.57) | copy-start | bytes 1540
  376.5 76.4 %all-to-all-start = ((bf16[4,512,64]{1,2,0:T(8,128)(2,1)}), bf16[4,512,64]{1,2,0:T(8,128)(2,1)S(1)}, u32[]{:S(2)}, u32[]{:S(2)}) async-start(bf16[4,512,64]{1,2,0:T(8,128)(2,1)} %bitcast.73), calls=%async_computation | async-start | bytes 524288 | tf_op jit(solution)/shard_map/all_to_all | solution.py:86
  452.9 9.3 %all-to-all-start.1 = ((bf16[4,512,64]{1,2,0:T(8,128)(2,1)}), bf16[4,512,64]{1,2,0:T(8,128)(2,1)S(1)}, u32[]{:S(2)}, u32[]{:S(2)}) async-start(bf16[4,512,64]{1,2,0:T(8,128)(2,1)} %bitcast.72), calls=%async_computation.1 | async-start | bytes 524288 | tf_op jit(solution)/shard_map/all_to_all | solution.py:87
Sparse Core Ops, SparseCore 0:
  83.7 102.8 all-reduce.6
where the time goes:
time: 474 us; the launch traced here: 473 us
  blocking collectives  387 us (82%)
  matrix products  44.1 us (9%)
  local copies, waits for them, and re-layouts  17.2 us (4%)
  between operations  14.8 us (3%)
  starting transfers between devices  6.85 us (1%)
    unnamed x2, blocking collectives  134 us
    psum x1, blocking collectives, shards(): totals = lax.psum(local_totals * rescale, 'ctx')  67.1 us
    pmax x1, blocking collectives, shards(): highest = lax.pmax(local_max, 'ctx')  64.8 us
    all_gather x1, blocking collectives, shards(): all_out = lax.all_gather(slot_out, ('ctx', 'exp'), axis=0, tiled=True)  63.2 us
    all_gather x1, blocking collectives, shards(): lax.all_gather(in_grad, ('ctx', 'exp'), axis=0, tiled=True)  57.8 us
    dot_general x5, matrix products, inner_rows(): lax.dot_general(left_rows, right_rows, (((1,), (1,)), ((), ())), preferre...  19.1 us
  transfers between devices with their start and end apart: 3, of which 1 were waited for; matrix products, arithmetic and copies ran while one was open for 5% of the time, Pallas kernels for 0%

commit v1 on v0

v1 whole, which is shorter than its diff:
```python
import functools

import jax
import jax.numpy as jnp
from jax import lax
from jax.experimental import pallas as pl
from jax.experimental.pallas import tpu as pltpu
from jax.sharding import Mesh
from jax.sharding import PartitionSpec as P

LOW = jnp.bfloat16
WIDE = jnp.float32
EXTRA = 128
LIMIT = 40 * 1024 * 1024


def product(left, right, left_dim, right_dim):
    return lax.dot_general(
        left, right, (((left_dim,), (right_dim,)), ((), ())), preferred_element_type=WIDE
    )


def split3(value):
    high = value.astype(LOW).astype(WIDE)
    rest = value - high
    mid = rest.astype(LOW).astype(WIDE)
    return [high, mid, rest - mid]


def place(pieces, shape, axis):
    index = lax.broadcasted_iota(jnp.int32, shape, axis)
    total = jnp.zeros(shape, WIDE)
    for at, piece in enumerate(pieces):
        total = jnp.where(index == at, piece, total)
    return total


def lanes(block, first):
    index = lax.broadcasted_iota(jnp.int32, block.shape, 1)
    inside = (index >= first) & (index < first + 3)
    return jnp.sum(jnp.where(inside, block, 0.0), axis=1, keepdims=True)


def opening_kernel(at_ref, tok_ref, weight_ref, cot_ref, comb_ref, logit_ref, order_ref, *outs):
    slots = weight_ref.shape[1]
    half = slots // 2
    width = tok_ref.shape[1]
    core = at_ref[1]
    to = lax.broadcasted_iota(jnp.int32, (slots, slots), 1)
    source = lax.broadcasted_iota(jnp.int32, (slots, slots), 0)
    other = to // half
    within = to % half
    wanted = (within // 8) * 16 + jnp.where(other == 0, core, 1 - core) * 8 + within % 8
    order = (source == wanted).astype(WIDE).astype(LOW)
    weight = product(weight_ref[...], order, 1, 0).astype(LOW)
    order_ref[...] = weight
    rows = tok_ref[...]
    logits = product(rows, weight, 1, 0)
    logit_ref[...] = logits
    col_max = jnp.max(logits, axis=0, keepdims=True)
    shifted = jnp.exp(logits - col_max)
    col_sum = jnp.sum(shifted, axis=0, keepdims=True)
    slot_part = product(shifted.astype(LOW), rows, 0, 0)
    raised = jnp.exp(logits - jnp.max(logits, axis=1, keepdims=True))
    combine = raised / jnp.sum(raised, axis=1, keepdims=True)
    comb_ref[...] = combine
    grad_part = product(combine.astype(LOW), cot_ref[...], 0, 0)
    pieces = place(split3(col_max) + split3(col_sum), (EXTRA, slots), 0).T
    for at, out in enumerate(outs):
        part = slice(at * half, (at + 1) * half)
        out[:, :width] = slot_part[part].astype(LOW)
        out[:, width : 2 * width] = grad_part[part].astype(LOW)
        out[:, 2 * width :] = pieces[part].astype(LOW)


def opening(at, tokens, slot_weight, cotangent):
    rows, width = cotangent.shape
    slots = slot_weight.shape[1]
    wide = 2 * width + EXTRA
    whole = lambda shape: pl.BlockSpec(shape, lambda i, at: (0, 0))
    return pl.pallas_call(
        opening_kernel,
        grid_spec=pltpu.PrefetchScalarGridSpec(
            num_scalar_prefetch=1,
            grid=(1,),
            in_specs=[
                pl.BlockSpec((rows, width), lambda i, at: (at[0], 0)),
                whole((width, slots)),
                whole((rows, width)),
            ],
            out_specs=[
                whole((rows, slots)),
                whole((rows, slots)),
                whole((width, slots)),
                whole((slots // 2, wide)),
                whole((slots // 2, wide)),
            ],
        ),
        out_shape=[
            jax.ShapeDtypeStruct((rows, slots), WIDE),
            jax.ShapeDtypeStruct((rows, slots), WIDE),
            jax.ShapeDtypeStruct((width, slots), LOW),
            jax.ShapeDtypeStruct((slots // 2, wide), LOW),
            jax.ShapeDtypeStruct((slots // 2, wide), LOW),
        ],
        compiler_params=pltpu.CompilerParams(vmem_limit_bytes=LIMIT),
        name="opening",
    )(at, tokens, slot_weight, cotangent)


def merge_kernel(kept_ref, taken_ref, out_ref):
    width = (out_ref.shape[1] - EXTRA) // 2
    kept, taken = kept_ref[:, 2 * width :].astype(WIDE), taken_ref[:, 2 * width :].astype(WIDE)
    kept_max, taken_max = lanes(kept, 0), lanes(taken, 0)
    top = jnp.maximum(kept_max, taken_max)
    kept_scale, taken_scale = jnp.exp(kept_max - top), jnp.exp(taken_max - top)
    total = kept_scale * lanes(kept, 3) + taken_scale * lanes(taken, 3)
    out_ref[:, :width] = (
        kept_scale * kept_ref[:, :width].astype(WIDE)
        + taken_scale * taken_ref[:, :width].astype(WIDE)
    ).astype(LOW)
    out_ref[:, width : 2 * width] = (
        kept_ref[:, width : 2 * width].astype(WIDE) + taken_ref[:, width : 2 * width].astype(WIDE)
    ).astype(LOW)
    out_ref[:, 2 * width :] = place(split3(top) + split3(total), kept.shape, 1).astype(LOW)


def merge(kept, taken):
    return pl.pallas_call(
        merge_kernel,
        out_shape=jax.ShapeDtypeStruct(kept.shape, LOW),
        compiler_params=pltpu.CompilerParams(vmem_limit_bytes=LIMIT),
        name="merge",
    )(kept, taken)


PARTS = 4


def expert_kernel(got_ref, in_hbm, out_hbm, told_ref, w_in, w_out, in_sem, out_sem):
    width, hidden = w_in.shape
    in_rows, out_rows = width // PARTS, hidden // PARTS

    in_copies = [
        pltpu.make_async_copy(
            in_hbm.at[0, pl.ds(at * in_rows, in_rows)],
            w_in.at[pl.ds(at * in_rows, in_rows)],
            in_sem.at[at],
        )
        for at in range(PARTS)
    ]
    out_copies = [
        pltpu.make_async_copy(
            out_hbm.at[0, pl.ds(at * out_rows, out_rows)],
            w_out.at[pl.ds(at * out_rows, out_rows)],
            out_sem.at[at],
        )
        for at in range(PARTS)
    ]
    for copy in in_copies + out_copies:
        copy.start()
    pieces = got_ref[:, 2 * width :].astype(WIDE)
    count = pieces.shape[0]
    block_max, block_sum = lanes(pieces, 0), lanes(pieces, 3)
    odd = lax.broadcasted_iota(jnp.int32, (count, 1), 0) % 2 == 1
    lowest = jnp.full((count, 1), -jnp.inf, WIDE)
    top = [
        jnp.max(jnp.where(odd, lowest, block_max), axis=0, keepdims=True),
        jnp.max(jnp.where(odd, block_max, lowest), axis=0, keepdims=True),
    ]
    scale = jnp.exp(block_max - jnp.where(odd, top[1], top[0]))
    scaled_sum = scale * block_sum
    totals = [
        jnp.sum(jnp.where(odd, 0.0, scaled_sum), axis=0, keepdims=True),
        jnp.sum(jnp.where(odd, scaled_sum, 0.0), axis=0, keepdims=True),
    ]
    scaled = scale * got_ref[:, :width].astype(WIDE)
    exact = [
        jnp.sum(jnp.where(odd, 0.0, scaled), axis=0, keepdims=True) / totals[0],
        jnp.sum(jnp.where(odd, scaled, 0.0), axis=0, keepdims=True) / totals[1],
    ]
    sent = got_ref[:, width : 2 * width].astype(WIDE)
    grads = [
        jnp.sum(jnp.where(odd, 0.0, sent), axis=0, keepdims=True),
        jnp.sum(jnp.where(odd, sent, 0.0), axis=0, keepdims=True),
    ]
    exact = place(exact, (8, width), 0)
    out_grad = place(grads, (8, width), 0).astype(LOW)
    slot_low = exact.astype(LOW)
    preact = jnp.zeros((8, hidden), WIDE)
    for at in range(PARTS):
        in_copies[at].wait()
        part = slice(at * in_rows, (at + 1) * in_rows)
        preact += product(slot_low[:, part], w_in[part, :], 1, 0)
    rate = 0.7978845608028654
    square = preact * preact
    curve = jnp.tanh(rate * (preact + 0.044715 * square * preact))
    low_hidden = (0.5 * preact * (1.0 + curve)).astype(LOW)
    slope = 0.5 * (1.0 + curve) + 0.5 * preact * (1.0 - curve * curve) * rate * (
        1.0 + 3.0 * 0.044715 * square
    )
    slot_out = jnp.zeros((8, width), WIDE)
    in_grad = jnp.zeros((8, width), WIDE)
    for at in range(PARTS):
        out_copies[at].wait()
        part = slice(at * out_rows, (at + 1) * out_rows)
        slot_out += product(low_hidden[:, part], w_out[part, :], 1, 0)
        pre_grad = (slope[:, part] * product(out_grad, w_out[part, :], 1, 1)).astype(LOW)
        in_grad += product(pre_grad, w_in[:, part], 1, 1)
    told_ref[:, :width] = slot_out.astype(LOW)
    told_ref[:, width : 2 * width] = in_grad.astype(LOW)
    slot_product = jnp.sum(exact * in_grad, axis=1, keepdims=True)
    top = place(top, (8, 1), 0)
    totals = place(totals, (8, 1), 0)
    told_ref[:, 2 * width :] = place(
        split3(slot_product) + split3(top) + split3(totals), (8, EXTRA), 1
    ).astype(LOW)


def expert(got, w_in, w_out):
    width, hidden = w_in.shape[1:]
    return pl.pallas_call(
        expert_kernel,
        in_specs=[
            pl.BlockSpec(memory_space=pltpu.VMEM),
            pl.BlockSpec(memory_space=pl.ANY),
            pl.BlockSpec(memory_space=pl.ANY),
        ],
        out_specs=pl.BlockSpec(memory_space=pltpu.VMEM),
        out_shape=jax.ShapeDtypeStruct((8, 2 * width + EXTRA), LOW),
        scratch_shapes=[
            pltpu.VMEM((width, hidden), LOW),
            pltpu.VMEM((hidden, width), LOW),
            pltpu.SemaphoreType.DMA((PARTS,)),
            pltpu.SemaphoreType.DMA((PARTS,)),
        ],
        compiler_params=pltpu.CompilerParams(vmem_limit_bytes=LIMIT),
        name="expert",
    )(got, w_in, w_out)


def closing_kernel(
    at_ref, tok_ref, cot_ref, comb_ref, logit_ref, weight_ref, mine_ref, pair_ref,
    mixed_ref, grad_ref, all_out, in_low, rows_ref,
):
    width = tok_ref.shape[1]
    half = mine_ref.shape[0]

    @pl.when(pl.program_id(0) == 0)
    def _():
        for at, ref in enumerate((mine_ref, pair_ref)):
            part = slice(at * half, (at + 1) * half)
            all_out[part, :] = ref[:, :width]
            in_low[part, :] = ref[:, width : 2 * width]
            pieces = ref[:, 2 * width :].astype(WIDE).T
            for row in range(3):
                rows_ref[row : row + 1, part] = jnp.sum(
                    pieces[3 * row : 3 * row + 3], axis=0, keepdims=True
                )

    slot_product, highest, totals = rows_ref[0:1], rows_ref[1:2], rows_ref[2:3]
    combine = comb_ref[...]
    mixed_ref[...] = product(combine.astype(LOW), all_out[...], 1, 0).astype(LOW)
    comb_grad = product(cot_ref[...], all_out[...], 1, 1)
    logit_grad = combine * (comb_grad - jnp.sum(combine * comb_grad, axis=1, keepdims=True))
    dispatch = jnp.exp(logit_ref[...] - highest) / totals
    logit_grad += dispatch * (product(tok_ref[...], in_low[...], 1, 1) - slot_product)
    token_grad = product(logit_grad.astype(LOW), weight_ref[...], 1, 1)
    token_grad += product(dispatch.astype(LOW), in_low[...], 1, 0)
    grad_ref[...] = token_grad.astype(LOW)


def closing(at, tokens, cotangent, combine, logits, weight, mine, pair):
    rows, width = cotangent.shape
    slots = weight.shape[1]
    steps = 2
    block = rows // steps
    whole = lambda shape: pl.BlockSpec(shape, lambda i, at: (0, 0))
    tall = lambda cols: pl.BlockSpec((block, cols), lambda i, at: (i, 0))
    return pl.pallas_call(
        closing_kernel,
        grid_spec=pltpu.PrefetchScalarGridSpec(
            num_scalar_prefetch=1,
            grid=(steps,),
            in_specs=[
                pl.BlockSpec((block, width), lambda i, at: (at[0] * steps + i, 0)),
                tall(width),
                tall(slots),
                tall(slots),
                whole(weight.shape),
                whole(mine.shape),
                whole(pair.shape),
            ],
            out_specs=[tall(width), tall(width)],
            scratch_shapes=[
                pltpu.VMEM((slots, width), LOW),
                pltpu.VMEM((slots, width), LOW),
                pltpu.VMEM((8, slots), WIDE),
            ],
        ),
        out_shape=[jax.ShapeDtypeStruct((rows, width), LOW)] * 2,
        compiler_params=pltpu.CompilerParams(vmem_limit_bytes=LIMIT),
        name="closing",
    )(at, tokens, cotangent, combine, logits, weight, mine, pair)


def shards(tokens, slot_weight, w_in, w_out, cotangent):
    chips, cores, exp_count = lax.axis_size("chip"), lax.axis_size("core"), lax.axis_size("exp")
    peers = chips * exp_count
    swap = [(0, 1), (1, 0)]
    at = jnp.stack([lax.axis_index("exp"), lax.axis_index("core")]).astype(jnp.int32)
    slots = slot_weight.shape[1]
    half = slots // cores
    combine, logits, weight, kept, given = opening(at, tokens, slot_weight, cotangent)
    merged = merge(kept, lax.ppermute(given, "core", swap))
    sent = merged.reshape(peers, half // peers, -1)
    got = lax.all_to_all(sent, ("chip", "exp"), split_axis=0, concat_axis=0, tiled=True)
    told = expert(got.reshape(half, -1), w_in, w_out)[: half // peers]
    told = jnp.broadcast_to(told[None], (peers,) + told.shape)
    told = lax.all_to_all(told, ("chip", "exp"), split_axis=0, concat_axis=0, tiled=True)
    told = told.reshape(half, -1)
    pair = lax.ppermute(told, "core", swap)
    mixed_out, token_grad = closing(at, tokens, cotangent, combine, logits, weight, told, pair)
    return (mixed_out, token_grad)


def solution(mesh):
    ctx, exp = mesh.devices.shape
    finer = Mesh(mesh.devices.reshape(ctx // 2, 2, exp), ("chip", "core", "exp"))
    rows = P(("chip", "core", "exp"), None)
    experts = P(("chip", "core", "exp"), None, None)
    return jax.shard_map(
        shards,
        mesh=finer,
        in_specs=(P(("chip", "core"), None), P(), experts, experts, rows),
        out_specs=(rows, rows),
        check_vma=False,
    )
```

time: 474 us -> 84.9 us (0.18)
  blocking collectives: 387 us -> 42.3 us
  matrix products: 44.1 us -> 0 us
  Pallas kernels: 0 us -> 15.2 us
  between operations: 14.8 us -> 0.72 us
    unnamed x2 -> x0, blocking collectives: 134 us -> none
    all_gather x2 -> x0, blocking collectives: 121 us -> none  [the longest x1 63.2 us: shards(): all_out = lax.all_gather(slot_out, ('ctx', 'exp'), axis=0, tiled=True)]
    psum x1 -> x0, blocking collectives: 67.1 us -> none  [shards(): totals = lax.psum(local_totals * rescale, 'ctx')]
    pmax x1 -> x0, blocking collectives: 64.8 us -> none  [shards(): highest = lax.pmax(local_max, 'ctx')]
    dot_general x13 -> x0, matrix products: 44.1 us -> none  [the longest x5 19.1 us: inner_rows(): lax.dot_general(left_rows, right_rows, (((1,), (1,)), ((), ())), preferre...]
    all_to_all x0 -> x2, blocking collectives: none -> 42.3 us  [the longest x1 24.6 us: shards(): lax.all_to_all(sent, ('chip', 'exp'), split_axis=0, concat_axis=0, tiled=...]
    pallas_call x0 -> x4, Pallas kernels: none -> 15.2 us  [the longest x1 8.66 us: expert(): pl.pallas_call(expert_kernel, in_specs=[pl.BlockSpec(memory_space=pltpu.V...]
    unnamed x13 -> x18, local copies, waits for them, and re-layouts: 5.68 us -> 14.9 us
  transfers between devices with their start and end apart: 3 -> 2, of which waited for: 1 -> 2; matrix products, arithmetic and copies ran while one was open for 5% -> 0% of each run, Pallas kernels for 0% -> 0%
where the time goes in v1:
time: 84.9 us; the launch traced here: 84.5 us
  blocking collectives  42.3 us (50%)
  local copies, waits for them, and re-layouts  17.9 us (21%)
  Pallas kernels  15.2 us (18%)
  starting transfers between devices  4.68 us (6%)
  waiting for transfers between devices  3.54 us (4%)
    all_to_all x1, blocking collectives, shards(): lax.all_to_all(sent, ('chip', 'exp'), split_axis=0, concat_axis=0, tiled=...  24.6 us
    all_to_all x1, blocking collectives, shards(): lax.all_to_all(told, ('chip', 'exp'), split_axis=0, concat_axis=0, tiled=...  17.6 us
    unnamed x18, local copies, waits for them, and re-layouts  14.9 us
    pallas_call x1, Pallas kernels, expert(): pl.pallas_call(expert_kernel, in_specs=[pl.BlockSpec(memory_space=pltpu.V...  8.66 us
    pallas_call x1, Pallas kernels, closing(): pl.pallas_call(closing_kernel, grid_spec=pltpu.PrefetchScalarGridSpec(num...  3.61 us
    ppermute x1, starting transfers between devices, shards(): pair = lax.ppermute(told, 'core', swap)  3.26 us
    pallas_call x1, Pallas kernels, opening(): pl.pallas_call(opening_kernel, grid_spec=pltpu.PrefetchScalarGridSpec(num...  2.56 us
    reshape x1, local copies, waits for them, and re-layouts, shards(): told = told.reshape(half, -1)  2.13 us
  transfers between devices with their start and end apart: 2, of which 2 were waited for; matrix products, arithmetic and copies ran while one was open for 0% of the time, Pallas kernels for 0%

profile of v1, /device:TPU:1, one launch (start us, length us, event | category | flops | bytes accessed | tf_op | source)
XLA Modules:
  0.0 84.5 jit_solution(2775070316827854148)
XLA Ops:
  0.6 0.1 pad_add_fusion.at_ref
  0.7 2.5 %copy-done = bf16[2048,1280]{1,0:T(8,128)(2,1)S(1)} copy-done((bf16[2048,1280]{1,0:T(8,128)(2,1)S(1)}, bf16[2048,1280]{1,0:T(8,128)(2,1)}, u32[]{:S(2)}) %copy-start) | copy-done | bytes 5242904
  3.2 1.3 %copy-done.4 = bf16[512,1280]{1,0:T(8,128)(2,1)S(1)} copy-done((bf16[512,1280]{1,0:T(8,128)(2,1)S(1)}, bf16[512,1280]{1,0:T(8,128)(2,1)}, u32[]{:S(2)}) %copy-start.4) | copy-done | bytes 1310744
  4.5 1.1 %copy-done.6 = bf16[1280,256]{1,0:T(8,128)(2,1)S(1)} copy-done((bf16[1280,256]{1,0:T(8,128)(2,1)S(1)}, bf16[1280,256]{1,0:T(8,128)(2,1)}, u32[]{:S(2)}) %copy-start.6) | copy-done | bytes 655384
  5.6 2.6 %opening.1 = (f32[512,256]{1,0:T(8,128)S(1)}, f32[512,256]{1,0:T(8,128)S(1)}, bf16[1280,256]{1,0:T(8,128)(2,1)S(1)}, bf16[128,2688]{1,0:T(8,128)(2,1)S(1)}, bf16[128,2688]{1,0:T(8,128)(2,1)S(1)}) custom-call(s32[2]{0:T(128)S(1)} %pad_add_fusion.at_ref, bf16[2048,1280]{1,0:T(8,128)(2,1)S(1)} %copy-done, bf16[1280,256]{1,0:T(8,128)(2,1)S(1)} %copy-done.6, ...), custom_call_target="tpu_custom_call" | custom-call | tf_op jit(solution)/shard_map/opening/pallas_call | solution.py:81
  8.2 0.0 copy-start.7
  8.2 0.8 copy-done.7
  9.0 1.4 %collective-permute-start = (bf16[128,2688]{1,0:T(8,128)(2,1)S(1)}, bf16[128,2688]{1,0:T(8,128)(2,1)S(1)}, u32[]{:S(2)}, u32[]{:S(2)}) collective-permute-start(bf16[128,2688]{1,0:T(8,128)(2,1)S(1)} %get-tuple-element.11), channel_id=1, source_target_pairs={{0,4},{4,0},{1,5},{5,1},{2,6},{6,2},{3,7},{7,3},{8,12},{12,8},{9,1... | collective-permute-start | bytes 2064392 | tf_op jit(solution)/shard_map/ppermute | solution.py:315
  10.4 1.8 %collective-permute-done.taken_ref = bf16[128,2688]{1,0:T(8,128)(2,1)S(1)} collective-permute-done((bf16[128,2688]{1,0:T(8,128)(2,1)S(1)}, bf16[128,2688]{1,0:T(8,128)(2,1)S(1)}, u32[]{:S(2)}, u32[]{:S(2)}) %collective-permute-start) | collective-permute-done | bytes 688160 | tf_op jit(solution)/shard_map/ppermute | solution.py:315
  12.2 0.4 merge.1
  12.6 0.3 reshape.14
  12.8 24.6 %all_to_all.10 = bf16[64,2,2688]{2,1,0:T(2,128)(2,1)S(1)} all-to-all(bf16[64,2,2688]{2,1,0:T(2,128)(2,1)S(1)} %reshape.14), channel_id=1, replica_groups=mesh['chip'=16,'core'=2,'exp'=4] {'chip','exp'}, dimensions={0} | all-to-all | bytes 1376256 | tf_op jit(solution)/shard_map/all_to_all | solution.py:317
  37.5 0.3 reshape.15.got_ref
  37.7 2.9 %copy-done.2 = bf16[1,1280,2560]{2,1,0:T(8,128)(2,1)S(1)} copy-done((bf16[1,1280,2560]{2,1,0:T(8,128)(2,1)S(1)}, bf16[1,1280,2560]{2,1,0:T(8,128)(2,1)}, u32[]{:S(2)}) %copy-start.2) | copy-done | bytes 6553624
  40.6 2.9 %copy-done.3 = bf16[1,2560,1280]{2,1,0:T(8,128)(2,1)S(1)} copy-done((bf16[1,2560,1280]{2,1,0:T(8,128)(2,1)S(1)}, bf16[1,2560,1280]{2,1,0:T(8,128)(2,1)}, u32[]{:S(2)}) %copy-start.3) | copy-done | bytes 6553624
  43.5 8.7 %expert.1 = bf16[8,2688]{1,0:T(8,128)(2,1)S(1)} custom-call(bf16[128,2688]{1,0:T(8,128)(2,1)S(1)} %reshape.15.got_ref, bf16[1,1280,2560]{2,1,0:T(8,128)(2,1)S(1)} %copy-done.2, bf16[1,2560,1280]{2,1,0:T(8,128)(2,1)S(1)} %copy-done.3), custom_call_target="tpu_custom_call" | custom-call | tf_op jit(solution)/shard_map/expert/pallas_call | solution.py:222
  52.1 0.4 broadcast_in_dim.2
  52.5 17.6 %all_to_all.11 = bf16[64,2,2688]{2,1,0:T(2,128)(2,1)} all-to-all(bf16[64,2,2688]{2,1,0:T(2,128)(2,1)S(1)} %broadcast_in_dim.2), channel_id=1, replica_groups=mesh['chip'=16,'core'=2,'exp'=4] {'chip','exp'}, dimensions={0} | all-to-all | bytes 1376256 | tf_op jit(solution)/shard_map/all_to_all | solution.py:320
  70.1 2.1 %reshape.16.mine_ref = bf16[128,2688]{1,0:T(8,128)(2,1)S(1)} reshape(bf16[64,2,2688]{2,1,0:T(2,128)(2,1)} %all_to_all.11) | data formatting | bytes 1376256 | tf_op jit(solution)/shard_map/reshape | solution.py:321
  72.3 3.3 %collective-permute-start.1 = (bf16[128,2688]{1,0:T(8,128)(2,1)S(1)}, bf16[128,2688]{1,0:T(8,128)(2,1)S(1)}, u32[]{:S(2)}, u32[]{:S(2)}) collective-permute-start(bf16[128,2688]{1,0:T(8,128)(2,1)S(1)} %reshape.16.mine_ref), channel_id=1, source_target_pairs={{0,4},{4,0},{1,5},{5,1},{2,6},{6,2},{3,7},{7,3},{8,12},{12,8},{9,1... | collective-permute-start | bytes 2064392 | tf_op jit(solution)/shard_map/ppermute | solution.py:322
  75.5 1.8 %collective-permute-done.1.pair_ref = bf16[128,2688]{1,0:T(8,128)(2,1)S(1)} collective-permute-done((bf16[128,2688]{1,0:T(8,128)(2,1)S(1)}, bf16[128,2688]{1,0:T(8,128)(2,1)S(1)}, u32[]{:S(2)}, u32[]{:S(2)}) %collective-permute-start.1) | collective-permute-done | bytes 688160 | tf_op jit(solution)/shard_map/ppermute | solution.py:322
  77.3 2.5 %copy-done.1 = bf16[2048,1280]{1,0:T(8,128)(2,1)S(1)} copy-done((bf16[2048,1280]{1,0:T(8,128)(2,1)S(1)}, bf16[2048,1280]{1,0:T(8,128)(2,1)}, u32[]{:S(2)}) %copy-start.1) | copy-done | bytes 5242904
  79.8 1.0 %copy-done.8 = f32[512,256]{1,0:T(8,128)S(1)} copy-done((f32[512,256]{1,0:T(8,128)S(1)}, f32[512,256]{1,0:T(8,128)}, u32[]{:S(2)}) %copy-start.8) | copy-done | bytes 524312
  80.8 3.6 %closing.1 = (bf16[512,1280]{1,0:T(8,128)(2,1)}, bf16[512,1280]{1,0:T(8,128)(2,1)}) custom-call(s32[2]{0:T(128)S(1)} %pad_add_fusion.at_ref, bf16[2048,1280]{1,0:T(8,128)(2,1)S(1)} %copy-done.1, bf16[512,1280]{1,0:T(8,128)(2,1)S(1)} %copy-done.5, f32[512,256]{1,0:T(8,128)S(1)} %get-tuple-element.7.comb_ref, f32[512,256]{1,0:T(8,128)S(1)} %copy-done.8, ...), custom_call_target="tpu_custom_call" | custom-call | tf_op jit(solution)/shard_map/closing/pallas_call | solution.py:280
  (10 shorter events, 0.0 us)
Async XLA Ops:
  0.7 2.5 %copy-start = (bf16[2048,1280]{1,0:T(8,128)(2,1)S(1)}, bf16[2048,1280]{1,0:T(8,128)(2,1)}, u32[]{:S(2)}) copy-start(bf16[2048,1280]{1,0:T(8,128)(2,1)} %tok_ref.3) | copy-start | bytes 15728644
  3.2 1.3 %copy-start.4 = (bf16[512,1280]{1,0:T(8,128)(2,1)S(1)}, bf16[512,1280]{1,0:T(8,128)(2,1)}, u32[]{:S(2)}) copy-start(bf16[512,1280]{1,0:T(8,128)(2,1)} %cot_ref.3) | copy-start | bytes 3932164
  4.5 1.1 %copy-start.6 = (bf16[1280,256]{1,0:T(8,128)(2,1)S(1)}, bf16[1280,256]{1,0:T(8,128)(2,1)}, u32[]{:S(2)}) copy-start(bf16[1280,256]{1,0:T(8,128)(2,1)} %weight_ref.1) | copy-start | bytes 1966084
  8.2 0.8 copy-start.7
  9.0 3.2 %collective-permute-start = (bf16[128,2688]{1,0:T(8,128)(2,1)S(1)}, bf16[128,2688]{1,0:T(8,128)(2,1)S(1)}, u32[]{:S(2)}, u32[]{:S(2)}) collective-permute-start(bf16[128,2688]{1,0:T(8,128)(2,1)S(1)} %get-tuple-element.11), channel_id=1, source_target_pairs={{0,4},{4,0},{1,5},{5,1},{2,6},{6,2},{3,7},{7,3},{8,12},{12,8},{9,1... | collective-permute-start | bytes 2064392 | tf_op jit(solution)/shard_map/ppermute | solution.py:315
  37.7 2.9 %copy-start.2 = (bf16[1,1280,2560]{2,1,0:T(8,128)(2,1)S(1)}, bf16[1,1280,2560]{2,1,0:T(8,128)(2,1)}, u32[]{:S(2)}) copy-start(bf16[1,1280,2560]{2,1,0:T(8,128)(2,1)} %in_hbm.1) | copy-start | bytes 19660804
  40.6 2.9 %copy-start.3 = (bf16[1,2560,1280]{2,1,0:T(8,128)(2,1)S(1)}, bf16[1,2560,1280]{2,1,0:T(8,128)(2,1)}, u32[]{:S(2)}) copy-start(bf16[1,2560,1280]{2,1,0:T(8,128)(2,1)} %out_hbm.1) | copy-start | bytes 19660804
  43.5 33.9 %copy-start.5 = (bf16[512,1280]{1,0:T(8,128)(2,1)S(1)}, bf16[512,1280]{1,0:T(8,128)(2,1)}, u32[]{:S(2)}) copy-start(bf16[512,1280]{1,0:T(8,128)(2,1)} %cot_ref.3) | copy-start | bytes 3932164
  72.3 5.0 %collective-permute-start.1 = (bf16[128,2688]{1,0:T(8,128)(2,1)S(1)}, bf16[128,2688]{1,0:T(8,128)(2,1)S(1)}, u32[]{:S(2)}, u32[]{:S(2)}) collective-permute-start(bf16[128,2688]{1,0:T(8,128)(2,1)S(1)} %reshape.16.mine_ref), channel_id=1, source_target_pairs={{0,4},{4,0},{1,5},{5,1},{2,6},{6,2},{3,7},{7,3},{8,12},{12,8},{9,1... | collective-permute-start | bytes 2064392 | tf_op jit(solution)/shard_map/ppermute | solution.py:322
  77.3 2.5 %copy-start.1 = (bf16[2048,1280]{1,0:T(8,128)(2,1)S(1)}, bf16[2048,1280]{1,0:T(8,128)(2,1)}, u32[]{:S(2)}) copy-start(bf16[2048,1280]{1,0:T(8,128)(2,1)} %tok_ref.3) | copy-start | bytes 15728644
  79.8 1.0 %copy-start.8 = (f32[512,256]{1,0:T(8,128)S(1)}, f32[512,256]{1,0:T(8,128)}, u32[]{:S(2)}) copy-start(f32[512,256]{1,0:T(8,128)} %copy-done.7) | copy-start | bytes 1572868

commit v2 on v1

v2 whole, which is shorter than its diff:
```python
import functools

import jax
import jax.numpy as jnp
from jax import lax
from jax.experimental import pallas as pl
from jax.experimental.pallas import tpu as pltpu
from jax.sharding import Mesh
from jax.sharding import PartitionSpec as P

LOW = jnp.bfloat16
WIDE = jnp.float32
EXTRA = 128
LIMIT = 20 * 1024 * 1024


def product(left, right, left_dim, right_dim):
    return lax.dot_general(
        left, right, (((left_dim,), (right_dim,)), ((), ())), preferred_element_type=WIDE
    )


def split3(value):
    high = value.astype(LOW).astype(WIDE)
    rest = value - high
    mid = rest.astype(LOW).astype(WIDE)
    return [high, mid, rest - mid]


def place(pieces, shape, axis):
    index = lax.broadcasted_iota(jnp.int32, shape, axis)
    total = jnp.zeros(shape, WIDE)
    for at, piece in enumerate(pieces):
        total = jnp.where(index == at, piece, total)
    return total


def lanes(block, first):
    index = lax.broadcasted_iota(jnp.int32, block.shape, 1)
    inside = (index >= first) & (index < first + 3)
    return jnp.sum(jnp.where(inside, block, 0.0), axis=1, keepdims=True)


IN_SMEM = pl.BlockSpec(memory_space=pltpu.SMEM)
IN_VMEM = pl.BlockSpec(memory_space=pltpu.VMEM)
IN_HBM = pl.BlockSpec(memory_space=pltpu.HBM)


def stay(array):
    return pltpu.with_memory_space_constraint(array, pltpu.HBM)


def call(kernel, name, args, specs, out_specs, out_shape, scratch=()):
    return pl.pallas_call(
        kernel,
        in_specs=specs,
        out_specs=out_specs,
        out_shape=out_shape,
        scratch_shapes=scratch,
        compiler_params=pltpu.CompilerParams(vmem_limit_bytes=LIMIT),
        name=name,
    )(*args)


def ordering(core, slots):
    to = lax.broadcasted_iota(jnp.int32, (slots, slots), 1)
    source = lax.broadcasted_iota(jnp.int32, (slots, slots), 0)
    half = slots // 2
    within = to % half
    other = jnp.where(to // half == 0, core, 1 - core)
    wanted = (within // 8) * 16 + other * 8 + within % 8
    return (source == wanted).astype(WIDE).astype(LOW)


def opening_kernel(
    at_ref, tok_hbm, weight_hbm, cot_hbm,
    kept_ref, given_ref, comb_ref, logit_ref, order_ref, rows_ref, cot_ref,
    weight_ref, sems,
):
    slots = weight_ref.shape[1]
    half = slots // 2
    count, width = rows_ref.shape
    start = pl.multiple_of(at_ref[0] * count, count)
    loads = [
        pltpu.make_async_copy(source, target, sems.at[at])
        for at, (source, target) in enumerate(
            (
                (weight_hbm, weight_ref),
                (tok_hbm.at[pl.ds(start, count)], rows_ref),
                (cot_hbm, cot_ref),
            )
        )
    ]
    for copy in loads:
        copy.start()
    order = ordering(at_ref[1], slots)
    loads[0].wait()
    weight = product(weight_ref[...], order, 1, 0).astype(LOW)
    order_ref[...] = weight
    loads[1].wait()
    rows = rows_ref[...]
    logits = product(rows, weight, 1, 0)
    logit_ref[...] = logits
    col_max = jnp.max(logits, axis=0, keepdims=True)
    shifted = jnp.exp(logits - col_max)
    col_sum = jnp.sum(shifted, axis=0, keepdims=True)
    slot_part = product(shifted.astype(LOW), rows, 0, 0)
    raised = jnp.exp(logits - jnp.max(logits, axis=1, keepdims=True))
    combine = raised / jnp.sum(raised, axis=1, keepdims=True)
    comb_ref[...] = combine
    loads[2].wait()
    grad_part = product(combine.astype(LOW), cot_ref[...], 0, 0)
    pieces = place(split3(col_max) + split3(col_sum), (EXTRA, slots), 0).T
    for at, out in enumerate((kept_ref, given_ref)):
        part = slice(at * half, (at + 1) * half)
        out[:, :width] = slot_part[part].astype(LOW)
        out[:, width : 2 * width] = grad_part[part].astype(LOW)
        out[:, 2 * width :] = pieces[part].astype(LOW)


def opening(at, tokens, slot_weight, cotangent):
    rows, width = cotangent.shape
    slots = slot_weight.shape[1]
    shapes = [((slots // 2, 2 * width + EXTRA), LOW)] * 2
    shapes += [((rows, slots), WIDE)] * 2 + [((width, slots), LOW)] + [((rows, width), LOW)] * 2
    return call(
        opening_kernel,
        "opening",
        (at, stay(tokens), stay(slot_weight), stay(cotangent)),
        [IN_SMEM] + [IN_HBM] * 3,
        [IN_VMEM] * len(shapes),
        [jax.ShapeDtypeStruct(*shape) for shape in shapes],
        [pltpu.VMEM((width, slots), LOW), pltpu.SemaphoreType.DMA((3,))],
    )


def merge_kernel(kept_ref, taken_ref, out_ref):
    width = (out_ref.shape[2] - EXTRA) // 2
    kept, taken = kept_ref[:, 2 * width :].astype(WIDE), taken_ref[:, 2 * width :].astype(WIDE)
    kept_max, taken_max = lanes(kept, 0), lanes(taken, 0)
    top = jnp.maximum(kept_max, taken_max)
    kept_scale, taken_scale = jnp.exp(kept_max - top), jnp.exp(taken_max - top)
    total = kept_scale * lanes(kept, 3) + taken_scale * lanes(taken, 3)
    slots = kept_scale * kept_ref[:, :width].astype(WIDE) + taken_scale * taken_ref[
        :, :width
    ].astype(WIDE)
    grads = kept_ref[:, width : 2 * width].astype(WIDE) + taken_ref[
        :, width : 2 * width
    ].astype(WIDE)
    pieces = place(split3(top) + split3(total), kept.shape, 1)
    peers, own = out_ref.shape[:2]
    out_ref[:, :, :width] = slots.astype(LOW).reshape(peers, own, width)
    out_ref[:, :, width : 2 * width] = grads.astype(LOW).reshape(peers, own, width)
    out_ref[:, :, 2 * width :] = pieces.astype(LOW).reshape(peers, own, EXTRA)


def merge(kept, taken, peers):
    shape = jax.ShapeDtypeStruct((peers, kept.shape[0] // peers, kept.shape[1]), LOW)
    return call(merge_kernel, "merge", (kept, taken), [IN_VMEM] * 2, IN_VMEM, shape)


def expert_kernel(got_ref, in_ref, out_ref, told_ref):
    w_in, w_out = in_ref[0], out_ref[0]
    peers, own, wide = got_ref.shape
    count, width = peers * own, w_in.shape[0]
    got = got_ref[...].reshape(count, wide)
    pieces = got[:, 2 * width :].astype(WIDE)
    block_max, block_sum = lanes(pieces, 0), lanes(pieces, 3)
    odd = lax.broadcasted_iota(jnp.int32, (count, 1), 0) % 2 == 1
    lowest = jnp.full((count, 1), -jnp.inf, WIDE)
    top = [
        jnp.max(jnp.where(odd, lowest, block_max), axis=0, keepdims=True),
        jnp.max(jnp.where(odd, block_max, lowest), axis=0, keepdims=True),
    ]
    scale = jnp.exp(block_max - jnp.where(odd, top[1], top[0]))
    scaled_sum = scale * block_sum
    totals = [
        jnp.sum(jnp.where(odd, 0.0, scaled_sum), axis=0, keepdims=True),
        jnp.sum(jnp.where(odd, scaled_sum, 0.0), axis=0, keepdims=True),
    ]
    scaled = scale * got[:, :width].astype(WIDE)
    exact = [
        jnp.sum(jnp.where(odd, 0.0, scaled), axis=0, keepdims=True) / totals[0],
        jnp.sum(jnp.where(odd, scaled, 0.0), axis=0, keepdims=True) / totals[1],
    ]
    sent = got[:, width : 2 * width].astype(WIDE)
    grads = [
        jnp.sum(jnp.where(odd, 0.0, sent), axis=0, keepdims=True),
        jnp.sum(jnp.where(odd, sent, 0.0), axis=0, keepdims=True),
    ]
    exact = place(exact, (8, width), 0)
    out_grad = place(grads, (8, width), 0).astype(LOW)
    slot_low = exact.astype(LOW)
    preact = product(slot_low, w_in, 1, 0)
    hid_grad = product(out_grad, w_out, 1, 1)
    rate = 0.7978845608028654
    square = preact * preact
    curve = jnp.tanh(rate * (preact + 0.044715 * square * preact))
    low_hidden = (0.5 * preact * (1.0 + curve)).astype(LOW)
    slope = 0.5 * (1.0 + curve) + 0.5 * preact * (1.0 - curve * curve) * rate * (
        1.0 + 3.0 * 0.044715 * square
    )
    pre_grad = (slope * hid_grad).astype(LOW)
    slot_out = product(low_hidden, w_out, 1, 0)
    in_grad = product(pre_grad, w_in, 1, 1)
    slot_product = jnp.sum(exact * in_grad, axis=1, keepdims=True)
    top = place(top, (8, 1), 0)
    totals = place(totals, (8, 1), 0)
    scalars = place(split3(slot_product) + split3(top) + split3(totals), (8, EXTRA), 1)
    spread = lambda block: jnp.broadcast_to(
        block[:own].astype(LOW)[None], (peers, own, block.shape[1])
    )
    told_ref[:, :, :width] = spread(slot_out)
    told_ref[:, :, width : 2 * width] = spread(in_grad)
    told_ref[:, :, 2 * width :] = spread(scalars)


def expert(got, w_in, w_out):
    shape = jax.ShapeDtypeStruct(got.shape, LOW)
    return call(expert_kernel, "expert", (got, w_in, w_out), [IN_VMEM] * 3, IN_VMEM, shape)


STEPS = 2


def closing_kernel(
    mine_ref, pair_ref, tok_ref, cot_ref, comb_ref, logit_ref, order_ref,
    mixed_hbm, grad_hbm,
    all_out, in_low, rows_ref, mixed_ref, grad_ref, out_sems,
):
    count, width = cot_ref.shape
    half = mine_ref.shape[0] * mine_ref.shape[1]
    block = count // STEPS
    for at, ref in enumerate((mine_ref, pair_ref)):
        part = slice(at * half, (at + 1) * half)
        all_out[part, :] = ref[:, :, :width].reshape(half, width)
        in_low[part, :] = ref[:, :, width : 2 * width].reshape(half, width)
        pieces = ref[:, :, 2 * width :].reshape(half, EXTRA).astype(WIDE).T
        for row in range(3):
            rows_ref[row : row + 1, part] = jnp.sum(
                pieces[3 * row : 3 * row + 3], axis=0, keepdims=True
            )
    slot_product, highest, totals = rows_ref[0:1], rows_ref[1:2], rows_ref[2:3]
    stores = []
    for step in range(STEPS):
        part = pl.ds(step * block, block)
        stores.append(
            pltpu.make_async_copy(mixed_ref.at[part], mixed_hbm.at[part], out_sems.at[0, step])
        )
        stores.append(
            pltpu.make_async_copy(grad_ref.at[part], grad_hbm.at[part], out_sems.at[1, step])
        )
        combine = comb_ref[part]
        mixed_ref[part, :] = product(combine.astype(LOW), all_out[...], 1, 0).astype(LOW)
        stores[-2].start()
        comb_grad = product(cot_ref[part], all_out[...], 1, 1)
        logit_grad = combine * (comb_grad - jnp.sum(combine * comb_grad, axis=1, keepdims=True))
        dispatch = jnp.exp(logit_ref[part] - highest) / totals
        logit_grad += dispatch * (product(tok_ref[part], in_low[...], 1, 1) - slot_product)
        token_grad = product(logit_grad.astype(LOW), order_ref[...], 1, 1)
        token_grad += product(dispatch.astype(LOW), in_low[...], 1, 0)
        grad_ref[part, :] = token_grad.astype(LOW)
        stores[-1].start()
    for copy in stores:
        copy.wait()


def closing(mine, pair, tokens, cotangent, combine, logits, weight):
    rows, width = cotangent.shape
    slots = weight.shape[1]
    return call(
        closing_kernel,
        "closing",
        (mine, pair, tokens, cotangent, combine, logits, weight),
        [IN_VMEM] * 7,
        [IN_HBM] * 2,
        [jax.ShapeDtypeStruct((rows, width), LOW)] * 2,
        [
            pltpu.VMEM((slots, width), LOW),
            pltpu.VMEM((slots, width), LOW),
            pltpu.VMEM((8, slots), WIDE),
            pltpu.VMEM((rows, width), LOW),
            pltpu.VMEM((rows, width), LOW),
            pltpu.SemaphoreType.DMA((2, STEPS)),
        ],
    )


def shards(tokens, slot_weight, w_in, w_out, cotangent):
    torus = ("x", "z", "exp")
    swap = [(0, 1), (1, 0)]
    at = jnp.stack([lax.axis_index("exp"), lax.axis_index("core")]).astype(jnp.int32)
    peers = lax.axis_size(torus)
    kept, given, combine, logits, weight, rows, cot = opening(at, tokens, slot_weight, cotangent)
    sent = merge(kept, lax.ppermute(given, "core", swap), peers)
    got = lax.all_to_all(sent, torus, split_axis=0, concat_axis=0, tiled=True)
    told = expert(got, w_in, w_out)
    told = lax.all_to_all(told, torus, split_axis=0, concat_axis=0, tiled=True)
    pair = lax.ppermute(told, "core", swap)
    return tuple(closing(told, pair, rows, cot, combine, logits, weight))


def solution(mesh):
    exp = mesh.devices.shape[1]
    finer = Mesh(mesh.devices.reshape(4, 4, 2, exp), ("x", "z", "core", "exp"))
    every = ("x", "z", "core", "exp")
    rows = P(every, None)
    experts = P(every, None, None)
    return jax.shard_map(
        shards,
        mesh=finer,
        in_specs=(P(("x", "z", "core"), None), P(), experts, experts, rows),
        out_specs=(rows, rows),
        check_vma=False,
    )
```

time: 84.9 us -> 68 us (0.80)
  local copies, waits for them, and re-layouts: 17.9 us -> 2.86 us
  Pallas kernels: 15.2 us -> 13.7 us
    unnamed x18 -> x4, local copies, waits for them, and re-layouts: 14.9 us -> 2.86 us
    reshape x3 -> x0, local copies, waits for them, and re-layouts: 2.65 us -> none  [the longest x1 2.13 us: shards(): told = told.reshape(half, -1)]
    pallas_call x4, Pallas kernels: 15.2 us -> 13.7 us  [call(): pl.pallas_call(kernel, in_specs=specs, out_specs=out_specs, out_shape=out...]
where the time goes in v2:
time: 68 us; the launch traced here: 67.7 us
  blocking collectives  42.2 us (62%)
  Pallas kernels  13.7 us (20%)
  starting transfers between devices  4.69 us (7%)
  waiting for transfers between devices  3.54 us (5%)
  local copies, waits for them, and re-layouts  2.86 us (4%)
    all_to_all x1, blocking collectives, shards(): got = lax.all_to_all(sent, torus, split_axis=0, concat_axis=0, tiled=True)  24.6 us
    all_to_all x1, blocking collectives, shards(): told = lax.all_to_all(told, torus, split_axis=0, concat_axis=0, tiled=True)  17.5 us
    pallas_call x4, Pallas kernels, call(): pl.pallas_call(kernel, in_specs=specs, out_specs=out_specs, out_shape=out...  13.7 us
    ppermute x1, starting transfers between devices, shards(): pair = lax.ppermute(told, 'core', swap)  3.18 us
    unnamed x4, local copies, waits for them, and re-layouts  2.86 us
    ppermute x1, waiting for transfers between devices, shards(): pair = lax.ppermute(told, 'core', swap)  1.77 us
    ppermute x1, waiting for transfers between devices, shards(): sent = merge(kept, lax.ppermute(given, 'core', swap), peers)  1.77 us
    ppermute x1, starting transfers between devices, shards(): sent = merge(kept, lax.ppermute(given, 'core', swap), peers)  1.5 us
  transfers between devices with their start and end apart: 2, of which 2 were waited for; matrix products, arithmetic and copies ran while one was open for 0% of the time, Pallas kernels for 0%

profile of v2, /device:TPU:1, one launch (start us, length us, event | category | flops | bytes accessed | tf_op | source)
XLA Modules:
  0.0 67.7 jit_solution(14922119501648879751)
XLA Ops:
  0.6 0.1 pad_add_fusion.at_ref
  0.7 0.0 copy-start
  0.7 4.6 %opening.1 = (bf16[128,2688]{1,0:T(8,128)(2,1)S(1)}, bf16[128,2688]{1,0:T(8,128)(2,1)S(1)}, f32[512,256]{1,0:T(8,128)S(1)}, f32[512,256]{1,0:T(8,128)S(1)}, bf16...) custom-call(s32[2]{0:T(128)S(1)} %pad_add_fusion.at_ref, ...), custom_call_target="tpu_custom_call" | custom-call | tf_op jit(solution)/shard_map/opening/pallas_call | solution.py:54
  5.3 1.5 %collective-permute-start = (bf16[128,2688]{1,0:T(8,128)(2,1)S(1)}, bf16[128,2688]{1,0:T(8,128)(2,1)S(1)}, u32[]{:S(2)}, u32[]{:S(2)}) collective-permute-start(bf16[128,2688]{1,0:T(8,128)(2,1)S(1)} %get-tuple-element.10), channel_id=1, source_target_pairs={{0,4},{4,0},{1,5},{5,1},{2,6},{6,2},{3,7},{7,3},{8,12},{12,8},{9,1... | collective-permute-start | bytes 2064392 | tf_op jit(solution)/shard_map/ppermute | solution.py:295
  6.8 1.8 %collective-permute-done.taken_ref = bf16[128,2688]{1,0:T(8,128)(2,1)S(1)} collective-permute-done((bf16[128,2688]{1,0:T(8,128)(2,1)S(1)}, bf16[128,2688]{1,0:T(8,128)(2,1)S(1)}, u32[]{:S(2)}, u32[]{:S(2)}) %collective-permute-start) | collective-permute-done | bytes 688160 | tf_op jit(solution)/shard_map/ppermute | solution.py:295
  8.6 0.5 merge.1
  9.1 24.6 %all_to_all.10.got_ref = bf16[64,2,2688]{2,1,0:T(2,128)(2,1)S(1)} all-to-all(bf16[64,2,2688]{2,1,0:T(2,128)(2,1)S(1)} %merge.1), channel_id=1, replica_groups=mesh['x'=4,'z'=4,'core'=2,'exp'=4] {'x','z','exp'}, dimensions={0} | all-to-all | bytes 1376256 | tf_op jit(solution)/shard_map/all_to_all | solution.py:296
  33.8 0.0 copy-done
  33.8 0.0 copy-start.1
  33.8 2.9 %copy-done.1 = bf16[1,2560,1280]{2,1,0:T(8,128)(2,1)S(1)} copy-done((bf16[1,2560,1280]{2,1,0:T(8,128)(2,1)S(1)}, bf16[1,2560,1280]{2,1,0:T(8,128)(2,1)}, u32[]{:S(2)}) %copy-start.1) | copy-done | bytes 6553624
  36.6 5.7 %expert.1 = bf16[64,2,2688]{2,1,0:T(2,128)(2,1)S(1)} custom-call(bf16[64,2,2688]{2,1,0:T(2,128)(2,1)S(1)} %all_to_all.10.got_ref, bf16[1,1280,2560]{2,1,0:T(8,128)(2,1)S(1)} %copy-done, bf16[1,2560,1280]{2,1,0:T(8,128)(2,1)S(1)} %copy-done.1), custom_call_target="tpu_custom_call" | custom-call | tf_op jit(solution)/shard_map/expert/pallas_call | solution.py:54
  42.4 17.5 %all_to_all.11.mine_ref = bf16[64,2,2688]{2,1,0:T(2,128)(2,1)S(1)} all-to-all(bf16[64,2,2688]{2,1,0:T(2,128)(2,1)S(1)} %expert.1), channel_id=1, replica_groups=mesh['x'=4,'z'=4,'core'=2,'exp'=4] {'x','z','exp'}, dimensions={0} | all-to-all | bytes 1376256 | tf_op jit(solution)/shard_map/all_to_all | solution.py:298
  59.9 3.2 %collective-permute-start.1 = (bf16[64,2,2688]{2,1,0:T(2,128)(2,1)S(1)}, bf16[64,2,2688]{2,1,0:T(2,128)(2,1)S(1)}, u32[]{:S(2)}, u32[]{:S(2)}) collective-permute-start(bf16[64,2,2688]{2,1,0:T(2,128)(2,1)S(1)} %all_to_all.11.mine_ref), channel_id=1, source_target_pairs={{0,4},{4,0},{1,5},{5,1},{2,6},{6,2},{3,7},{7,3},{8,12},{12,8},{9,1... | collective-permute-start | bytes 2064392 | tf_op jit(solution)/shard_map/ppermute | solution.py:299
  63.1 1.8 %collective-permute-done.1.pair_ref = bf16[64,2,2688]{2,1,0:T(2,128)(2,1)S(1)} collective-permute-done((bf16[64,2,2688]{2,1,0:T(2,128)(2,1)S(1)}, bf16[64,2,2688]{2,1,0:T(2,128)(2,1)S(1)}, u32[]{:S(2)}, u32[]{:S(2)}) %collective-permute-start.1) | collective-permute-done | bytes 688160 | tf_op jit(solution)/shard_map/ppermute | solution.py:299
  64.8 2.9 %closing.1 = (bf16[512,1280]{1,0:T(8,128)(2,1)}, bf16[512,1280]{1,0:T(8,128)(2,1)}) custom-call(bf16[64,2,2688]{2,1,0:T(2,128)(2,1)S(1)} %all_to_all.11.mine_ref, bf16[64,2,2688]{2,1,0:T(2,128)(2,1)S(1)} %collective-permute-done.1.pair_ref, bf16[512,1280]{1,0:T(8,128)(2,1)S(1)} %get-tuple-element.11.tok_ref, ...), custom_call_target="tpu_custom_call" | custom-call | tf_op jit(solution)/shard_map/closing/pallas_call | solution.py:54
Async XLA Ops:
  0.7 33.1 %copy-start = (bf16[1,1280,2560]{2,1,0:T(8,128)(2,1)S(1)}, bf16[1,1280,2560]{2,1,0:T(8,128)(2,1)}, u32[]{:S(2)}) copy-start(bf16[1,1280,2560]{2,1,0:T(8,128)(2,1)} %in_ref.1) | copy-start | bytes 19660804
  5.3 3.3 %collective-permute-start = (bf16[128,2688]{1,0:T(8,128)(2,1)S(1)}, bf16[128,2688]{1,0:T(8,128)(2,1)S(1)}, u32[]{:S(2)}, u32[]{:S(2)}) collective-permute-start(bf16[128,2688]{1,0:T(8,128)(2,1)S(1)} %get-tuple-element.10), channel_id=1, source_target_pairs={{0,4},{4,0},{1,5},{5,1},{2,6},{6,2},{3,7},{7,3},{8,12},{12,8},{9,1... | collective-permute-start | bytes 2064392 | tf_op jit(solution)/shard_map/ppermute | solution.py:295
  33.8 2.9 %copy-start.1 = (bf16[1,2560,1280]{2,1,0:T(8,128)(2,1)S(1)}, bf16[1,2560,1280]{2,1,0:T(8,128)(2,1)}, u32[]{:S(2)}) copy-start(bf16[1,2560,1280]{2,1,0:T(8,128)(2,1)} %out_ref.1) | copy-start | bytes 19660804
  59.9 5.0 %collective-permute-start.1 = (bf16[64,2,2688]{2,1,0:T(2,128)(2,1)S(1)}, bf16[64,2,2688]{2,1,0:T(2,128)(2,1)S(1)}, u32[]{:S(2)}, u32[]{:S(2)}) collective-permute-start(bf16[64,2,2688]{2,1,0:T(2,128)(2,1)S(1)} %all_to_all.11.mine_ref), channel_id=1, source_target_pairs={{0,4},{4,0},{1,5},{5,1},{2,6},{6,2},{3,7},{7,3},{8,12},{12,8},{9,1... | collective-permute-start | bytes 2064392 | tf_op jit(solution)/shard_map/ppermute | solution.py:299

commit v3 on v2

--- a/solution.py
+++ b/solution.py
@@ -50,7 +50,10 @@
     return pltpu.with_memory_space_constraint(array, pltpu.HBM)
 
 
-def call(kernel, name, args, specs, out_specs, out_shape, scratch=()):
+SPAN = pl.CostEstimate(flops=9_000_000_000, bytes_accessed=20_000_000, transcendentals=0)
+
+
+def call(kernel, name, args, specs, out_specs, out_shape, scratch=(), cost=None):
     return pl.pallas_call(
         kernel,
         in_specs=specs,
@@ -58,13 +61,14 @@
         out_shape=out_shape,
         scratch_shapes=scratch,
         compiler_params=pltpu.CompilerParams(vmem_limit_bytes=LIMIT),
+        cost_estimate=cost,
         name=name,
     )(*args)
 
 
 def ordering(core, slots):
-    to = lax.broadcasted_iota(jnp.int32, (slots, slots), 1)
-    source = lax.broadcasted_iota(jnp.int32, (slots, slots), 0)
+    to = lax.broadcasted_iota(jnp.int32, (slots, 1), 0)
+    source = lax.broadcasted_iota(jnp.int32, (slots, slots), 1)
     half = slots // 2
     within = to % half
     other = jnp.where(to // half == 0, core, 1 - core)
@@ -73,8 +77,7 @@
 
 
 def opening_kernel(
-    at_ref, tok_hbm, weight_hbm, cot_hbm,
-    kept_ref, given_ref, comb_ref, logit_ref, order_ref, rows_ref, cot_ref,
+    at_ref, tok_hbm, weight_hbm, cot_hbm, kept_ref, given_ref, order_ref, rows_ref, cot_ref,
     weight_ref, sems,
 ):
     slots = weight_ref.shape[1]
@@ -95,22 +98,20 @@
         copy.start()
     order = ordering(at_ref[1], slots)
     loads[0].wait()
-    weight = product(weight_ref[...], order, 1, 0).astype(LOW)
+    weight = product(order, weight_ref[...], 1, 1).astype(LOW)
     order_ref[...] = weight
     loads[1].wait()
     rows = rows_ref[...]
-    logits = product(rows, weight, 1, 0)
-    logit_ref[...] = logits
-    col_max = jnp.max(logits, axis=0, keepdims=True)
-    shifted = jnp.exp(logits - col_max)
-    col_sum = jnp.sum(shifted, axis=0, keepdims=True)
-    slot_part = product(shifted.astype(LOW), rows, 0, 0)
-    raised = jnp.exp(logits - jnp.max(logits, axis=1, keepdims=True))
-    combine = raised / jnp.sum(raised, axis=1, keepdims=True)
-    comb_ref[...] = combine
+    logits = product(weight, rows, 1, 1)
+    slot_max = jnp.max(logits, axis=1, keepdims=True)
+    shifted = jnp.exp(logits - slot_max)
+    slot_sum = jnp.sum(shifted, axis=1, keepdims=True)
+    slot_part = product(shifted.astype(LOW), rows, 1, 0)
+    raised = jnp.exp(logits - jnp.max(logits, axis=0, keepdims=True))
+    combine = raised * (1.0 / jnp.sum(raised, axis=0, keepdims=True))
     loads[2].wait()
-    grad_part = product(combine.astype(LOW), cot_ref[...], 0, 0)
-    pieces = place(split3(col_max) + split3(col_sum), (EXTRA, slots), 0).T
+    grad_part = product(combine.astype(LOW), cot_ref[...], 1, 0)
+    pieces = place(split3(slot_max) + split3(slot_sum), (slots, EXTRA), 1)
     for at, out in enumerate((kept_ref, given_ref)):
         part = slice(at * half, (at + 1) * half)
         out[:, :width] = slot_part[part].astype(LOW)
@@ -121,16 +122,30 @@
 def opening(at, tokens, slot_weight, cotangent):
     rows, width = cotangent.shape
     slots = slot_weight.shape[1]
-    shapes = [((slots // 2, 2 * width + EXTRA), LOW)] * 2
-    shapes += [((rows, slots), WIDE)] * 2 + [((width, slots), LOW)] + [((rows, width), LOW)] * 2
+    shapes = [(slots // 2, 2 * width + EXTRA)] * 2 + [(slots, width)] + [(rows, width)] * 2
     return call(
         opening_kernel,
         "opening",
         (at, stay(tokens), stay(slot_weight), stay(cotangent)),
         [IN_SMEM] + [IN_HBM] * 3,
         [IN_VMEM] * len(shapes),
-        [jax.ShapeDtypeStruct(*shape) for shape in shapes],
+        [jax.ShapeDtypeStruct(shape, LOW) for shape in shapes],
         [pltpu.VMEM((width, slots), LOW), pltpu.SemaphoreType.DMA((3,))],
+    )
+
+
+def combine_kernel(rows_ref, order_ref, logit_ref, comb_ref):
+    logits = product(rows_ref[...], order_ref[...], 1, 1)
+    logit_ref[...] = logits
+    raised = jnp.exp(logits - jnp.max(logits, axis=1, keepdims=True))
+    comb_ref[...] = raised * (1.0 / jnp.sum(raised, axis=1, keepdims=True))
+
+
+def combining(rows, order):
+    shape = jax.ShapeDtypeStruct((rows.shape[0], order.shape[0]), WIDE)
+    cost = pl.CostEstimate(flops=1_000_000_000, bytes_accessed=4_000_000, transcendentals=131_072)
+    return call(
+        combine_kernel, "combining", (rows, order), [IN_VMEM] * 2, [IN_VMEM] * 2, [shape] * 2, (), cost
     )
 
 
@@ -156,7 +171,7 @@
 
 def merge(kept, taken, peers):
     shape = jax.ShapeDtypeStruct((peers, kept.shape[0] // peers, kept.shape[1]), LOW)
-    return call(merge_kernel, "merge", (kept, taken), [IN_VMEM] * 2, IN_VMEM, shape)
+    return call(merge_kernel, "merge", (kept, taken), [IN_VMEM] * 2, IN_VMEM, shape, (), SPAN)
 
 
 def expert_kernel(got_ref, in_ref, out_ref, told_ref):
@@ -220,17 +235,24 @@
     return call(expert_kernel, "expert", (got, w_in, w_out), [IN_VMEM] * 3, IN_VMEM, shape)
 
 
-STEPS = 2
+COLUMNS = (slice(0, 768), slice(768, 1280))
 
 
 def closing_kernel(
     mine_ref, pair_ref, tok_ref, cot_ref, comb_ref, logit_ref, order_ref,
     mixed_hbm, grad_hbm,
-    all_out, in_low, rows_ref, mixed_ref, grad_ref, out_sems,
+    all_out, in_low, rows_ref, mixed_ref, grad_ref, sems,
 ):
-    count, width = cot_ref.shape
+    width = cot_ref.shape[1]
     half = mine_ref.shape[0] * mine_ref.shape[1]
-    block = count // STEPS
+    stores = []
+
+    def store(source, target, columns):
+        at = len(stores)
+        where = (slice(None), pl.ds(columns.start, columns.stop - columns.start))
+        stores.append(pltpu.make_async_copy(source.at[where], target.at[where], sems.at[at]))
+        stores[at].start()
+
     for at, ref in enumerate((mine_ref, pair_ref)):
         part = slice(at * half, (at + 1) * half)
         all_out[part, :] = ref[:, :, :width].reshape(half, width)
@@ -241,33 +263,28 @@
                 pieces[3 * row : 3 * row + 3], axis=0, keepdims=True
             )
     slot_product, highest, totals = rows_ref[0:1], rows_ref[1:2], rows_ref[2:3]
-    stores = []
-    for step in range(STEPS):
-        part = pl.ds(step * block, block)
-        stores.append(
-            pltpu.make_async_copy(mixed_ref.at[part], mixed_hbm.at[part], out_sems.at[0, step])
-        )
-        stores.append(
-            pltpu.make_async_copy(grad_ref.at[part], grad_hbm.at[part], out_sems.at[1, step])
-        )
-        combine = comb_ref[part]
-        mixed_ref[part, :] = product(combine.astype(LOW), all_out[...], 1, 0).astype(LOW)
-        stores[-2].start()
-        comb_grad = product(cot_ref[part], all_out[...], 1, 1)
-        logit_grad = combine * (comb_grad - jnp.sum(combine * comb_grad, axis=1, keepdims=True))
-        dispatch = jnp.exp(logit_ref[part] - highest) / totals
-        logit_grad += dispatch * (product(tok_ref[part], in_low[...], 1, 1) - slot_product)
-        token_grad = product(logit_grad.astype(LOW), order_ref[...], 1, 1)
-        token_grad += product(dispatch.astype(LOW), in_low[...], 1, 0)
-        grad_ref[part, :] = token_grad.astype(LOW)
-        stores[-1].start()
+    combine = comb_ref[...]
+    combine_low = combine.astype(LOW)
+    for columns in COLUMNS:
+        mixed_ref[:, columns] = product(combine_low, all_out[:, columns], 1, 0).astype(LOW)
+        store(mixed_ref, mixed_hbm, columns)
+    comb_grad = product(cot_ref[...], all_out[...], 1, 1)
+    logit_grad = combine * (comb_grad - jnp.sum(combine * comb_grad, axis=1, keepdims=True))
+    dispatch = jnp.exp(logit_ref[...] - highest) * (1.0 / totals)
+    logit_grad += dispatch * (product(tok_ref[...], in_low[...], 1, 1) - slot_product)
+    logit_low, dispatch_low = logit_grad.astype(LOW), dispatch.astype(LOW)
+    for columns in COLUMNS:
+        token_grad = product(logit_low, order_ref[:, columns], 1, 0)
+        token_grad += product(dispatch_low, in_low[:, columns], 1, 0)
+        grad_ref[:, columns] = token_grad.astype(LOW)
+        store(grad_ref, grad_hbm, columns)
     for copy in stores:
         copy.wait()
 
 
 def closing(mine, pair, tokens, cotangent, combine, logits, weight):
     rows, width = cotangent.shape
-    slots = weight.shape[1]
+    slots = weight.shape[0]
     return call(
         closing_kernel,
         "closing",
@@ -281,7 +298,7 @@
             pltpu.VMEM((8, slots), WIDE),
             pltpu.VMEM((rows, width), LOW),
             pltpu.VMEM((rows, width), LOW),
-            pltpu.SemaphoreType.DMA((2, STEPS)),
+            pltpu.SemaphoreType.DMA((2 * len(COLUMNS),)),
         ],
     )
 
@@ -291,7 +308,8 @@
     swap = [(0, 1), (1, 0)]
     at = jnp.stack([lax.axis_index("exp"), lax.axis_index("core")]).astype(jnp.int32)
     peers = lax.axis_size(torus)
-    kept, given, combine, logits, weight, rows, cot = opening(at, tokens, slot_weight, cotangent)
+    kept, given, weight, rows, cot = opening(at, tokens, slot_weight, cotangent)
+    logits, combine = combining(rows, weight)
     sent = merge(kept, lax.ppermute(given, "core", swap), peers)
     got = lax.all_to_all(sent, torus, split_axis=0, concat_axis=0, tiled=True)
     told = expert(got, w_in, w_out)

time: 68 us -> 65.3 us (0.960)
  local copies, waits for them, and re-layouts: 2.86 us -> 0.01 us
  waiting for transfers between devices: 3.54 us -> 2.83 us
  Pallas kernels: 13.7 us -> 14.4 us
    unnamed x4 -> x8, local copies, waits for them, and re-layouts: 2.86 us -> 0.01 us
    ppermute x1, waiting for transfers between devices: 1.77 us -> 1.06 us  [shards(): pair = lax.ppermute(told, 'core', swap)]
    pallas_call x4 -> x5, Pallas kernels: 13.7 us -> 14.4 us  [call(): pl.pallas_call(kernel, in_specs=specs, out_specs=out_specs, out_shape=out...]
  transfers between devices with their start and end apart: 2 -> 2, of which waited for: 2 -> 2; matrix products, arithmetic and copies ran while one was open for 0% -> 0% of each run, Pallas kernels for 0% -> 1%
where the time goes in v3:
time: 65.3 us; the launch traced here: 65.1 us
  blocking collectives  42.4 us (65%)
  Pallas kernels  14.4 us (22%)
  starting transfers between devices  4.68 us (7%)
  waiting for transfers between devices  2.83 us (4%)
  between operations  0.7 us (1%)
    all_to_all x1, blocking collectives, shards(): got = lax.all_to_all(sent, torus, split_axis=0, concat_axis=0, tiled=True)  24.9 us
    all_to_all x1, blocking collectives, shards(): told = lax.all_to_all(told, torus, split_axis=0, concat_axis=0, tiled=True)  17.5 us
    pallas_call x5, Pallas kernels, call(): pl.pallas_call(kernel, in_specs=specs, out_specs=out_specs, out_shape=out...  14.4 us
    ppermute x1, starting transfers between devices, shards(): pair = lax.ppermute(told, 'core', swap)  3.18 us
    ppermute x1, waiting for transfers between devices, shards(): sent = merge(kept, lax.ppermute(given, 'core', swap), peers)  1.77 us
    ppermute x1, starting transfers between devices, shards(): sent = merge(kept, lax.ppermute(given, 'core', swap), peers)  1.5 us
  transfers between devices with their start and end apart: 2, of which 2 were waited for; matrix products, arithmetic and copies ran while one was open for 0% of the time, Pallas kernels for 1%

profile of v3, /device:TPU:1, one launch (start us, length us, event | category | flops | bytes accessed | tf_op | source)
XLA Modules:
  0.0 65.1 jit_solution(11753533856430545520)
XLA Ops:
  0.6 0.1 pad_add_fusion.at_ref
  0.7 0.0 slice-start
  0.7 0.0 slice-start.2
  0.7 4.3 %opening.1 = (bf16[128,2688]{1,0:T(8,128)(2,1)S(1)}, bf16[128,2688]{1,0:T(8,128)(2,1)S(1)}, bf16[256,1280]{1,0:T(8,128)(2,1)S(1)}, bf16[512,1280]{1,0:T(8,128)(2,1)S(1)}, bf16[512,1280]{1,0:T(8,128)(2,1)S(1)}) custom-call(s32[2]{0:T(128)S(1)} %pad_add_fusion.at_ref, bf16[2048,1280]{1,0:T(8,128)(2,1)} %tok_hbm.1, bf16[1280,256]{1,0:T(8,128)(2,1)} %weight_hbm.1, ...), custom_call_target="tpu_custom_call" | custom-call | tf_op jit(solution)/shard_map/opening/pallas_call | solution.py:57
  5.0 1.5 %collective-permute-start = (bf16[128,2688]{1,0:T(8,128)(2,1)S(1)}, bf16[128,2688]{1,0:T(8,128)(2,1)S(1)}, u32[]{:S(2)}, u32[]{:S(2)}) collective-permute-start(bf16[128,2688]{1,0:T(8,128)(2,1)S(1)} %get-tuple-element.10), channel_id=1, source_target_pairs={{0,4},{4,0},{1,5},{5,1},{2,6},{6,2},{3,7},{7,3},{8,12},{12,8},{9,1... | collective-permute-start | bytes 2064392 | tf_op jit(solution)/shard_map/ppermute | solution.py:313
  6.5 1.8 %collective-permute-done.taken_ref = bf16[128,2688]{1,0:T(8,128)(2,1)S(1)} collective-permute-done((bf16[128,2688]{1,0:T(8,128)(2,1)S(1)}, bf16[128,2688]{1,0:T(8,128)(2,1)S(1)}, u32[]{:S(2)}, u32[]{:S(2)}) %collective-permute-start) | collective-permute-done | bytes 688160 | tf_op jit(solution)/shard_map/ppermute | solution.py:313
  8.3 0.0 slice-start.1
  8.3 0.0 slice-start.3
  8.3 0.5 merge.1
  8.8 24.9 %all_to_all.10.got_ref = bf16[64,2,2688]{2,1,0:T(2,128)(2,1)S(1)} all-to-all(bf16[64,2,2688]{2,1,0:T(2,128)(2,1)S(1)} %merge.1), channel_id=1, replica_groups=mesh['x'=4,'z'=4,'core'=2,'exp'=4] {'x','z','exp'}, dimensions={0} | all-to-all | bytes 1376256 | tf_op jit(solution)/shard_map/all_to_all | solution.py:314
  33.7 0.0 slice-done
  33.7 0.0 slice-done.2
  33.7 0.0 slice-done.1
  33.7 0.0 slice-done.3
  33.8 5.7 %expert.1 = bf16[64,2,2688]{2,1,0:T(2,128)(2,1)S(1)} custom-call(bf16[64,2,2688]{2,1,0:T(2,128)(2,1)S(1)} %all_to_all.10.got_ref, bf16[1,1280,2560]{2,1,0:T(8,128)(2,1)S(1)} %bitcast.3, bf16[1,2560,1280]{2,1,0:T(8,128)(2,1)S(1)} %bitcast.5), custom_call_target="tpu_custom_call" | custom-call | tf_op jit(solution)/shard_map/expert/pallas_call | solution.py:57
  39.5 17.5 %all_to_all.11.mine_ref = bf16[64,2,2688]{2,1,0:T(2,128)(2,1)S(1)} all-to-all(bf16[64,2,2688]{2,1,0:T(2,128)(2,1)S(1)} %expert.1), channel_id=1, replica_groups=mesh['x'=4,'z'=4,'core'=2,'exp'=4] {'x','z','exp'}, dimensions={0} | all-to-all | bytes 1376256 | tf_op jit(solution)/shard_map/all_to_all | solution.py:316
  57.0 3.2 %collective-permute-start.1 = (bf16[64,2,2688]{2,1,0:T(2,128)(2,1)S(1)}, bf16[64,2,2688]{2,1,0:T(2,128)(2,1)S(1)}, u32[]{:S(2)}, u32[]{:S(2)}) collective-permute-start(bf16[64,2,2688]{2,1,0:T(2,128)(2,1)S(1)} %all_to_all.11.mine_ref), channel_id=1, source_target_pairs={{0,4},{4,0},{1,5},{5,1},{2,6},{6,2},{3,7},{7,3},{8,12},{12,8},{9,1... | collective-permute-start | bytes 2064392 | tf_op jit(solution)/shard_map/ppermute | solution.py:317
  60.2 0.7 %combining.1 = (f32[512,256]{1,0:T(8,128)S(1)}, f32[512,256]{1,0:T(8,128)S(1)}) custom-call(bf16[512,1280]{1,0:T(8,128)(2,1)S(1)} %get-tuple-element.11.rows_ref.tok_ref, bf16[256,1280]{1,0:T(8,128)(2,1)S(1)} %get-tuple-element.13.order_ref), custom_call_target="tpu_custom_call" | custom-call | flops 1000000000 | bytes 4000000 | tf_op jit(solution)/shard_map/combining/pallas_call | solution.py:57
  60.9 1.1 %collective-permute-done.1.pair_ref = bf16[64,2,2688]{2,1,0:T(2,128)(2,1)S(1)} collective-permute-done((bf16[64,2,2688]{2,1,0:T(2,128)(2,1)S(1)}, bf16[64,2,2688]{2,1,0:T(2,128)(2,1)S(1)}, u32[]{:S(2)}, u32[]{:S(2)}) %collective-permute-start.1) | collective-permute-done | bytes 688160 | tf_op jit(solution)/shard_map/ppermute | solution.py:317
  62.0 3.1 %closing.1 = (bf16[512,1280]{1,0:T(8,128)(2,1)}, bf16[512,1280]{1,0:T(8,128)(2,1)}) custom-call(bf16[64,2,2688]{2,1,0:T(2,128)(2,1)S(1)} %all_to_all.11.mine_ref, bf16[64,2,2688]{2,1,0:T(2,128)(2,1)S(1)} %collective-permute-done.1.pair_ref, bf16[512,1280]{1,0:T(8,128)(2,1)S(1)} %get-tuple-element.11.rows_ref.tok_ref, ...), custom_call_target="tpu_custom_call" | custom-call | tf_op jit(solution)/shard_map/closing/pallas_call | solution.py:57
  (2 shorter events, 0.0 us)
Async XLA Ops:
  0.7 33.0 %slice-start = ((s8[6553600]{0:T(1024)(128)(4,1)}), s8[4194304]{0:T(1024)(128)(4,1)S(1)}, s32[]{:S(2)}) async-start(s8[6553600]{0:T(1024)(128)(4,1)} %bitcast.2), calls=%async_computation.2 | async-start | bytes 8388608
  0.7 33.0 %slice-start.2 = ((s8[6553600]{0:T(1024)(128)(4,1)}), s8[2359296]{0:T(1024)(128)(4,1)S(1)}, s32[]{:S(2)}) async-start(s8[6553600]{0:T(1024)(128)(4,1)} %bitcast.4), calls=%async_computation.4 | async-start | bytes 4718592
  5.0 3.3 %collective-permute-start = (bf16[128,2688]{1,0:T(8,128)(2,1)S(1)}, bf16[128,2688]{1,0:T(8,128)(2,1)S(1)}, u32[]{:S(2)}, u32[]{:S(2)}) collective-permute-start(bf16[128,2688]{1,0:T(8,128)(2,1)S(1)} %get-tuple-element.10), channel_id=1, source_target_pairs={{0,4},{4,0},{1,5},{5,1},{2,6},{6,2},{3,7},{7,3},{8,12},{12,8},{9,1... | collective-permute-start | bytes 2064392 | tf_op jit(solution)/shard_map/ppermute | solution.py:313
  8.3 25.4 %slice-start.1 = ((s8[6553600]{0:T(1024)(128)(4,1)}), s8[2359296]{0:T(1024)(128)(4,1)S(1)}, s32[]{:S(2)}) async-start(s8[6553600]{0:T(1024)(128)(4,1)} %bitcast.2), calls=%async_computation.3 | async-start | bytes 4718592
  8.3 25.4 %slice-start.3 = ((s8[6553600]{0:T(1024)(128)(4,1)}), s8[4194304]{0:T(1024)(128)(4,1)S(1)}, s32[]{:S(2)}) async-start(s8[6553600]{0:T(1024)(128)(4,1)} %bitcast.4), calls=%async_computation.5 | async-start | bytes 8388608
  57.0 5.0 %collective-permute-start.1 = (bf16[64,2,2688]{2,1,0:T(2,128)(2,1)S(1)}, bf16[64,2,2688]{2,1,0:T(2,128)(2,1)S(1)}, u32[]{:S(2)}, u32[]{:S(2)}) collective-permute-start(bf16[64,2,2688]{2,1,0:T(2,128)(2,1)S(1)} %all_to_all.11.mine_ref), channel_id=1, source_target_pairs={{0,4},{4,0},{1,5},{5,1},{2,6},{6,2},{3,7},{7,3},{8,12},{12,8},{9,1... | collective-permute-start | bytes 2064392 | tf_op jit(solution)/shard_map/ppermute | solution.py:317

commit v4 on v2

--- a/solution.py
+++ b/solution.py
@@ -50,7 +50,10 @@
     return pltpu.with_memory_space_constraint(array, pltpu.HBM)
 
 
-def call(kernel, name, args, specs, out_specs, out_shape, scratch=()):
+SPAN = pl.CostEstimate(flops=9_000_000_000, bytes_accessed=20_000_000, transcendentals=0)
+
+
+def call(kernel, name, args, specs, out_specs, out_shape, scratch=(), cost=None):
     return pl.pallas_call(
         kernel,
         in_specs=specs,
@@ -58,13 +61,14 @@
         out_shape=out_shape,
         scratch_shapes=scratch,
         compiler_params=pltpu.CompilerParams(vmem_limit_bytes=LIMIT),
+        cost_estimate=cost,
         name=name,
     )(*args)
 
 
 def ordering(core, slots):
-    to = lax.broadcasted_iota(jnp.int32, (slots, slots), 1)
-    source = lax.broadcasted_iota(jnp.int32, (slots, slots), 0)
+    to = lax.broadcasted_iota(jnp.int32, (slots, 1), 0)
+    source = lax.broadcasted_iota(jnp.int32, (slots, slots), 1)
     half = slots // 2
     within = to % half
     other = jnp.where(to // half == 0, core, 1 - core)
@@ -72,13 +76,18 @@
     return (source == wanted).astype(WIDE).astype(LOW)
 
 
+def halves(value, outs, columns):
+    half = outs[0].shape[0]
+    for at, out in enumerate(outs):
+        out[:, columns] = value[at * half : (at + 1) * half].astype(LOW)
+
+
 def opening_kernel(
     at_ref, tok_hbm, weight_hbm, cot_hbm,
-    kept_ref, given_ref, comb_ref, logit_ref, order_ref, rows_ref, cot_ref,
+    kept_ref, given_ref, logit_ref, order_ref, rows_ref, cot_ref,
     weight_ref, sems,
 ):
     slots = weight_ref.shape[1]
-    half = slots // 2
     count, width = rows_ref.shape
     start = pl.multiple_of(at_ref[0] * count, count)
     loads = [
@@ -91,38 +100,32 @@
             )
         )
     ]
-    for copy in loads:
-        copy.start()
+    loads[0].start()
+    loads[1].start()
     order = ordering(at_ref[1], slots)
     loads[0].wait()
-    weight = product(weight_ref[...], order, 1, 0).astype(LOW)
+    weight = product(order, weight_ref[...], 1, 1).astype(LOW)
     order_ref[...] = weight
     loads[1].wait()
+    loads[2].start()
     rows = rows_ref[...]
-    logits = product(rows, weight, 1, 0)
+    logits = product(weight, rows, 1, 1)
     logit_ref[...] = logits
-    col_max = jnp.max(logits, axis=0, keepdims=True)
-    shifted = jnp.exp(logits - col_max)
-    col_sum = jnp.sum(shifted, axis=0, keepdims=True)
-    slot_part = product(shifted.astype(LOW), rows, 0, 0)
-    raised = jnp.exp(logits - jnp.max(logits, axis=1, keepdims=True))
-    combine = raised / jnp.sum(raised, axis=1, keepdims=True)
-    comb_ref[...] = combine
+    slot_max = jnp.max(logits, axis=1, keepdims=True)
+    shifted = jnp.exp(logits - slot_max)
+    slot_sum = jnp.sum(shifted, axis=1, keepdims=True)
+    outs = (kept_ref, given_ref)
+    halves(product(shifted.astype(LOW), rows, 1, 0), outs, slice(0, width))
+    pieces = place(split3(slot_max) + split3(slot_sum), (slots, EXTRA), 1)
+    halves(pieces, outs, slice(width, width + EXTRA))
     loads[2].wait()
-    grad_part = product(combine.astype(LOW), cot_ref[...], 0, 0)
-    pieces = place(split3(col_max) + split3(col_sum), (EXTRA, slots), 0).T
-    for at, out in enumerate((kept_ref, given_ref)):
-        part = slice(at * half, (at + 1) * half)
-        out[:, :width] = slot_part[part].astype(LOW)
-        out[:, width : 2 * width] = grad_part[part].astype(LOW)
-        out[:, 2 * width :] = pieces[part].astype(LOW)
 
 
 def opening(at, tokens, slot_weight, cotangent):
     rows, width = cotangent.shape
     slots = slot_weight.shape[1]
-    shapes = [((slots // 2, 2 * width + EXTRA), LOW)] * 2
-    shapes += [((rows, slots), WIDE)] * 2 + [((width, slots), LOW)] + [((rows, width), LOW)] * 2
+    shapes = [((slots // 2, width + EXTRA), LOW)] * 2 + [((slots, rows), WIDE)]
+    shapes += [((slots, width), LOW)] + [((rows, width), LOW)] * 2
     return call(
         opening_kernel,
         "opening",
@@ -134,9 +137,41 @@
     )
 
 
-def merge_kernel(kept_ref, taken_ref, out_ref):
-    width = (out_ref.shape[2] - EXTRA) // 2
-    kept, taken = kept_ref[:, 2 * width :].astype(WIDE), taken_ref[:, 2 * width :].astype(WIDE)
+def grads_kernel(logit_ref, cot_ref, kept_ref, given_ref):
+    logits = logit_ref[...]
+    raised = jnp.exp(logits - jnp.max(logits, axis=0, keepdims=True))
+    combine = raised * (1.0 / jnp.sum(raised, axis=0, keepdims=True))
+    grad_part = product(combine.astype(LOW), cot_ref[...], 1, 0)
+    halves(grad_part, (kept_ref, given_ref), slice(0, grad_part.shape[1]))
+
+
+SIDE = pl.CostEstimate(flops=1_000_000_000, bytes_accessed=4_000_000, transcendentals=131_072)
+
+
+def grads_of(logits, cotangent):
+    shape = jax.ShapeDtypeStruct((logits.shape[0] // 2, cotangent.shape[1]), LOW)
+    args = (logits, cotangent)
+    return call(grads_kernel, "grads", args, [IN_VMEM] * 2, [IN_VMEM] * 2, [shape] * 2, (), SIDE)
+
+
+def combine_kernel(rows_ref, order_ref, logit_ref, comb_ref):
+    logits = product(rows_ref[...], order_ref[...], 1, 1)
+    logit_ref[...] = logits
+    raised = jnp.exp(logits - jnp.max(logits, axis=1, keepdims=True))
+    comb_ref[...] = raised * (1.0 / jnp.sum(raised, axis=1, keepdims=True))
+
+
+def combining(rows, order):
+    shape = jax.ShapeDtypeStruct((rows.shape[0], order.shape[0]), WIDE)
+    args = (rows, order)
+    return call(
+        combine_kernel, "combining", args, [IN_VMEM] * 2, [IN_VMEM] * 2, [shape] * 2, (), SIDE
+    )
+
+
+def merge_kernel(kept_ref, taken_ref, kept_grad_ref, taken_grad_ref, out_ref):
+    width = kept_grad_ref.shape[1]
+    kept, taken = kept_ref[:, width:].astype(WIDE), taken_ref[:, width:].astype(WIDE)
     kept_max, taken_max = lanes(kept, 0), lanes(taken, 0)
     top = jnp.maximum(kept_max, taken_max)
     kept_scale, taken_scale = jnp.exp(kept_max - top), jnp.exp(taken_max - top)
@@ -144,9 +179,7 @@
     slots = kept_scale * kept_ref[:, :width].astype(WIDE) + taken_scale * taken_ref[
         :, :width
     ].astype(WIDE)
-    grads = kept_ref[:, width : 2 * width].astype(WIDE) + taken_ref[
-        :, width : 2 * width
-    ].astype(WIDE)
+    grads = kept_grad_ref[...].astype(WIDE) + taken_grad_ref[...].astype(WIDE)
     pieces = place(split3(top) + split3(total), kept.shape, 1)
     peers, own = out_ref.shape[:2]
     out_ref[:, :, :width] = slots.astype(LOW).reshape(peers, own, width)
@@ -154,9 +187,11 @@
     out_ref[:, :, 2 * width :] = pieces.astype(LOW).reshape(peers, own, EXTRA)
 
 
-def merge(kept, taken, peers):
-    shape = jax.ShapeDtypeStruct((peers, kept.shape[0] // peers, kept.shape[1]), LOW)
-    return call(merge_kernel, "merge", (kept, taken), [IN_VMEM] * 2, IN_VMEM, shape)
+def merge(kept, taken, kept_grad, taken_grad, peers):
+    wide = kept.shape[1] + kept_grad.shape[1]
+    shape = jax.ShapeDtypeStruct((peers, kept.shape[0] // peers, wide), LOW)
+    args = (kept, taken, kept_grad, taken_grad)
+    return call(merge_kernel, "merge", args, [IN_VMEM] * 4, IN_VMEM, shape, (), SPAN)
 
 
 def expert_kernel(got_ref, in_ref, out_ref, told_ref):
@@ -178,18 +213,18 @@
         jnp.sum(jnp.where(odd, 0.0, scaled_sum), axis=0, keepdims=True),
         jnp.sum(jnp.where(odd, scaled_sum, 0.0), axis=0, keepdims=True),
     ]
-    scaled = scale * got[:, :width].astype(WIDE)
-    exact = [
-        jnp.sum(jnp.where(odd, 0.0, scaled), axis=0, keepdims=True) / totals[0],
-        jnp.sum(jnp.where(odd, scaled, 0.0), axis=0, keepdims=True) / totals[1],
-    ]
-    sent = got[:, width : 2 * width].astype(WIDE)
-    grads = [
-        jnp.sum(jnp.where(odd, 0.0, sent), axis=0, keepdims=True),
-        jnp.sum(jnp.where(odd, sent, 0.0), axis=0, keepdims=True),
-    ]
+    high = scale.astype(LOW).astype(WIDE)
+    rest, ones = scale - high, jnp.ones_like(scale)
+    columns = []
+    for column in (high, rest, ones):
+        columns += [jnp.where(odd, 0.0, column), jnp.where(odd, column, 0.0)]
+    picks = place(columns, (count, EXTRA), 1).T[:8].astype(LOW)
+    sums = product(picks, got[:, : 2 * width], 1, 0)
+    sums_of = lambda row, part: sums[row : row + 1, part]
+    front, back = slice(0, width), slice(width, 2 * width)
+    exact = [(sums_of(row, front) + sums_of(row + 2, front)) / totals[row] for row in range(2)]
     exact = place(exact, (8, width), 0)
-    out_grad = place(grads, (8, width), 0).astype(LOW)
+    out_grad = place([sums_of(4, back), sums_of(5, back)], (8, width), 0).astype(LOW)
     slot_low = exact.astype(LOW)
     preact = product(slot_low, w_in, 1, 0)
     hid_grad = product(out_grad, w_out, 1, 1)
@@ -240,7 +275,7 @@
             rows_ref[row : row + 1, part] = jnp.sum(
                 pieces[3 * row : 3 * row + 3], axis=0, keepdims=True
             )
-    slot_product, highest, totals = rows_ref[0:1], rows_ref[1:2], rows_ref[2:3]
+    slot_product, highest, scale = rows_ref[0:1], rows_ref[1:2], 1.0 / rows_ref[2:3]
     stores = []
     for step in range(STEPS):
         part = pl.ds(step * block, block)
@@ -255,9 +290,9 @@
         stores[-2].start()
         comb_grad = product(cot_ref[part], all_out[...], 1, 1)
         logit_grad = combine * (comb_grad - jnp.sum(combine * comb_grad, axis=1, keepdims=True))
-        dispatch = jnp.exp(logit_ref[part] - highest) / totals
+        dispatch = jnp.exp(logit_ref[part] - highest) * scale
         logit_grad += dispatch * (product(tok_ref[part], in_low[...], 1, 1) - slot_product)
-        token_grad = product(logit_grad.astype(LOW), order_ref[...], 1, 1)
+        token_grad = product(logit_grad.astype(LOW), order_ref[...], 1, 0)
         token_grad += product(dispatch.astype(LOW), in_low[...], 1, 0)
         grad_ref[part, :] = token_grad.astype(LOW)
         stores[-1].start()
@@ -267,7 +302,7 @@
 
 def closing(mine, pair, tokens, cotangent, combine, logits, weight):
     rows, width = cotangent.shape
-    slots = weight.shape[1]
+    slots = weight.shape[0]
     return call(
         closing_kernel,
         "closing",
@@ -291,8 +326,12 @@
     swap = [(0, 1), (1, 0)]
     at = jnp.stack([lax.axis_index("exp"), lax.axis_index("core")]).astype(jnp.int32)
     peers = lax.axis_size(torus)
-    kept, given, combine, logits, weight, rows, cot = opening(at, tokens, slot_weight, cotangent)
-    sent = merge(kept, lax.ppermute(given, "core", swap), peers)
+    kept, given, columns, weight, rows, cot = opening(at, tokens, slot_weight, cotangent)
+    taken = lax.ppermute(given, "core", swap)
+    kept_grad, given_grad = grads_of(columns, cot)
+    taken_grad = lax.ppermute(given_grad, "core", swap)
+    logits, combine = combining(rows, weight)
+    sent = merge(kept, taken, kept_grad, taken_grad, peers)
     got = lax.all_to_all(sent, torus, split_axis=0, concat_axis=0, tiled=True)
     told = expert(got, w_in, w_out)
     told = lax.all_to_all(told, torus, split_axis=0, concat_axis=0, tiled=True)

time: 68 us -> 64.6 us (0.950)
  local copies, waits for them, and re-layouts: 2.86 us -> 0.01 us
  waiting for transfers between devices: 3.54 us -> 2.66 us
    unnamed x4 -> x8, local copies, waits for them, and re-layouts: 2.86 us -> 0.01 us
    ppermute x1, waiting for transfers between devices: 1.77 us -> 1.07 us  [shards(): pair = lax.ppermute(told, 'core', swap)]
    ppermute x1 -> x2, waiting for transfers between devices: 1.77 us -> 1.59 us  [the longest x1 1.59 us: shards(): taken_grad = lax.ppermute(given_grad, 'core', swap)]
    ppermute x1 -> x2, starting transfers between devices: 1.5 us -> 1.62 us  [the longest x1 1.5 us: shards(): taken = lax.ppermute(given, 'core', swap)]
    pallas_call x4 -> x6, Pallas kernels: 13.7 us -> 13.7 us  [call(): pl.pallas_call(kernel, in_specs=specs, out_specs=out_specs, out_shape=out...]
  transfers between devices with their start and end apart: 2 -> 3, of which waited for: 2 -> 2; matrix products, arithmetic and copies ran while one was open for 0% -> 0% of each run, Pallas kernels for 0% -> 2%
where the time goes in v4:
time: 64.6 us; the launch traced here: 64.4 us
  blocking collectives  42.4 us (66%)
  Pallas kernels  13.7 us (21%)
  starting transfers between devices  4.78 us (7%)
  waiting for transfers between devices  2.66 us (4%)
  between operations  0.7 us (1%)
    all_to_all x1, blocking collectives, shards(): got = lax.all_to_all(sent, torus, split_axis=0, concat_axis=0, tiled=True)  25.2 us
    all_to_all x1, blocking collectives, shards(): told = lax.all_to_all(told, torus, split_axis=0, concat_axis=0, tiled=True)  17.3 us
    pallas_call x6, Pallas kernels, call(): pl.pallas_call(kernel, in_specs=specs, out_specs=out_specs, out_shape=out...  13.7 us
    ppermute x1, starting transfers between devices, shards(): pair = lax.ppermute(told, 'core', swap)  3.16 us
    ppermute x1, waiting for transfers between devices, shards(): taken_grad = lax.ppermute(given_grad, 'core', swap)  1.59 us
    ppermute x1, starting transfers between devices, shards(): taken = lax.ppermute(given, 'core', swap)  1.5 us
  transfers between devices with their start and end apart: 3, of which 2 were waited for; matrix products, arithmetic and copies ran while one was open for 0% of the time, Pallas kernels for 2%

profile of v4, /device:TPU:1, one launch (start us, length us, event | category | flops | bytes accessed | tf_op | source)
XLA Modules:
  0.0 64.4 jit_solution(14531111321473407624)
XLA Ops:
  0.6 0.1 pad_add_fusion.at_ref
  0.7 3.4 %opening.1 = (bf16[128,1408]{1,0:T(8,128)(2,1)S(1)}, bf16[128,1408]{1,0:T(8,128)(2,1)S(1)}, f32[256,512]{1,0:T(8,128)S(1)}, bf16[256,1280]{1,0:T(8,128)(2,1)S(1)...) custom-call(s32[2]{0:T(128)S(1)} %pad_add_fusion.at_ref, bf16[2048,1280]{1,0:T(8,128)(2,1)} %tok_hbm.1, ...), custom_call_target="tpu_custom_call" | custom-call | tf_op jit(solution)/shard_map/opening/pallas_call | solution.py:57
  4.1 1.5 %collective-permute-start = (bf16[128,1408]{1,0:T(8,128)(2,1)S(1)}, bf16[128,1408]{1,0:T(8,128)(2,1)S(1)}, u32[]{:S(2)}, u32[]{:S(2)}) collective-permute-start(bf16[128,1408]{1,0:T(8,128)(2,1)S(1)} %get-tuple-element.13), channel_id=1, source_target_pairs={{0,4},{4,0},{1,5},{5,1},{2,6},{6,2},{3,7},{7,3},{8,12},{12,8},{9,1... | collective-permute-start | bytes 1081352 | tf_op jit(solution)/shard_map/ppermute | solution.py:330
  5.6 0.0 slice-start
  5.6 0.0 slice-start.2
  5.6 0.6 grads.1
  6.3 0.1 collective-permute-start.1
  6.4 1.6 %collective-permute-done.1.taken_grad_ref = bf16[128,1280]{1,0:T(8,128)(2,1)S(1)} collective-permute-done((bf16[128,1280]{1,0:T(8,128)(2,1)S(1)}, bf16[128,1280]{1,0:T(8,128)(2,1)S(1)}, u32[]{:S(2)}, u32[]{:S(2)}) %collective-permute-start.1) | collective-permute-done | bytes 327712 | tf_op jit(solution)/shard_map/ppermute | solution.py:332
  8.0 0.0 collective-permute-done.taken_ref
  8.0 0.0 slice-start.1
  8.0 0.0 slice-start.3
  8.0 0.5 merge.1
  8.5 25.2 %all_to_all.10.got_ref = bf16[64,2,2688]{2,1,0:T(2,128)(2,1)S(1)} all-to-all(bf16[64,2,2688]{2,1,0:T(2,128)(2,1)S(1)} %merge.1), channel_id=1, replica_groups=mesh['x'=4,'z'=4,'core'=2,'exp'=4] {'x','z','exp'}, dimensions={0} | all-to-all | bytes 1376256 | tf_op jit(solution)/shard_map/all_to_all | solution.py:335
  33.7 0.0 slice-done
  33.7 0.0 slice-done.2
  33.7 0.0 slice-done.1
  33.7 0.0 slice-done.3
  33.7 5.6 %expert.1 = bf16[64,2,2688]{2,1,0:T(2,128)(2,1)S(1)} custom-call(bf16[64,2,2688]{2,1,0:T(2,128)(2,1)S(1)} %all_to_all.10.got_ref, bf16[1,1280,2560]{2,1,0:T(8,128)(2,1)S(1)} %bitcast.3, bf16[1,2560,1280]{2,1,0:T(8,128)(2,1)S(1)} %bitcast.5), custom_call_target="tpu_custom_call" | custom-call | tf_op jit(solution)/shard_map/expert/pallas_call | solution.py:57
  39.3 17.3 %all_to_all.11.mine_ref = bf16[64,2,2688]{2,1,0:T(2,128)(2,1)S(1)} all-to-all(bf16[64,2,2688]{2,1,0:T(2,128)(2,1)S(1)} %expert.1), channel_id=1, replica_groups=mesh['x'=4,'z'=4,'core'=2,'exp'=4] {'x','z','exp'}, dimensions={0} | all-to-all | bytes 1376256 | tf_op jit(solution)/shard_map/all_to_all | solution.py:337
  56.6 3.2 %collective-permute-start.2 = (bf16[64,2,2688]{2,1,0:T(2,128)(2,1)S(1)}, bf16[64,2,2688]{2,1,0:T(2,128)(2,1)S(1)}, u32[]{:S(2)}, u32[]{:S(2)}) collective-permute-start(bf16[64,2,2688]{2,1,0:T(2,128)(2,1)S(1)} %all_to_all.11.mine_ref), channel_id=1, source_target_pairs={{0,4},{4,0},{1,5},{5,1},{2,6},{6,2},{3,7},{7,3},{8,12},{12,8},{9,1... | collective-permute-start | bytes 2064392 | tf_op jit(solution)/shard_map/ppermute | solution.py:338
  59.7 0.7 %combining.1 = (f32[512,256]{1,0:T(8,128)S(1)}, f32[512,256]{1,0:T(8,128)S(1)}) custom-call(bf16[512,1280]{1,0:T(8,128)(2,1)S(1)} %get-tuple-element.18.rows_ref.tok_ref, bf16[256,1280]{1,0:T(8,128)(2,1)S(1)} %get-tuple-element.19.order_ref), custom_call_target="tpu_custom_call" | custom-call | flops 1000000000 | bytes 4000000 | tf_op jit(solution)/shard_map/combining/pallas_call | solution.py:57
  60.4 1.1 %collective-permute-done.2.pair_ref = bf16[64,2,2688]{2,1,0:T(2,128)(2,1)S(1)} collective-permute-done((bf16[64,2,2688]{2,1,0:T(2,128)(2,1)S(1)}, bf16[64,2,2688]{2,1,0:T(2,128)(2,1)S(1)}, u32[]{:S(2)}, u32[]{:S(2)}) %collective-permute-start.2) | collective-permute-done | bytes 688160 | tf_op jit(solution)/shard_map/ppermute | solution.py:338
  61.5 2.9 %closing.1 = (bf16[512,1280]{1,0:T(8,128)(2,1)}, bf16[512,1280]{1,0:T(8,128)(2,1)}) custom-call(bf16[64,2,2688]{2,1,0:T(2,128)(2,1)S(1)} %all_to_all.11.mine_ref, bf16[64,2,2688]{2,1,0:T(2,128)(2,1)S(1)} %collective-permute-done.2.pair_ref, bf16[512,1280]{1,0:T(8,128)(2,1)S(1)} %get-tuple-element.18.rows_ref.tok_ref, ...), custom_call_target="tpu_custom_call" | custom-call | tf_op jit(solution)/shard_map/closing/pallas_call | solution.py:57
  (2 shorter events, 0.0 us)
Async XLA Ops:
  4.1 3.8 %collective-permute-start = (bf16[128,1408]{1,0:T(8,128)(2,1)S(1)}, bf16[128,1408]{1,0:T(8,128)(2,1)S(1)}, u32[]{:S(2)}, u32[]{:S(2)}) collective-permute-start(bf16[128,1408]{1,0:T(8,128)(2,1)S(1)} %get-tuple-element.13), channel_id=1, source_target_pairs={{0,4},{4,0},{1,5},{5,1},{2,6},{6,2},{3,7},{7,3},{8,12},{12,8},{9,1... | collective-permute-start | bytes 1081352 | tf_op jit(solution)/shard_map/ppermute | solution.py:330
  5.6 28.1 %slice-start = ((s8[6553600]{0:T(1024)(128)(4,1)}), s8[4194304]{0:T(1024)(128)(4,1)S(1)}, s32[]{:S(2)}) async-start(s8[6553600]{0:T(1024)(128)(4,1)} %bitcast.2), calls=%async_computation.2 | async-start | bytes 8388608
  5.6 28.1 %slice-start.2 = ((s8[6553600]{0:T(1024)(128)(4,1)}), s8[2359296]{0:T(1024)(128)(4,1)S(1)}, s32[]{:S(2)}) async-start(s8[6553600]{0:T(1024)(128)(4,1)} %bitcast.4), calls=%async_computation.4 | async-start | bytes 4718592
  6.3 1.7 %collective-permute-start.1 = (bf16[128,1280]{1,0:T(8,128)(2,1)S(1)}, bf16[128,1280]{1,0:T(8,128)(2,1)S(1)}, u32[]{:S(2)}, u32[]{:S(2)}) collective-permute-start(bf16[128,1280]{1,0:T(8,128)(2,1)S(1)} %get-tuple-element.17), channel_id=1, source_target_pairs={{0,4},{4,0},{1,5},{5,1},{2,6},{6,2},{3,7},{7,3},{8,12},{12,8},{9,1... | collective-permute-start | bytes 983048 | tf_op jit(solution)/shard_map/ppermute | solution.py:332
  8.0 25.7 %slice-start.1 = ((s8[6553600]{0:T(1024)(128)(4,1)}), s8[2359296]{0:T(1024)(128)(4,1)S(1)}, s32[]{:S(2)}) async-start(s8[6553600]{0:T(1024)(128)(4,1)} %bitcast.2), calls=%async_computation.3 | async-start | bytes 4718592
  8.0 25.7 %slice-start.3 = ((s8[6553600]{0:T(1024)(128)(4,1)}), s8[4194304]{0:T(1024)(128)(4,1)S(1)}, s32[]{:S(2)}) async-start(s8[6553600]{0:T(1024)(128)(4,1)} %bitcast.4), calls=%async_computation.5 | async-start | bytes 8388608
  56.6 4.9 %collective-permute-start.2 = (bf16[64,2,2688]{2,1,0:T(2,128)(2,1)S(1)}, bf16[64,2,2688]{2,1,0:T(2,128)(2,1)S(1)}, u32[]{:S(2)}, u32[]{:S(2)}) collective-permute-start(bf16[64,2,2688]{2,1,0:T(2,128)(2,1)S(1)} %all_to_all.11.mine_ref), channel_id=1, source_target_pairs={{0,4},{4,0},{1,5},{5,1},{2,6},{6,2},{3,7},{7,3},{8,12},{12,8},{9,1... | collective-permute-start | bytes 2064392 | tf_op jit(solution)/shard_map/ppermute | solution.py:338

commit v5 on v4

--- a/solution.py
+++ b/solution.py
@@ -194,10 +194,23 @@
     return call(merge_kernel, "merge", args, [IN_VMEM] * 4, IN_VMEM, shape, (), SPAN)
 
 
+PART = 256
+FEW = 32
+
+
+def two_rows(left, right_ref, first):
+    columns = [[], []]
+    for at in range(first, first + PART, FEW):
+        right = right_ref[0, at : at + FEW, :].astype(WIDE)
+        for row in range(2):
+            columns[row].append(jnp.sum(left[row] * right, axis=1, keepdims=True))
+    columns = [jnp.concatenate(column, axis=0) for column in columns]
+    return place(columns, (PART, EXTRA), 1).T[:8]
+
+
 def expert_kernel(got_ref, in_ref, out_ref, told_ref):
-    w_in, w_out = in_ref[0], out_ref[0]
     peers, own, wide = got_ref.shape
-    count, width = peers * own, w_in.shape[0]
+    count, width = peers * own, in_ref.shape[1]
     got = got_ref[...].reshape(count, wide)
     pieces = got[:, 2 * width :].astype(WIDE)
     block_max, block_sum = lanes(pieces, 0), lanes(pieces, 3)
@@ -224,20 +237,23 @@
     front, back = slice(0, width), slice(width, 2 * width)
     exact = [(sums_of(row, front) + sums_of(row + 2, front)) / totals[row] for row in range(2)]
     exact = place(exact, (8, width), 0)
-    out_grad = place([sums_of(4, back), sums_of(5, back)], (8, width), 0).astype(LOW)
+    out_grad = [sums_of(4, back).astype(LOW).astype(WIDE), sums_of(5, back).astype(LOW).astype(WIDE)]
     slot_low = exact.astype(LOW)
-    preact = product(slot_low, w_in, 1, 0)
-    hid_grad = product(out_grad, w_out, 1, 1)
     rate = 0.7978845608028654
-    square = preact * preact
-    curve = jnp.tanh(rate * (preact + 0.044715 * square * preact))
-    low_hidden = (0.5 * preact * (1.0 + curve)).astype(LOW)
-    slope = 0.5 * (1.0 + curve) + 0.5 * preact * (1.0 - curve * curve) * rate * (
-        1.0 + 3.0 * 0.044715 * square
-    )
-    pre_grad = (slope * hid_grad).astype(LOW)
-    slot_out = product(low_hidden, w_out, 1, 0)
-    in_grad = product(pre_grad, w_in, 1, 1)
+    slot_out = jnp.zeros((8, width), WIDE)
+    in_grad = jnp.zeros((8, width), WIDE)
+    for first in range(0, in_ref.shape[2], PART):
+        part = slice(first, first + PART)
+        preact = product(slot_low, in_ref[0, :, part], 1, 0)
+        hid_grad = two_rows(out_grad, out_ref, first)
+        square = preact * preact
+        curve = jnp.tanh(rate * (preact + 0.044715 * square * preact))
+        low_hidden = (0.5 * preact * (1.0 + curve)).astype(LOW)
+        slope = 0.5 * (1.0 + curve) + 0.5 * preact * (1.0 - curve * curve) * rate * (
+            1.0 + 3.0 * 0.044715 * square
+        )
+        slot_out += product(low_hidden, out_ref[0, part, :], 1, 0)
+        in_grad += product((slope * hid_grad).astype(LOW), in_ref[0, :, part], 1, 1)
     slot_product = jnp.sum(exact * in_grad, axis=1, keepdims=True)
     top = place(top, (8, 1), 0)
     totals = place(totals, (8, 1), 0)

time: 64.6 us -> 65 us (level)
  no operation moved by 1% of the time
where the time goes in v5:
time: 65 us; the launch traced here: 64.8 us
  blocking collectives  42.4 us (65%)
  Pallas kernels  14 us (22%)
  starting transfers between devices  4.78 us (7%)
  waiting for transfers between devices  2.65 us (4%)
  between operations  0.86 us (1%)
    all_to_all x1, blocking collectives, shards(): got = lax.all_to_all(sent, torus, split_axis=0, concat_axis=0, tiled=True)  25.2 us
    all_to_all x1, blocking collectives, shards(): told = lax.all_to_all(told, torus, split_axis=0, concat_axis=0, tiled=True)  17.3 us
    pallas_call x6, Pallas kernels, call(): pl.pallas_call(kernel, in_specs=specs, out_specs=out_specs, out_shape=out...  14 us
    ppermute x1, starting transfers between devices, shards(): pair = lax.ppermute(told, 'core', swap)  3.16 us
    ppermute x1, waiting for transfers between devices, shards(): taken_grad = lax.ppermute(given_grad, 'core', swap)  1.59 us
    ppermute x1, starting transfers between devices, shards(): taken = lax.ppermute(given, 'core', swap)  1.5 us
  transfers between devices with their start and end apart: 3, of which 2 were waited for; matrix products, arithmetic and copies ran while one was open for 0% of the time, Pallas kernels for 2%

profile of v5, /device:TPU:1, one launch (start us, length us, event | category | flops | bytes accessed | tf_op | source)
XLA Modules:
  0.0 64.8 jit_solution(2152438437984047492)
XLA Ops:
  0.6 0.1 pad_add_fusion.at_ref
  0.7 3.4 %opening.1 = (bf16[128,1408]{1,0:T(8,128)(2,1)S(1)}, bf16[128,1408]{1,0:T(8,128)(2,1)S(1)}, f32[256,512]{1,0:T(8,128)S(1)}, bf16[256,1280]{1,0:T(8,128)(2,1)S(1)...) custom-call(s32[2]{0:T(128)S(1)} %pad_add_fusion.at_ref, bf16[2048,1280]{1,0:T(8,128)(2,1)} %tok_hbm.1, ...), custom_call_target="tpu_custom_call" | custom-call | tf_op jit(solution)/shard_map/opening/pallas_call | solution.py:57
  4.1 1.5 %collective-permute-start = (bf16[128,1408]{1,0:T(8,128)(2,1)S(1)}, bf16[128,1408]{1,0:T(8,128)(2,1)S(1)}, u32[]{:S(2)}, u32[]{:S(2)}) collective-permute-start(bf16[128,1408]{1,0:T(8,128)(2,1)S(1)} %get-tuple-element.13), channel_id=1, source_target_pairs={{0,4},{4,0},{1,5},{5,1},{2,6},{6,2},{3,7},{7,3},{8,12},{12,8},{9,1... | collective-permute-start | bytes 1081352 | tf_op jit(solution)/shard_map/ppermute | solution.py:346
  5.6 0.0 slice-start
  5.6 0.0 slice-start.2
  5.6 0.6 grads.1
  6.3 0.1 collective-permute-start.1
  6.4 1.6 %collective-permute-done.1.taken_grad_ref = bf16[128,1280]{1,0:T(8,128)(2,1)S(1)} collective-permute-done((bf16[128,1280]{1,0:T(8,128)(2,1)S(1)}, bf16[128,1280]{1,0:T(8,128)(2,1)S(1)}, u32[]{:S(2)}, u32[]{:S(2)}) %collective-permute-start.1) | collective-permute-done | bytes 327712 | tf_op jit(solution)/shard_map/ppermute | solution.py:348
  8.0 0.0 collective-permute-done.taken_ref
  8.0 0.0 slice-start.1
  8.0 0.0 slice-start.3
  8.0 0.5 merge.1
  8.5 25.2 %all_to_all.10.got_ref = bf16[64,2,2688]{2,1,0:T(2,128)(2,1)S(1)} all-to-all(bf16[64,2,2688]{2,1,0:T(2,128)(2,1)S(1)} %merge.1), channel_id=1, replica_groups=mesh['x'=4,'z'=4,'core'=2,'exp'=4] {'x','z','exp'}, dimensions={0} | all-to-all | bytes 1376256 | tf_op jit(solution)/shard_map/all_to_all | solution.py:351
  33.7 0.0 slice-done
  33.7 0.0 slice-done.2
  33.7 0.0 slice-done.1
  33.7 0.0 slice-done.3
  33.7 5.9 %expert.1 = bf16[64,2,2688]{2,1,0:T(2,128)(2,1)S(1)} custom-call(bf16[64,2,2688]{2,1,0:T(2,128)(2,1)S(1)} %all_to_all.10.got_ref, bf16[1,1280,2560]{2,1,0:T(8,128)(2,1)S(1)} %bitcast.3, bf16[1,2560,1280]{2,1,0:T(8,128)(2,1)S(1)} %bitcast.5), custom_call_target="tpu_custom_call" | custom-call | tf_op jit(solution)/shard_map/expert/pallas_call | solution.py:57
  39.6 17.3 %all_to_all.11.mine_ref = bf16[64,2,2688]{2,1,0:T(2,128)(2,1)S(1)} all-to-all(bf16[64,2,2688]{2,1,0:T(2,128)(2,1)S(1)} %expert.1), channel_id=1, replica_groups=mesh['x'=4,'z'=4,'core'=2,'exp'=4] {'x','z','exp'}, dimensions={0} | all-to-all | bytes 1376256 | tf_op jit(solution)/shard_map/all_to_all | solution.py:353
  56.8 3.2 %collective-permute-start.2 = (bf16[64,2,2688]{2,1,0:T(2,128)(2,1)S(1)}, bf16[64,2,2688]{2,1,0:T(2,128)(2,1)S(1)}, u32[]{:S(2)}, u32[]{:S(2)}) collective-permute-start(bf16[64,2,2688]{2,1,0:T(2,128)(2,1)S(1)} %all_to_all.11.mine_ref), channel_id=1, source_target_pairs={{0,4},{4,0},{1,5},{5,1},{2,6},{6,2},{3,7},{7,3},{8,12},{12,8},{9,1... | collective-permute-start | bytes 2064392 | tf_op jit(solution)/shard_map/ppermute | solution.py:354
  60.0 0.7 %combining.1 = (f32[512,256]{1,0:T(8,128)S(1)}, f32[512,256]{1,0:T(8,128)S(1)}) custom-call(bf16[512,1280]{1,0:T(8,128)(2,1)S(1)} %get-tuple-element.18.rows_ref.tok_ref, bf16[256,1280]{1,0:T(8,128)(2,1)S(1)} %get-tuple-element.19.order_ref), custom_call_target="tpu_custom_call" | custom-call | flops 1000000000 | bytes 4000000 | tf_op jit(solution)/shard_map/combining/pallas_call | solution.py:57
  60.7 1.1 %collective-permute-done.2.pair_ref = bf16[64,2,2688]{2,1,0:T(2,128)(2,1)S(1)} collective-permute-done((bf16[64,2,2688]{2,1,0:T(2,128)(2,1)S(1)}, bf16[64,2,2688]{2,1,0:T(2,128)(2,1)S(1)}, u32[]{:S(2)}, u32[]{:S(2)}) %collective-permute-start.2) | collective-permute-done | bytes 688160 | tf_op jit(solution)/shard_map/ppermute | solution.py:354
  61.8 2.9 %closing.1 = (bf16[512,1280]{1,0:T(8,128)(2,1)}, bf16[512,1280]{1,0:T(8,128)(2,1)}) custom-call(bf16[64,2,2688]{2,1,0:T(2,128)(2,1)S(1)} %all_to_all.11.mine_ref, bf16[64,2,2688]{2,1,0:T(2,128)(2,1)S(1)} %collective-permute-done.2.pair_ref, bf16[512,1280]{1,0:T(8,128)(2,1)S(1)} %get-tuple-element.18.rows_ref.tok_ref, ...), custom_call_target="tpu_custom_call" | custom-call | tf_op jit(solution)/shard_map/closing/pallas_call | solution.py:57
  (2 shorter events, 0.0 us)
Async XLA Ops:
  4.1 3.8 %collective-permute-start = (bf16[128,1408]{1,0:T(8,128)(2,1)S(1)}, bf16[128,1408]{1,0:T(8,128)(2,1)S(1)}, u32[]{:S(2)}, u32[]{:S(2)}) collective-permute-start(bf16[128,1408]{1,0:T(8,128)(2,1)S(1)} %get-tuple-element.13), channel_id=1, source_target_pairs={{0,4},{4,0},{1,5},{5,1},{2,6},{6,2},{3,7},{7,3},{8,12},{12,8},{9,1... | collective-permute-start | bytes 1081352 | tf_op jit(solution)/shard_map/ppermute | solution.py:346
  5.6 28.1 %slice-start = ((s8[6553600]{0:T(1024)(128)(4,1)}), s8[4194304]{0:T(1024)(128)(4,1)S(1)}, s32[]{:S(2)}) async-start(s8[6553600]{0:T(1024)(128)(4,1)} %bitcast.2), calls=%async_computation.2 | async-start | bytes 8388608
  5.6 28.1 %slice-start.2 = ((s8[6553600]{0:T(1024)(128)(4,1)}), s8[2359296]{0:T(1024)(128)(4,1)S(1)}, s32[]{:S(2)}) async-start(s8[6553600]{0:T(1024)(128)(4,1)} %bitcast.4), calls=%async_computation.4 | async-start | bytes 4718592
  6.3 1.7 %collective-permute-start.1 = (bf16[128,1280]{1,0:T(8,128)(2,1)S(1)}, bf16[128,1280]{1,0:T(8,128)(2,1)S(1)}, u32[]{:S(2)}, u32[]{:S(2)}) collective-permute-start(bf16[128,1280]{1,0:T(8,128)(2,1)S(1)} %get-tuple-element.17), channel_id=1, source_target_pairs={{0,4},{4,0},{1,5},{5,1},{2,6},{6,2},{3,7},{7,3},{8,12},{12,8},{9,1... | collective-permute-start | bytes 983048 | tf_op jit(solution)/shard_map/ppermute | solution.py:348
  8.0 25.7 %slice-start.1 = ((s8[6553600]{0:T(1024)(128)(4,1)}), s8[2359296]{0:T(1024)(128)(4,1)S(1)}, s32[]{:S(2)}) async-start(s8[6553600]{0:T(1024)(128)(4,1)} %bitcast.2), calls=%async_computation.3 | async-start | bytes 4718592
  8.0 25.7 %slice-start.3 = ((s8[6553600]{0:T(1024)(128)(4,1)}), s8[4194304]{0:T(1024)(128)(4,1)S(1)}, s32[]{:S(2)}) async-start(s8[6553600]{0:T(1024)(128)(4,1)} %bitcast.4), calls=%async_computation.5 | async-start | bytes 8388608
  56.8 4.9 %collective-permute-start.2 = (bf16[64,2,2688]{2,1,0:T(2,128)(2,1)S(1)}, bf16[64,2,2688]{2,1,0:T(2,128)(2,1)S(1)}, u32[]{:S(2)}, u32[]{:S(2)}) collective-permute-start(bf16[64,2,2688]{2,1,0:T(2,128)(2,1)S(1)} %all_to_all.11.mine_ref), channel_id=1, source_target_pairs={{0,4},{4,0},{1,5},{5,1},{2,6},{6,2},{3,7},{7,3},{8,12},{12,8},{9,1... | collective-permute-start | bytes 2064392 | tf_op jit(solution)/shard_map/ppermute | solution.py:354

commit v6 on v4

--- a/solution.py
+++ b/solution.py
@@ -90,26 +90,26 @@
     slots = weight_ref.shape[1]
     count, width = rows_ref.shape
     start = pl.multiple_of(at_ref[0] * count, count)
-    loads = [
-        pltpu.make_async_copy(source, target, sems.at[at])
-        for at, (source, target) in enumerate(
-            (
-                (weight_hbm, weight_ref),
-                (tok_hbm.at[pl.ds(start, count)], rows_ref),
-                (cot_hbm, cot_ref),
-            )
-        )
-    ]
-    loads[0].start()
-    loads[1].start()
+    block = width // 2
+    parts = [pl.ds(at * block, block) for at in range(2)]
+    loads = []
+    for part in parts:
+        source = tok_hbm.at[pl.ds(start, count), part]
+        loads.append(pltpu.make_async_copy(weight_hbm.at[part], weight_ref.at[part], sems.at[len(loads)]))
+        loads.append(pltpu.make_async_copy(source, rows_ref.at[:, part], sems.at[len(loads)]))
+    loads.append(pltpu.make_async_copy(cot_hbm, cot_ref, sems.at[4]))
+    for copy in loads[:4]:
+        copy.start()
     order = ordering(at_ref[1], slots)
-    loads[0].wait()
-    weight = product(order, weight_ref[...], 1, 1).astype(LOW)
-    order_ref[...] = weight
-    loads[1].wait()
-    loads[2].start()
+    logits = 0.0
+    for at, part in enumerate(parts):
+        loads[2 * at].wait()
+        weight = product(order, weight_ref[part, :], 1, 1).astype(LOW)
+        order_ref[:, part] = weight
+        loads[2 * at + 1].wait()
+        logits += product(weight, rows_ref[:, part], 1, 1)
+    loads[4].start()
     rows = rows_ref[...]
-    logits = product(weight, rows, 1, 1)
     logit_ref[...] = logits
     slot_max = jnp.max(logits, axis=1, keepdims=True)
     shifted = jnp.exp(logits - slot_max)
@@ -118,7 +118,7 @@
     halves(product(shifted.astype(LOW), rows, 1, 0), outs, slice(0, width))
     pieces = place(split3(slot_max) + split3(slot_sum), (slots, EXTRA), 1)
     halves(pieces, outs, slice(width, width + EXTRA))
-    loads[2].wait()
+    loads[4].wait()
 
 
 def opening(at, tokens, slot_weight, cotangent):
@@ -133,7 +133,7 @@
         [IN_SMEM] + [IN_HBM] * 3,
         [IN_VMEM] * len(shapes),
         [jax.ShapeDtypeStruct(*shape) for shape in shapes],
-        [pltpu.VMEM((width, slots), LOW), pltpu.SemaphoreType.DMA((3,))],
+        [pltpu.VMEM((width, slots), LOW), pltpu.SemaphoreType.DMA((5,))],
     )
 
 
@@ -198,8 +198,15 @@
     w_in, w_out = in_ref[0], out_ref[0]
     peers, own, wide = got_ref.shape
     count, width = peers * own, w_in.shape[0]
-    got = got_ref[...].reshape(count, wide)
-    pieces = got[:, 2 * width :].astype(WIDE)
+    spread = lambda block: jnp.broadcast_to(
+        block[:own].astype(LOW)[None], (peers, own, block.shape[1])
+    )
+    index = lambda axis: lax.broadcasted_iota(jnp.int32, (8, count), axis)
+    picks = (index(1) % 2 == index(0)).astype(WIDE).astype(LOW)
+    grads = got_ref[:, :, width : 2 * width].reshape(count, width)
+    out_grad = product(picks, grads, 1, 0).astype(LOW)
+    hid_grad = product(out_grad, w_out, 1, 1)
+    pieces = got_ref[:, :, 2 * width :].reshape(count, EXTRA).astype(WIDE)
     block_max, block_sum = lanes(pieces, 0), lanes(pieces, 3)
     odd = lax.broadcasted_iota(jnp.int32, (count, 1), 0) % 2 == 1
     lowest = jnp.full((count, 1), -jnp.inf, WIDE)
@@ -214,20 +221,14 @@
         jnp.sum(jnp.where(odd, scaled_sum, 0.0), axis=0, keepdims=True),
     ]
     high = scale.astype(LOW).astype(WIDE)
-    rest, ones = scale - high, jnp.ones_like(scale)
     columns = []
-    for column in (high, rest, ones):
+    for column in (high, scale - high):
         columns += [jnp.where(odd, 0.0, column), jnp.where(odd, column, 0.0)]
     picks = place(columns, (count, EXTRA), 1).T[:8].astype(LOW)
-    sums = product(picks, got[:, : 2 * width], 1, 0)
-    sums_of = lambda row, part: sums[row : row + 1, part]
-    front, back = slice(0, width), slice(width, 2 * width)
-    exact = [(sums_of(row, front) + sums_of(row + 2, front)) / totals[row] for row in range(2)]
+    sums = product(picks, got_ref[:, :, :width].reshape(count, width), 1, 0)
+    exact = [(sums[row : row + 1] + sums[row + 2 : row + 3]) / totals[row] for row in range(2)]
     exact = place(exact, (8, width), 0)
-    out_grad = place([sums_of(4, back), sums_of(5, back)], (8, width), 0).astype(LOW)
-    slot_low = exact.astype(LOW)
-    preact = product(slot_low, w_in, 1, 0)
-    hid_grad = product(out_grad, w_out, 1, 1)
+    preact = product(exact.astype(LOW), w_in, 1, 0)
     rate = 0.7978845608028654
     square = preact * preact
     curve = jnp.tanh(rate * (preact + 0.044715 * square * preact))
@@ -235,18 +236,13 @@
     slope = 0.5 * (1.0 + curve) + 0.5 * preact * (1.0 - curve * curve) * rate * (
         1.0 + 3.0 * 0.044715 * square
     )
-    pre_grad = (slope * hid_grad).astype(LOW)
-    slot_out = product(low_hidden, w_out, 1, 0)
-    in_grad = product(pre_grad, w_in, 1, 1)
+    told_ref[:, :, :width] = spread(product(low_hidden, w_out, 1, 0))
+    in_grad = product((slope * hid_grad).astype(LOW), w_in, 1, 1)
+    told_ref[:, :, width : 2 * width] = spread(in_grad)
     slot_product = jnp.sum(exact * in_grad, axis=1, keepdims=True)
     top = place(top, (8, 1), 0)
     totals = place(totals, (8, 1), 0)
     scalars = place(split3(slot_product) + split3(top) + split3(totals), (8, EXTRA), 1)
-    spread = lambda block: jnp.broadcast_to(
-        block[:own].astype(LOW)[None], (peers, own, block.shape[1])
-    )
-    told_ref[:, :, :width] = spread(slot_out)
-    told_ref[:, :, width : 2 * width] = spread(in_grad)
     told_ref[:, :, 2 * width :] = spread(scalars)
 
 
@@ -261,41 +257,51 @@
 def closing_kernel(
     mine_ref, pair_ref, tok_ref, cot_ref, comb_ref, logit_ref, order_ref,
     mixed_hbm, grad_hbm,
-    all_out, in_low, rows_ref, mixed_ref, grad_ref, out_sems,
+    all_out, in_low, rows_ref, mixed_ref, grad_ref, sems,
 ):
     count, width = cot_ref.shape
     half = mine_ref.shape[0] * mine_ref.shape[1]
     block = count // STEPS
-    for at, ref in enumerate((mine_ref, pair_ref)):
-        part = slice(at * half, (at + 1) * half)
-        all_out[part, :] = ref[:, :, :width].reshape(half, width)
-        in_low[part, :] = ref[:, :, width : 2 * width].reshape(half, width)
+    parts = [pl.ds(step * block, block) for step in range(STEPS)]
+    sides = [(slice(0, half), mine_ref), (slice(half, 2 * half), pair_ref)]
+    stores = []
+
+    def store(source, target, where):
+        at = len(stores)
+        stores.append(pltpu.make_async_copy(source.at[where], target.at[where], sems.at[at]))
+        stores[at].start()
+
+    for side, ref in sides:
+        all_out[side, :] = ref[:, :, :width].reshape(half, width)
+    combs = []
+    for part in parts:
+        combine = comb_ref[part]
+        mixed_ref[part, :] = product(combine.astype(LOW), all_out[...], 1, 0).astype(LOW)
+        store(mixed_ref, mixed_hbm, part)
+        comb_grad = product(cot_ref[part], all_out[...], 1, 1)
+        mean = jnp.sum(combine * comb_grad, axis=1, keepdims=True)
+        combs.append(combine * (comb_grad - mean))
+    for side, ref in sides:
+        in_low[side, :] = ref[:, :, width : 2 * width].reshape(half, width)
         pieces = ref[:, :, 2 * width :].reshape(half, EXTRA).astype(WIDE).T
         for row in range(3):
-            rows_ref[row : row + 1, part] = jnp.sum(
+            rows_ref[row : row + 1, side] = jnp.sum(
                 pieces[3 * row : 3 * row + 3], axis=0, keepdims=True
             )
     slot_product, highest, scale = rows_ref[0:1], rows_ref[1:2], 1.0 / rows_ref[2:3]
-    stores = []
-    for step in range(STEPS):
-        part = pl.ds(step * block, block)
-        stores.append(
-            pltpu.make_async_copy(mixed_ref.at[part], mixed_hbm.at[part], out_sems.at[0, step])
+    for step, part in enumerate(parts):
+        dispatch = jnp.exp(logit_ref[part] - highest) * scale
+        logit_grad = combs[step] + dispatch * (
+            product(tok_ref[part], in_low[...], 1, 1) - slot_product
         )
-        stores.append(
-            pltpu.make_async_copy(grad_ref.at[part], grad_hbm.at[part], out_sems.at[1, step])
-        )
-        combine = comb_ref[part]
-        mixed_ref[part, :] = product(combine.astype(LOW), all_out[...], 1, 0).astype(LOW)
-        stores[-2].start()
-        comb_grad = product(cot_ref[part], all_out[...], 1, 1)
-        logit_grad = combine * (comb_grad - jnp.sum(combine * comb_grad, axis=1, keepdims=True))
-        dispatch = jnp.exp(logit_ref[part] - highest) * scale
-        logit_grad += dispatch * (product(tok_ref[part], in_low[...], 1, 1) - slot_product)
-        token_grad = product(logit_grad.astype(LOW), order_ref[...], 1, 0)
-        token_grad += product(dispatch.astype(LOW), in_low[...], 1, 0)
-        grad_ref[part, :] = token_grad.astype(LOW)
-        stores[-1].start()
+        logit_grad, dispatch = logit_grad.astype(LOW), dispatch.astype(LOW)
+        cuts = [0, width] if step + 1 < STEPS else [0, width - 256, width]
+        for first, last in zip(cuts, cuts[1:]):
+            columns = slice(first, last)
+            token_grad = product(logit_grad, order_ref[:, columns], 1, 0)
+            token_grad += product(dispatch, in_low[:, columns], 1, 0)
+            grad_ref[part, columns] = token_grad.astype(LOW)
+            store(grad_ref, grad_hbm, (part, pl.ds(first, last - first)))
     for copy in stores:
         copy.wait()
 
@@ -316,7 +322,7 @@
             pltpu.VMEM((8, slots), WIDE),
             pltpu.VMEM((rows, width), LOW),
             pltpu.VMEM((rows, width), LOW),
-            pltpu.SemaphoreType.DMA((2, STEPS)),
+            pltpu.SemaphoreType.DMA((2 * STEPS + 1,)),
         ],
     )
 

time: 64.6 us -> 65.1 us (level)
  no operation moved by 1% of the time
where the time goes in v6:
time: 65.1 us; the launch traced here: 64.9 us
  blocking collectives  42.4 us (65%)
  Pallas kernels  14.2 us (22%)
  starting transfers between devices  4.78 us (7%)
  waiting for transfers between devices  2.66 us (4%)
  between operations  0.7 us (1%)
    all_to_all x1, blocking collectives, shards(): got = lax.all_to_all(sent, torus, split_axis=0, concat_axis=0, tiled=True)  25.2 us
    all_to_all x1, blocking collectives, shards(): told = lax.all_to_all(told, torus, split_axis=0, concat_axis=0, tiled=True)  17.3 us
    pallas_call x6, Pallas kernels, call(): pl.pallas_call(kernel, in_specs=specs, out_specs=out_specs, out_shape=out...  14.2 us
    ppermute x1, starting transfers between devices, shards(): pair = lax.ppermute(told, 'core', swap)  3.16 us
    ppermute x1, waiting for transfers between devices, shards(): taken_grad = lax.ppermute(given_grad, 'core', swap)  1.59 us
    ppermute x1, starting transfers between devices, shards(): taken = lax.ppermute(given, 'core', swap)  1.5 us
  transfers between devices with their start and end apart: 3, of which 2 were waited for; matrix products, arithmetic and copies ran while one was open for 0% of the time, Pallas kernels for 2%

profile of v6, /device:TPU:1, one launch (start us, length us, event | category | flops | bytes accessed | tf_op | source)
XLA Modules:
  0.0 64.9 jit_solution(12008891557179574723)
XLA Ops:
  0.6 0.1 pad_add_fusion.at_ref
  0.7 3.6 %opening.1 = (bf16[128,1408]{1,0:T(8,128)(2,1)S(1)}, bf16[128,1408]{1,0:T(8,128)(2,1)S(1)}, f32[256,512]{1,0:T(8,128)S(1)}, bf16[256,1280]{1,0:T(8,128)(2,1)S(1)...) custom-call(s32[2]{0:T(128)S(1)} %pad_add_fusion.at_ref, bf16[2048,1280]{1,0:T(8,128)(2,1)} %tok_hbm.1, ...), custom_call_target="tpu_custom_call" | custom-call | tf_op jit(solution)/shard_map/opening/pallas_call | solution.py:57
  4.3 1.5 %collective-permute-start = (bf16[128,1408]{1,0:T(8,128)(2,1)S(1)}, bf16[128,1408]{1,0:T(8,128)(2,1)S(1)}, u32[]{:S(2)}, u32[]{:S(2)}) collective-permute-start(bf16[128,1408]{1,0:T(8,128)(2,1)S(1)} %get-tuple-element.13), channel_id=1, source_target_pairs={{0,4},{4,0},{1,5},{5,1},{2,6},{6,2},{3,7},{7,3},{8,12},{12,8},{9,1... | collective-permute-start | bytes 1081352 | tf_op jit(solution)/shard_map/ppermute | solution.py:336
  5.8 0.0 slice-start
  5.8 0.0 slice-start.2
  5.8 0.6 grads.1
  6.4 0.1 collective-permute-start.1
  6.6 1.6 %collective-permute-done.1.taken_grad_ref = bf16[128,1280]{1,0:T(8,128)(2,1)S(1)} collective-permute-done((bf16[128,1280]{1,0:T(8,128)(2,1)S(1)}, bf16[128,1280]{1,0:T(8,128)(2,1)S(1)}, u32[]{:S(2)}, u32[]{:S(2)}) %collective-permute-start.1) | collective-permute-done | bytes 327712 | tf_op jit(solution)/shard_map/ppermute | solution.py:338
  8.1 0.0 collective-permute-done.taken_ref
  8.2 0.0 slice-start.1
  8.2 0.0 slice-start.3
  8.2 0.5 merge.1
  8.7 25.2 %all_to_all.10.got_ref = bf16[64,2,2688]{2,1,0:T(2,128)(2,1)S(1)} all-to-all(bf16[64,2,2688]{2,1,0:T(2,128)(2,1)S(1)} %merge.1), channel_id=1, replica_groups=mesh['x'=4,'z'=4,'core'=2,'exp'=4] {'x','z','exp'}, dimensions={0} | all-to-all | bytes 1376256 | tf_op jit(solution)/shard_map/all_to_all | solution.py:341
  33.9 0.0 slice-done
  33.9 0.0 slice-done.2
  33.9 0.0 slice-done.1
  33.9 0.0 slice-done.3
  33.9 5.7 %expert.1 = bf16[64,2,2688]{2,1,0:T(2,128)(2,1)S(1)} custom-call(bf16[64,2,2688]{2,1,0:T(2,128)(2,1)S(1)} %all_to_all.10.got_ref, bf16[1,1280,2560]{2,1,0:T(8,128)(2,1)S(1)} %bitcast.3, bf16[1,2560,1280]{2,1,0:T(8,128)(2,1)S(1)} %bitcast.5), custom_call_target="tpu_custom_call" | custom-call | tf_op jit(solution)/shard_map/expert/pallas_call | solution.py:57
  39.7 17.3 %all_to_all.11.mine_ref = bf16[64,2,2688]{2,1,0:T(2,128)(2,1)S(1)} all-to-all(bf16[64,2,2688]{2,1,0:T(2,128)(2,1)S(1)} %expert.1), channel_id=1, replica_groups=mesh['x'=4,'z'=4,'core'=2,'exp'=4] {'x','z','exp'}, dimensions={0} | all-to-all | bytes 1376256 | tf_op jit(solution)/shard_map/all_to_all | solution.py:343
  56.9 3.2 %collective-permute-start.2 = (bf16[64,2,2688]{2,1,0:T(2,128)(2,1)S(1)}, bf16[64,2,2688]{2,1,0:T(2,128)(2,1)S(1)}, u32[]{:S(2)}, u32[]{:S(2)}) collective-permute-start(bf16[64,2,2688]{2,1,0:T(2,128)(2,1)S(1)} %all_to_all.11.mine_ref), channel_id=1, source_target_pairs={{0,4},{4,0},{1,5},{5,1},{2,6},{6,2},{3,7},{7,3},{8,12},{12,8},{9,1... | collective-permute-start | bytes 2064392 | tf_op jit(solution)/shard_map/ppermute | solution.py:344
  60.1 0.7 %combining.1 = (f32[512,256]{1,0:T(8,128)S(1)}, f32[512,256]{1,0:T(8,128)S(1)}) custom-call(bf16[512,1280]{1,0:T(8,128)(2,1)S(1)} %get-tuple-element.18.rows_ref.tok_ref, bf16[256,1280]{1,0:T(8,128)(2,1)S(1)} %get-tuple-element.19.order_ref), custom_call_target="tpu_custom_call" | custom-call | flops 1000000000 | bytes 4000000 | tf_op jit(solution)/shard_map/combining/pallas_call | solution.py:57
  60.8 1.1 %collective-permute-done.2.pair_ref = bf16[64,2,2688]{2,1,0:T(2,128)(2,1)S(1)} collective-permute-done((bf16[64,2,2688]{2,1,0:T(2,128)(2,1)S(1)}, bf16[64,2,2688]{2,1,0:T(2,128)(2,1)S(1)}, u32[]{:S(2)}, u32[]{:S(2)}) %collective-permute-start.2) | collective-permute-done | bytes 688160 | tf_op jit(solution)/shard_map/ppermute | solution.py:344
  61.8 3.0 %closing.1 = (bf16[512,1280]{1,0:T(8,128)(2,1)}, bf16[512,1280]{1,0:T(8,128)(2,1)}) custom-call(bf16[64,2,2688]{2,1,0:T(2,128)(2,1)S(1)} %all_to_all.11.mine_ref, bf16[64,2,2688]{2,1,0:T(2,128)(2,1)S(1)} %collective-permute-done.2.pair_ref, bf16[512,1280]{1,0:T(8,128)(2,1)S(1)} %get-tuple-element.18.rows_ref.tok_ref, ...), custom_call_target="tpu_custom_call" | custom-call | tf_op jit(solution)/shard_map/closing/pallas_call | solution.py:57
  (2 shorter events, 0.0 us)
Async XLA Ops:
  4.3 3.8 %collective-permute-start = (bf16[128,1408]{1,0:T(8,128)(2,1)S(1)}, bf16[128,1408]{1,0:T(8,128)(2,1)S(1)}, u32[]{:S(2)}, u32[]{:S(2)}) collective-permute-start(bf16[128,1408]{1,0:T(8,128)(2,1)S(1)} %get-tuple-element.13), channel_id=1, source_target_pairs={{0,4},{4,0},{1,5},{5,1},{2,6},{6,2},{3,7},{7,3},{8,12},{12,8},{9,1... | collective-permute-start | bytes 1081352 | tf_op jit(solution)/shard_map/ppermute | solution.py:336
  5.8 28.1 %slice-start = ((s8[6553600]{0:T(1024)(128)(4,1)}), s8[4194304]{0:T(1024)(128)(4,1)S(1)}, s32[]{:S(2)}) async-start(s8[6553600]{0:T(1024)(128)(4,1)} %bitcast.2), calls=%async_computation.2 | async-start | bytes 8388608
  5.8 28.1 %slice-start.2 = ((s8[6553600]{0:T(1024)(128)(4,1)}), s8[2359296]{0:T(1024)(128)(4,1)S(1)}, s32[]{:S(2)}) async-start(s8[6553600]{0:T(1024)(128)(4,1)} %bitcast.4), calls=%async_computation.4 | async-start | bytes 4718592
  6.4 1.7 %collective-permute-start.1 = (bf16[128,1280]{1,0:T(8,128)(2,1)S(1)}, bf16[128,1280]{1,0:T(8,128)(2,1)S(1)}, u32[]{:S(2)}, u32[]{:S(2)}) collective-permute-start(bf16[128,1280]{1,0:T(8,128)(2,1)S(1)} %get-tuple-element.17), channel_id=1, source_target_pairs={{0,4},{4,0},{1,5},{5,1},{2,6},{6,2},{3,7},{7,3},{8,12},{12,8},{9,1... | collective-permute-start | bytes 983048 | tf_op jit(solution)/shard_map/ppermute | solution.py:338
  8.2 25.7 %slice-start.1 = ((s8[6553600]{0:T(1024)(128)(4,1)}), s8[2359296]{0:T(1024)(128)(4,1)S(1)}, s32[]{:S(2)}) async-start(s8[6553600]{0:T(1024)(128)(4,1)} %bitcast.2), calls=%async_computation.3 | async-start | bytes 4718592
  8.2 25.7 %slice-start.3 = ((s8[6553600]{0:T(1024)(128)(4,1)}), s8[4194304]{0:T(1024)(128)(4,1)S(1)}, s32[]{:S(2)}) async-start(s8[6553600]{0:T(1024)(128)(4,1)} %bitcast.4), calls=%async_computation.5 | async-start | bytes 8388608
  56.9 4.9 %collective-permute-start.2 = (bf16[64,2,2688]{2,1,0:T(2,128)(2,1)S(1)}, bf16[64,2,2688]{2,1,0:T(2,128)(2,1)S(1)}, u32[]{:S(2)}, u32[]{:S(2)}) collective-permute-start(bf16[64,2,2688]{2,1,0:T(2,128)(2,1)S(1)} %all_to_all.11.mine_ref), channel_id=1, source_target_pairs={{0,4},{4,0},{1,5},{5,1},{2,6},{6,2},{3,7},{7,3},{8,12},{12,8},{9,1... | collective-permute-start | bytes 2064392 | tf_op jit(solution)/shard_map/ppermute | solution.py:344

commit v7 on v5

--- a/solution.py
+++ b/solution.py
@@ -90,24 +90,22 @@
     slots = weight_ref.shape[1]
     count, width = rows_ref.shape
     start = pl.multiple_of(at_ref[0] * count, count)
-    loads = [
-        pltpu.make_async_copy(source, target, sems.at[at])
-        for at, (source, target) in enumerate(
-            (
-                (weight_hbm, weight_ref),
-                (tok_hbm.at[pl.ds(start, count)], rows_ref),
-                (cot_hbm, cot_ref),
-            )
-        )
-    ]
-    loads[0].start()
-    loads[1].start()
+    block = count // 4
+    parts = [pl.ds(at * block, block) for at in range(4)]
+    loads = [pltpu.make_async_copy(weight_hbm, weight_ref, sems.at[0])]
+    for at, part in enumerate(parts):
+        source = tok_hbm.at[pl.ds(start + at * block, block)]
+        loads.append(pltpu.make_async_copy(source, rows_ref.at[part], sems.at[1 + at]))
+    loads.append(pltpu.make_async_copy(cot_hbm, cot_ref, sems.at[5]))
+    for copy in loads[:5]:
+        copy.start()
     order = ordering(at_ref[1], slots)
     loads[0].wait()
     weight = product(order, weight_ref[...], 1, 1).astype(LOW)
     order_ref[...] = weight
-    loads[1].wait()
-    loads[2].start()
+    for copy in loads[1:5]:
+        copy.wait()
+    loads[5].start()
     rows = rows_ref[...]
     logits = product(weight, rows, 1, 1)
     logit_ref[...] = logits
@@ -118,7 +116,7 @@
     halves(product(shifted.astype(LOW), rows, 1, 0), outs, slice(0, width))
     pieces = place(split3(slot_max) + split3(slot_sum), (slots, EXTRA), 1)
     halves(pieces, outs, slice(width, width + EXTRA))
-    loads[2].wait()
+    loads[5].wait()
 
 
 def opening(at, tokens, slot_weight, cotangent):
@@ -133,7 +131,7 @@
         [IN_SMEM] + [IN_HBM] * 3,
         [IN_VMEM] * len(shapes),
         [jax.ShapeDtypeStruct(*shape) for shape in shapes],
-        [pltpu.VMEM((width, slots), LOW), pltpu.SemaphoreType.DMA((3,))],
+        [pltpu.VMEM((width, slots), LOW), pltpu.SemaphoreType.DMA((6,))],
     )
 
 
@@ -169,8 +167,9 @@
     )
 
 
-def merge_kernel(kept_ref, taken_ref, kept_grad_ref, taken_grad_ref, out_ref):
-    width = kept_grad_ref.shape[1]
+def merge_slots_kernel(kept_ref, taken_ref, out_ref):
+    peers, own, wide = out_ref.shape
+    width = kept_ref.shape[1] - EXTRA
     kept, taken = kept_ref[:, width:].astype(WIDE), taken_ref[:, width:].astype(WIDE)
     kept_max, taken_max = lanes(kept, 0), lanes(taken, 0)
     top = jnp.maximum(kept_max, taken_max)
@@ -179,33 +178,38 @@
     slots = kept_scale * kept_ref[:, :width].astype(WIDE) + taken_scale * taken_ref[
         :, :width
     ].astype(WIDE)
-    grads = kept_grad_ref[...].astype(WIDE) + taken_grad_ref[...].astype(WIDE)
     pieces = place(split3(top) + split3(total), kept.shape, 1)
+    out_ref[:, :, :width] = slots.astype(LOW).reshape(peers, own, width)
+    out_ref[:, :, wide - EXTRA :] = pieces.astype(LOW).reshape(peers, own, EXTRA)
+
+
+def merge_grads_kernel(sent_ref, kept_ref, taken_ref, out_ref):
     peers, own = out_ref.shape[:2]
-    out_ref[:, :, :width] = slots.astype(LOW).reshape(peers, own, width)
+    width = kept_ref.shape[1]
+    grads = kept_ref[...].astype(WIDE) + taken_ref[...].astype(WIDE)
     out_ref[:, :, width : 2 * width] = grads.astype(LOW).reshape(peers, own, width)
-    out_ref[:, :, 2 * width :] = pieces.astype(LOW).reshape(peers, own, EXTRA)
-
-
-def merge(kept, taken, kept_grad, taken_grad, peers):
-    wide = kept.shape[1] + kept_grad.shape[1]
-    shape = jax.ShapeDtypeStruct((peers, kept.shape[0] // peers, wide), LOW)
-    args = (kept, taken, kept_grad, taken_grad)
-    return call(merge_kernel, "merge", args, [IN_VMEM] * 4, IN_VMEM, shape, (), SPAN)
-
-
-PART = 256
-FEW = 32
-
-
-def two_rows(left, right_ref, first):
-    columns = [[], []]
-    for at in range(first, first + PART, FEW):
-        right = right_ref[0, at : at + FEW, :].astype(WIDE)
-        for row in range(2):
-            columns[row].append(jnp.sum(left[row] * right, axis=1, keepdims=True))
-    columns = [jnp.concatenate(column, axis=0) for column in columns]
-    return place(columns, (PART, EXTRA), 1).T[:8]
+
+
+def merge_slots(kept, taken, width, peers):
+    shape = jax.ShapeDtypeStruct((peers, kept.shape[0] // peers, kept.shape[1] + width), LOW)
+    args = (kept, taken)
+    return call(merge_slots_kernel, "merge_slots", args, [IN_VMEM] * 2, IN_VMEM, shape, (), SIDE)
+
+
+def merge_grads(sent, kept, taken):
+    return pl.pallas_call(
+        merge_grads_kernel,
+        in_specs=[IN_VMEM] * 3,
+        out_specs=IN_VMEM,
+        out_shape=jax.ShapeDtypeStruct(sent.shape, LOW),
+        input_output_aliases={0: 0},
+        compiler_params=pltpu.CompilerParams(vmem_limit_bytes=LIMIT),
+        cost_estimate=SPAN,
+        name="merge_grads",
+    )(sent, kept, taken)
+
+
+PART = 512
 
 
 def expert_kernel(got_ref, in_ref, out_ref, told_ref):
@@ -237,7 +241,7 @@
     front, back = slice(0, width), slice(width, 2 * width)
     exact = [(sums_of(row, front) + sums_of(row + 2, front)) / totals[row] for row in range(2)]
     exact = place(exact, (8, width), 0)
-    out_grad = [sums_of(4, back).astype(LOW).astype(WIDE), sums_of(5, back).astype(LOW).astype(WIDE)]
+    out_grad = place([sums_of(4, back), sums_of(5, back)], (8, width), 0).astype(LOW)
     slot_low = exact.astype(LOW)
     rate = 0.7978845608028654
     slot_out = jnp.zeros((8, width), WIDE)
@@ -245,7 +249,7 @@
     for first in range(0, in_ref.shape[2], PART):
         part = slice(first, first + PART)
         preact = product(slot_low, in_ref[0, :, part], 1, 0)
-        hid_grad = two_rows(out_grad, out_ref, first)
+        hid_grad = product(out_grad, out_ref[0, part, :], 1, 1)
         square = preact * preact
         curve = jnp.tanh(rate * (preact + 0.044715 * square * preact))
         low_hidden = (0.5 * preact * (1.0 + curve)).astype(LOW)
@@ -347,7 +351,9 @@
     kept_grad, given_grad = grads_of(columns, cot)
     taken_grad = lax.ppermute(given_grad, "core", swap)
     logits, combine = combining(rows, weight)
-    sent = merge(kept, taken, kept_grad, taken_grad, peers)
+    sent = merge_grads(
+        merge_slots(kept, taken, cotangent.shape[1], peers), kept_grad, taken_grad
+    )
     got = lax.all_to_all(sent, torus, split_axis=0, concat_axis=0, tiled=True)
     told = expert(got, w_in, w_out)
     told = lax.all_to_all(told, torus, split_axis=0, concat_axis=0, tiled=True)

time: 65 us -> 64.2 us (0.988)
    ppermute x1, waiting for transfers between devices: 1.59 us -> 0.68 us  [shards(): taken_grad = lax.ppermute(given_grad, 'core', swap)]
  transfers between devices with their start and end apart: 3 -> 3, of which waited for: 2 -> 3; matrix products, arithmetic and copies ran while one was open for 0% -> 0% of each run, Pallas kernels for 2% -> 3%
where the time goes in v7:
time: 64.2 us; the launch traced here: 64 us
  blocking collectives  42.4 us (66%)
  Pallas kernels  13.7 us (21%)
  starting transfers between devices  4.75 us (7%)
  waiting for transfers between devices  2.33 us (4%)
  between operations  0.71 us (1%)
    all_to_all x1, blocking collectives, shards(): got = lax.all_to_all(sent, torus, split_axis=0, concat_axis=0, tiled=True)  25.2 us
    all_to_all x1, blocking collectives, shards(): told = lax.all_to_all(told, torus, split_axis=0, concat_axis=0, tiled=True)  17.3 us
    pallas_call x6, Pallas kernels, call(): pl.pallas_call(kernel, in_specs=specs, out_specs=out_specs, out_shape=out...  13.6 us
    ppermute x1, starting transfers between devices, shards(): pair = lax.ppermute(told, 'core', swap)  3.16 us
    ppermute x1, starting transfers between devices, shards(): taken = lax.ppermute(given, 'core', swap)  1.5 us
  transfers between devices with their start and end apart: 3, of which 3 were waited for; matrix products, arithmetic and copies ran while one was open for 0% of the time, Pallas kernels for 3%

profile of v7, /device:TPU:1, one launch (start us, length us, event | category | flops | bytes accessed | tf_op | source)
XLA Modules:
  0.0 64.0 jit_solution(2759058213362853579)
XLA Ops:
  0.6 0.1 pad_add_fusion.at_ref
  0.7 3.4 %opening.1 = (bf16[128,1408]{1,0:T(8,128)(2,1)S(1)}, bf16[128,1408]{1,0:T(8,128)(2,1)S(1)}, f32[256,512]{1,0:T(8,128)S(1)}, bf16[256,1280]{1,0:T(8,128)(2,1)S(1)...) custom-call(s32[2]{0:T(128)S(1)} %pad_add_fusion.at_ref, bf16[2048,1280]{1,0:T(8,128)(2,1)} %tok_hbm.1, ...), custom_call_target="tpu_custom_call" | custom-call | tf_op jit(solution)/shard_map/opening/pallas_call | solution.py:57
  4.1 1.5 %collective-permute-start = (bf16[128,1408]{1,0:T(8,128)(2,1)S(1)}, bf16[128,1408]{1,0:T(8,128)(2,1)S(1)}, u32[]{:S(2)}, u32[]{:S(2)}) collective-permute-start(bf16[128,1408]{1,0:T(8,128)(2,1)S(1)} %get-tuple-element.13), channel_id=1, source_target_pairs={{0,4},{4,0},{1,5},{5,1},{2,6},{6,2},{3,7},{7,3},{8,12},{12,8},{9,1... | collective-permute-start | bytes 1081352 | tf_op jit(solution)/shard_map/ppermute | solution.py:350
  5.6 0.6 grads.1
  6.3 0.1 collective-permute-start.1
  6.3 0.6 collective-permute-done.taken_ref
  6.9 0.0 slice-start
  6.9 0.0 slice-start.2
  6.9 0.3 merge_slots.1.sent_ref
  7.3 0.7 %collective-permute-done.1.taken_ref = bf16[128,1280]{1,0:T(8,128)(2,1)S(1)} collective-permute-done((bf16[128,1280]{1,0:T(8,128)(2,1)S(1)}, bf16[128,1280]{1,0:T(8,128)(2,1)S(1)}, u32[]{:S(2)}, u32[]{:S(2)}) %collective-permute-start.1) | collective-permute-done | bytes 327712 | tf_op jit(solution)/shard_map/ppermute | solution.py:352
  8.0 0.0 slice-start.1
  8.0 0.0 slice-start.3
  8.0 0.1 merge_grads.1
  8.1 25.2 %all_to_all.10.got_ref = bf16[64,2,2688]{2,1,0:T(2,128)(2,1)S(1)} all-to-all(bf16[64,2,2688]{2,1,0:T(2,128)(2,1)S(1)} %merge_grads.1), channel_id=1, replica_groups=mesh['x'=4,'z'=4,'core'=2,'exp'=4] {'x','z','exp'}, dimensions={0} | all-to-all | bytes 1376256 | tf_op jit(solution)/shard_map/all_to_all | solution.py:357
  33.3 0.0 slice-done
  33.3 0.0 slice-done.2
  33.3 0.0 slice-done.1
  33.3 0.0 slice-done.3
  33.3 5.6 %expert.1 = bf16[64,2,2688]{2,1,0:T(2,128)(2,1)S(1)} custom-call(bf16[64,2,2688]{2,1,0:T(2,128)(2,1)S(1)} %all_to_all.10.got_ref, bf16[1,1280,2560]{2,1,0:T(8,128)(2,1)S(1)} %bitcast.3, bf16[1,2560,1280]{2,1,0:T(8,128)(2,1)S(1)} %bitcast.5), custom_call_target="tpu_custom_call" | custom-call | tf_op jit(solution)/shard_map/expert/pallas_call | solution.py:57
  38.9 17.3 %all_to_all.11.mine_ref = bf16[64,2,2688]{2,1,0:T(2,128)(2,1)S(1)} all-to-all(bf16[64,2,2688]{2,1,0:T(2,128)(2,1)S(1)} %expert.1), channel_id=1, replica_groups=mesh['x'=4,'z'=4,'core'=2,'exp'=4] {'x','z','exp'}, dimensions={0} | all-to-all | bytes 1376256 | tf_op jit(solution)/shard_map/all_to_all | solution.py:359
  56.2 3.2 %collective-permute-start.2 = (bf16[64,2,2688]{2,1,0:T(2,128)(2,1)S(1)}, bf16[64,2,2688]{2,1,0:T(2,128)(2,1)S(1)}, u32[]{:S(2)}, u32[]{:S(2)}) collective-permute-start(bf16[64,2,2688]{2,1,0:T(2,128)(2,1)S(1)} %all_to_all.11.mine_ref), channel_id=1, source_target_pairs={{0,4},{4,0},{1,5},{5,1},{2,6},{6,2},{3,7},{7,3},{8,12},{12,8},{9,1... | collective-permute-start | bytes 2064392 | tf_op jit(solution)/shard_map/ppermute | solution.py:360
  59.4 0.7 %combining.1 = (f32[512,256]{1,0:T(8,128)S(1)}, f32[512,256]{1,0:T(8,128)S(1)}) custom-call(bf16[512,1280]{1,0:T(8,128)(2,1)S(1)} %get-tuple-element.18.rows_ref.tok_ref, bf16[256,1280]{1,0:T(8,128)(2,1)S(1)} %get-tuple-element.19.order_ref), custom_call_target="tpu_custom_call" | custom-call | flops 1000000000 | bytes 4000000 | tf_op jit(solution)/shard_map/combining/pallas_call | solution.py:57
  60.1 1.1 %collective-permute-done.2.pair_ref = bf16[64,2,2688]{2,1,0:T(2,128)(2,1)S(1)} collective-permute-done((bf16[64,2,2688]{2,1,0:T(2,128)(2,1)S(1)}, bf16[64,2,2688]{2,1,0:T(2,128)(2,1)S(1)}, u32[]{:S(2)}, u32[]{:S(2)}) %collective-permute-start.2) | collective-permute-done | bytes 688160 | tf_op jit(solution)/shard_map/ppermute | solution.py:360
  61.1 2.9 %closing.1 = (bf16[512,1280]{1,0:T(8,128)(2,1)}, bf16[512,1280]{1,0:T(8,128)(2,1)}) custom-call(bf16[64,2,2688]{2,1,0:T(2,128)(2,1)S(1)} %all_to_all.11.mine_ref, bf16[64,2,2688]{2,1,0:T(2,128)(2,1)S(1)} %collective-permute-done.2.pair_ref, bf16[512,1280]{1,0:T(8,128)(2,1)S(1)} %get-tuple-element.18.rows_ref.tok_ref, ...), custom_call_target="tpu_custom_call" | custom-call | tf_op jit(solution)/shard_map/closing/pallas_call | solution.py:57
  (2 shorter events, 0.0 us)
Async XLA Ops:
  4.1 2.8 %collective-permute-start = (bf16[128,1408]{1,0:T(8,128)(2,1)S(1)}, bf16[128,1408]{1,0:T(8,128)(2,1)S(1)}, u32[]{:S(2)}, u32[]{:S(2)}) collective-permute-start(bf16[128,1408]{1,0:T(8,128)(2,1)S(1)} %get-tuple-element.13), channel_id=1, source_target_pairs={{0,4},{4,0},{1,5},{5,1},{2,6},{6,2},{3,7},{7,3},{8,12},{12,8},{9,1... | collective-permute-start | bytes 1081352 | tf_op jit(solution)/shard_map/ppermute | solution.py:350
  6.3 1.7 %collective-permute-start.1 = (bf16[128,1280]{1,0:T(8,128)(2,1)S(1)}, bf16[128,1280]{1,0:T(8,128)(2,1)S(1)}, u32[]{:S(2)}, u32[]{:S(2)}) collective-permute-start(bf16[128,1280]{1,0:T(8,128)(2,1)S(1)} %get-tuple-element.17), channel_id=1, source_target_pairs={{0,4},{4,0},{1,5},{5,1},{2,6},{6,2},{3,7},{7,3},{8,12},{12,8},{9,1... | collective-permute-start | bytes 983048 | tf_op jit(solution)/shard_map/ppermute | solution.py:352
  6.9 26.4 %slice-start = ((s8[6553600]{0:T(1024)(128)(4,1)}), s8[4194304]{0:T(1024)(128)(4,1)S(1)}, s32[]{:S(2)}) async-start(s8[6553600]{0:T(1024)(128)(4,1)} %bitcast.2), calls=%async_computation.2 | async-start | bytes 8388608
  6.9 26.4 %slice-start.2 = ((s8[6553600]{0:T(1024)(128)(4,1)}), s8[2359296]{0:T(1024)(128)(4,1)S(1)}, s32[]{:S(2)}) async-start(s8[6553600]{0:T(1024)(128)(4,1)} %bitcast.4), calls=%async_computation.4 | async-start | bytes 4718592
  8.0 25.3 %slice-start.1 = ((s8[6553600]{0:T(1024)(128)(4,1)}), s8[2359296]{0:T(1024)(128)(4,1)S(1)}, s32[]{:S(2)}) async-start(s8[6553600]{0:T(1024)(128)(4,1)} %bitcast.2), calls=%async_computation.3 | async-start | bytes 4718592
  8.0 25.3 %slice-start.3 = ((s8[6553600]{0:T(1024)(128)(4,1)}), s8[4194304]{0:T(1024)(128)(4,1)S(1)}, s32[]{:S(2)}) async-start(s8[6553600]{0:T(1024)(128)(4,1)} %bitcast.4), calls=%async_computation.5 | async-start | bytes 8388608
  56.2 4.9 %collective-permute-start.2 = (bf16[64,2,2688]{2,1,0:T(2,128)(2,1)S(1)}, bf16[64,2,2688]{2,1,0:T(2,128)(2,1)S(1)}, u32[]{:S(2)}, u32[]{:S(2)}) collective-permute-start(bf16[64,2,2688]{2,1,0:T(2,128)(2,1)S(1)} %all_to_all.11.mine_ref), channel_id=1, source_target_pairs={{0,4},{4,0},{1,5},{5,1},{2,6},{6,2},{3,7},{7,3},{8,12},{12,8},{9,1... | collective-permute-start | bytes 2064392 | tf_op jit(solution)/shard_map/ppermute | solution.py:360

commit v8 on v7

--- a/solution.py
+++ b/solution.py
@@ -275,68 +275,94 @@
     return call(expert_kernel, "expert", (got, w_in, w_out), [IN_VMEM] * 3, IN_VMEM, shape)
 
 
+def unpack_kernel(told_ref, out_ref, in_ref):
+    half, width = out_ref.shape
+    out_ref[...] = told_ref[:, :, :width].reshape(half, width)
+    in_ref[...] = told_ref[:, :, width:].reshape(half, width + EXTRA)
+
+
+def unpack(told, width):
+    half = told.shape[0] * told.shape[1]
+    shapes = [jax.ShapeDtypeStruct((half, wide), LOW) for wide in (width, width + EXTRA)]
+    return call(unpack_kernel, "unpack", (told,), [IN_VMEM], [IN_VMEM] * 2, shapes)
+
+
 STEPS = 2
 
 
+def mixing_kernel(mine_ref, pair_ref, cot_ref, comb_ref, mixed_ref, logit_ref, all_out):
+    half = mine_ref.shape[0]
+    block = cot_ref.shape[0] // STEPS
+    all_out[:half, :] = mine_ref[...]
+    all_out[half:, :] = pair_ref[...]
+    for step in range(STEPS):
+        part = pl.ds(step * block, block)
+        combine = comb_ref[part]
+        mixed_ref[part, :] = product(combine.astype(LOW), all_out[...], 1, 0).astype(LOW)
+        comb_grad = product(cot_ref[part], all_out[...], 1, 1)
+        mean = jnp.sum(combine * comb_grad, axis=1, keepdims=True)
+        logit_ref[part, :] = combine * (comb_grad - mean)
+
+
+def mixing(mine, pair, cotangent, combine):
+    rows, width = cotangent.shape
+    slots = combine.shape[1]
+    shapes = [jax.ShapeDtypeStruct((rows, width), LOW), jax.ShapeDtypeStruct((rows, slots), WIDE)]
+    args = (mine, pair, cotangent, combine)
+    scratch = [pltpu.VMEM((slots, width), LOW)]
+    return call(
+        mixing_kernel, "mixing", args, [IN_VMEM] * 4, [IN_VMEM] * 2, shapes, scratch, SIDE
+    )
+
+
 def closing_kernel(
-    mine_ref, pair_ref, tok_ref, cot_ref, comb_ref, logit_ref, order_ref,
+    mixed_ref, mine_ref, pair_ref, tok_ref, comb_ref, logit_ref, order_ref,
     mixed_hbm, grad_hbm,
-    all_out, in_low, rows_ref, mixed_ref, grad_ref, out_sems,
+    in_low, rows_ref, grad_ref, sems,
 ):
-    count, width = cot_ref.shape
-    half = mine_ref.shape[0] * mine_ref.shape[1]
+    count, width = tok_ref.shape
+    half = mine_ref.shape[0]
     block = count // STEPS
+    stores = [pltpu.make_async_copy(mixed_ref, mixed_hbm, sems.at[STEPS])]
+    stores[0].start()
     for at, ref in enumerate((mine_ref, pair_ref)):
         part = slice(at * half, (at + 1) * half)
-        all_out[part, :] = ref[:, :, :width].reshape(half, width)
-        in_low[part, :] = ref[:, :, width : 2 * width].reshape(half, width)
-        pieces = ref[:, :, 2 * width :].reshape(half, EXTRA).astype(WIDE).T
+        in_low[part, :] = ref[:, :width]
+        pieces = ref[:, width:].astype(WIDE).T
         for row in range(3):
             rows_ref[row : row + 1, part] = jnp.sum(
                 pieces[3 * row : 3 * row + 3], axis=0, keepdims=True
             )
     slot_product, highest, scale = rows_ref[0:1], rows_ref[1:2], 1.0 / rows_ref[2:3]
-    stores = []
     for step in range(STEPS):
         part = pl.ds(step * block, block)
-        stores.append(
-            pltpu.make_async_copy(mixed_ref.at[part], mixed_hbm.at[part], out_sems.at[0, step])
-        )
-        stores.append(
-            pltpu.make_async_copy(grad_ref.at[part], grad_hbm.at[part], out_sems.at[1, step])
-        )
-        combine = comb_ref[part]
-        mixed_ref[part, :] = product(combine.astype(LOW), all_out[...], 1, 0).astype(LOW)
-        stores[-2].start()
-        comb_grad = product(cot_ref[part], all_out[...], 1, 1)
-        logit_grad = combine * (comb_grad - jnp.sum(combine * comb_grad, axis=1, keepdims=True))
         dispatch = jnp.exp(logit_ref[part] - highest) * scale
-        logit_grad += dispatch * (product(tok_ref[part], in_low[...], 1, 1) - slot_product)
+        logit_grad = dispatch * (product(tok_ref[part], in_low[...], 1, 1) - slot_product)
+        logit_grad += comb_ref[part]
         token_grad = product(logit_grad.astype(LOW), order_ref[...], 1, 0)
         token_grad += product(dispatch.astype(LOW), in_low[...], 1, 0)
         grad_ref[part, :] = token_grad.astype(LOW)
+        stores.append(pltpu.make_async_copy(grad_ref.at[part], grad_hbm.at[part], sems.at[step]))
         stores[-1].start()
     for copy in stores:
         copy.wait()
 
 
-def closing(mine, pair, tokens, cotangent, combine, logits, weight):
-    rows, width = cotangent.shape
-    slots = weight.shape[0]
+def closing(mixed, mine, pair, tokens, logit_comb, logits, weight):
+    slots, width = weight.shape
+    shape = jax.ShapeDtypeStruct(tokens.shape, LOW)
     return call(
         closing_kernel,
         "closing",
-        (mine, pair, tokens, cotangent, combine, logits, weight),
+        (mixed, mine, pair, tokens, logit_comb, logits, weight),
         [IN_VMEM] * 7,
         [IN_HBM] * 2,
-        [jax.ShapeDtypeStruct((rows, width), LOW)] * 2,
+        [shape] * 2,
         [
             pltpu.VMEM((slots, width), LOW),
-            pltpu.VMEM((slots, width), LOW),
             pltpu.VMEM((8, slots), WIDE),
-            pltpu.VMEM((rows, width), LOW),
-            pltpu.VMEM((rows, width), LOW),
-            pltpu.SemaphoreType.DMA((2, STEPS)),
+            pltpu.VMEM(tokens.shape, LOW),
+            pltpu.SemaphoreType.DMA((STEPS + 1,)),
         ],
     )
 
@@ -357,8 +383,11 @@
     got = lax.all_to_all(sent, torus, split_axis=0, concat_axis=0, tiled=True)
     told = expert(got, w_in, w_out)
     told = lax.all_to_all(told, torus, split_axis=0, concat_axis=0, tiled=True)
-    pair = lax.ppermute(told, "core", swap)
-    return tuple(closing(told, pair, rows, cot, combine, logits, weight))
+    slot_out, in_grad = unpack(told, cotangent.shape[1])
+    pair_out = lax.ppermute(slot_out, "core", swap)
+    pair_grad = lax.ppermute(in_grad, "core", swap)
+    mixed, logit_comb = mixing(slot_out, pair_out, cot, combine)
+    return tuple(closing(mixed, in_grad, pair_grad, rows, logit_comb, logits, weight))
 
 
 def solution(mesh):

time: 64.2 us -> 64.1 us (level)
    pallas_call x6 -> x8, Pallas kernels: 13.6 us -> 13.9 us  [call(): pl.pallas_call(kernel, in_specs=specs, out_specs=out_specs, out_shape=out...]
    ppermute x1 -> x2, starting transfers between devices: 3.16 us -> 3.33 us  [the longest x1 3.24 us: shards(): pair_out = lax.ppermute(slot_out, 'core', swap)]
  transfers between devices with their start and end apart: 3 -> 4, of which waited for: 3 -> 3; matrix products, arithmetic and copies ran while one was open for 0% -> 0% of each run, Pallas kernels for 3% -> 4%
where the time goes in v8:
time: 64.1 us; the launch traced here: 63.9 us
  blocking collectives  42.4 us (66%)
  Pallas kernels  14 us (22%)
  starting transfers between devices  4.93 us (8%)
  waiting for transfers between devices  1.72 us (3%)
  between operations  0.73 us (1%)
    all_to_all x1, blocking collectives, shards(): got = lax.all_to_all(sent, torus, split_axis=0, concat_axis=0, tiled=True)  25.2 us
    all_to_all x1, blocking collectives, shards(): told = lax.all_to_all(told, torus, split_axis=0, concat_axis=0, tiled=True)  17.3 us
    pallas_call x8, Pallas kernels, call(): pl.pallas_call(kernel, in_specs=specs, out_specs=out_specs, out_shape=out...  13.9 us
    ppermute x1, starting transfers between devices, shards(): pair_out = lax.ppermute(slot_out, 'core', swap)  3.24 us
    ppermute x1, starting transfers between devices, shards(): taken = lax.ppermute(given, 'core', swap)  1.5 us
  transfers between devices with their start and end apart: 4, of which 3 were waited for; matrix products, arithmetic and copies ran while one was open for 0% of the time, Pallas kernels for 4%

profile of v8, /device:TPU:1, one launch (start us, length us, event | category | flops | bytes accessed | tf_op | source)
XLA Modules:
  0.0 63.9 jit_solution(5461811779119432499)
XLA Ops:
  0.6 0.1 pad_add_fusion.at_ref
  0.7 3.4 %opening.1 = (bf16[128,1408]{1,0:T(8,128)(2,1)S(1)}, bf16[128,1408]{1,0:T(8,128)(2,1)S(1)}, f32[256,512]{1,0:T(8,128)S(1)}, bf16[256,1280]{1,0:T(8,128)(2,1)S(1)...) custom-call(s32[2]{0:T(128)S(1)} %pad_add_fusion.at_ref, bf16[2048,1280]{1,0:T(8,128)(2,1)} %tok_hbm.1, ...), custom_call_target="tpu_custom_call" | custom-call | tf_op jit(solution)/shard_map/opening/pallas_call | solution.py:57
  4.1 1.5 %collective-permute-start = (bf16[128,1408]{1,0:T(8,128)(2,1)S(1)}, bf16[128,1408]{1,0:T(8,128)(2,1)S(1)}, u32[]{:S(2)}, u32[]{:S(2)}) collective-permute-start(bf16[128,1408]{1,0:T(8,128)(2,1)S(1)} %get-tuple-element.17), channel_id=1, source_target_pairs={{0,4},{4,0},{1,5},{5,1},{2,6},{6,2},{3,7},{7,3},{8,12},{12,8},{9,1... | collective-permute-start | bytes 1081352 | tf_op jit(solution)/shard_map/ppermute | solution.py:376
  5.6 0.6 grads.1
  6.3 0.1 collective-permute-start.1
  6.3 0.6 collective-permute-done.taken_ref
  6.9 0.3 merge_slots.1.sent_ref
  7.3 0.7 %collective-permute-done.1.taken_ref = bf16[128,1280]{1,0:T(8,128)(2,1)S(1)} collective-permute-done((bf16[128,1280]{1,0:T(8,128)(2,1)S(1)}, bf16[128,1280]{1,0:T(8,128)(2,1)S(1)}, u32[]{:S(2)}, u32[]{:S(2)}) %collective-permute-start.1) | collective-permute-done | bytes 327712 | tf_op jit(solution)/shard_map/ppermute | solution.py:378
  8.0 0.1 merge_grads.1
  8.1 25.2 %all_to_all.10.got_ref = bf16[64,2,2688]{2,1,0:T(2,128)(2,1)S(1)} all-to-all(bf16[64,2,2688]{2,1,0:T(2,128)(2,1)S(1)} %merge_grads.1), channel_id=1, replica_groups=mesh['x'=4,'z'=4,'core'=2,'exp'=4] {'x','z','exp'}, dimensions={0} | all-to-all | bytes 1376256 | tf_op jit(solution)/shard_map/all_to_all | solution.py:383
  33.3 0.0 slice-done
  33.3 0.0 slice-done.2
  33.3 0.0 slice-done.1
  33.3 0.0 slice-done.3
  33.3 5.6 %expert.1 = bf16[64,2,2688]{2,1,0:T(2,128)(2,1)S(1)} custom-call(bf16[64,2,2688]{2,1,0:T(2,128)(2,1)S(1)} %all_to_all.10.got_ref, bf16[1,1280,2560]{2,1,0:T(8,128)(2,1)S(1)} %bitcast.3, bf16[1,2560,1280]{2,1,0:T(8,128)(2,1)S(1)} %bitcast.5), custom_call_target="tpu_custom_call" | custom-call | tf_op jit(solution)/shard_map/expert/pallas_call | solution.py:57
  38.9 17.3 %all_to_all.11.told_ref = bf16[64,2,2688]{2,1,0:T(2,128)(2,1)S(1)} all-to-all(bf16[64,2,2688]{2,1,0:T(2,128)(2,1)S(1)} %expert.1), channel_id=1, replica_groups=mesh['x'=4,'z'=4,'core'=2,'exp'=4] {'x','z','exp'}, dimensions={0} | all-to-all | bytes 1376256 | tf_op jit(solution)/shard_map/all_to_all | solution.py:385
  56.2 0.1 unpack.1
  56.3 3.2 %collective-permute-start.2 = (bf16[128,1280]{1,0:T(8,128)(2,1)S(1)}, bf16[128,1280]{1,0:T(8,128)(2,1)S(1)}, u32[]{:S(2)}, u32[]{:S(2)}) collective-permute-start(bf16[128,1280]{1,0:T(8,128)(2,1)S(1)} %get-tuple-element.22.mine_ref), channel_id=1, source_target_pairs={{0,4},{4,0},{1,5},{5,1},{2,6},{6,2},{3,7},{7,3},{8,12},{12,8},{9,1... | collective-permute-start | bytes 983048 | tf_op jit(solution)/shard_map/ppermute | solution.py:387
  59.5 0.1 collective-permute-start.3
  59.6 0.7 %combining.1 = (f32[512,256]{1,0:T(8,128)S(1)}, f32[512,256]{1,0:T(8,128)S(1)}) custom-call(bf16[512,1280]{1,0:T(8,128)(2,1)S(1)} %get-tuple-element.23.rows_ref.tok_ref, bf16[256,1280]{1,0:T(8,128)(2,1)S(1)} %get-tuple-element.24.order_ref), custom_call_target="tpu_custom_call" | custom-call | flops 1000000000 | bytes 4000000 | tf_op jit(solution)/shard_map/combining/pallas_call | solution.py:57
  60.3 0.5 collective-permute-done.2.pair_ref
  60.8 0.9 %mixing.1 = (bf16[512,1280]{1,0:T(8,128)(2,1)S(1)}, f32[512,256]{1,0:T(8,128)S(1)}) custom-call(bf16[128,1280]{1,0:T(8,128)(2,1)S(1)} %get-tuple-element.22.mine_ref, bf16[128,1280]{1,0:T(8,128)(2,1)S(1)} %collective-permute-done.2.pair_ref, bf16[512,1280]{1,0:T(8,128)(2,1)S(1)} %get-tuple-element.19.cot_ref, f32[512,256]{1,0:T(8,128)S(1)} %get-tuple-element.25.comb_ref), custom_call_target="tpu_custom_call" | custom-call | flops 1000000000 | bytes 4000000 | tf_op jit(solution)/shard_map/mixing/pallas_call | solution.py:57
  61.7 0.0 collective-permute-done.3.pair_ref
  61.7 2.2 %closing.1 = (bf16[512,1280]{1,0:T(8,128)(2,1)}, bf16[512,1280]{1,0:T(8,128)(2,1)}) custom-call(bf16[512,1280]{1,0:T(8,128)(2,1)S(1)} %get-tuple-element.26.mixed_ref, bf16[128,1408]{1,0:T(8,128)(2,1)S(1)} %get-tuple-element.27.mine_ref, bf16[128,1408]{1,0:T(8,128)(2,1)S(1)} %collective-permute-done.3.pair_ref, ...), custom_call_target="tpu_custom_call" | custom-call | tf_op jit(solution)/shard_map/closing/pallas_call | solution.py:57
  (6 shorter events, 0.0 us)
Async XLA Ops:
  4.1 2.8 %collective-permute-start = (bf16[128,1408]{1,0:T(8,128)(2,1)S(1)}, bf16[128,1408]{1,0:T(8,128)(2,1)S(1)}, u32[]{:S(2)}, u32[]{:S(2)}) collective-permute-start(bf16[128,1408]{1,0:T(8,128)(2,1)S(1)} %get-tuple-element.17), channel_id=1, source_target_pairs={{0,4},{4,0},{1,5},{5,1},{2,6},{6,2},{3,7},{7,3},{8,12},{12,8},{9,1... | collective-permute-start | bytes 1081352 | tf_op jit(solution)/shard_map/ppermute | solution.py:376
  6.3 1.7 %collective-permute-start.1 = (bf16[128,1280]{1,0:T(8,128)(2,1)S(1)}, bf16[128,1280]{1,0:T(8,128)(2,1)S(1)}, u32[]{:S(2)}, u32[]{:S(2)}) collective-permute-start(bf16[128,1280]{1,0:T(8,128)(2,1)S(1)} %get-tuple-element.21), channel_id=1, source_target_pairs={{0,4},{4,0},{1,5},{5,1},{2,6},{6,2},{3,7},{7,3},{8,12},{12,8},{9,1... | collective-permute-start | bytes 983048 | tf_op jit(solution)/shard_map/ppermute | solution.py:378
  6.9 26.4 %slice-start = ((s8[6553600]{0:T(1024)(128)(4,1)}), s8[4194304]{0:T(1024)(128)(4,1)S(1)}, s32[]{:S(2)}) async-start(s8[6553600]{0:T(1024)(128)(4,1)} %bitcast.2), calls=%async_computation.2 | async-start | bytes 8388608
  6.9 26.4 %slice-start.2 = ((s8[6553600]{0:T(1024)(128)(4,1)}), s8[2359296]{0:T(1024)(128)(4,1)S(1)}, s32[]{:S(2)}) async-start(s8[6553600]{0:T(1024)(128)(4,1)} %bitcast.4), calls=%async_computation.4 | async-start | bytes 4718592
  8.0 25.3 %slice-start.1 = ((s8[6553600]{0:T(1024)(128)(4,1)}), s8[2359296]{0:T(1024)(128)(4,1)S(1)}, s32[]{:S(2)}) async-start(s8[6553600]{0:T(1024)(128)(4,1)} %bitcast.2), calls=%async_computation.3 | async-start | bytes 4718592
  8.0 25.3 %slice-start.3 = ((s8[6553600]{0:T(1024)(128)(4,1)}), s8[4194304]{0:T(1024)(128)(4,1)S(1)}, s32[]{:S(2)}) async-start(s8[6553600]{0:T(1024)(128)(4,1)} %bitcast.4), calls=%async_computation.5 | async-start | bytes 8388608
  56.3 4.5 %collective-permute-start.2 = (bf16[128,1280]{1,0:T(8,128)(2,1)S(1)}, bf16[128,1280]{1,0:T(8,128)(2,1)S(1)}, u32[]{:S(2)}, u32[]{:S(2)}) collective-permute-start(bf16[128,1280]{1,0:T(8,128)(2,1)S(1)} %get-tuple-element.22.mine_ref), channel_id=1, source_target_pairs={{0,4},{4,0},{1,5},{5,1},{2,6},{6,2},{3,7},{7,3},{8,12},{12,8},{9,1... | collective-permute-start | bytes 983048 | tf_op jit(solution)/shard_map/ppermute | solution.py:387
  59.5 2.2 %collective-permute-start.3 = (bf16[128,1408]{1,0:T(8,128)(2,1)S(1)}, bf16[128,1408]{1,0:T(8,128)(2,1)S(1)}, u32[]{:S(2)}, u32[]{:S(2)}) collective-permute-start(bf16[128,1408]{1,0:T(8,128)(2,1)S(1)} %get-tuple-element.27.mine_ref), channel_id=1, source_target_pairs={{0,4},{4,0},{1,5},{5,1},{2,6},{6,2},{3,7},{7,3},{8,12},{12,8},{9,1... | collective-permute-start | bytes 1081352 | tf_op jit(solution)/shard_map/ppermute | solution.py:388

commit v9 on v7

--- a/solution.py
+++ b/solution.py
@@ -66,13 +66,14 @@
     )(*args)
 
 
-def ordering(core, slots):
+def ordering(group, slots):
     to = lax.broadcasted_iota(jnp.int32, (slots, 1), 0)
     source = lax.broadcasted_iota(jnp.int32, (slots, slots), 1)
     half = slots // 2
     within = to % half
-    other = jnp.where(to // half == 0, core, 1 - core)
-    wanted = (within // 8) * 16 + other * 8 + within % 8
+    chip, y = within // 8, (within // 2) % 4
+    core = (group + to // half + chip // 4 + chip % 4 + y) % 2
+    wanted = chip * 16 + core * 8 + within % 8
     return (source == wanted).astype(WIDE).astype(LOW)
 
 
@@ -341,23 +342,38 @@
     )
 
 
+def place_of(x, z, core, y):
+    return ((x * 4 + z) * 2 + core) * 4 + y
+
+
+def groups_of():
+    chips = [(x, z, y) for x in range(4) for z in range(4) for y in range(4)]
+    return [
+        [place_of(x, z, (group + x + z + y) % 2, y) for x, z, y in chips] for group in range(2)
+    ]
+
+
 def shards(tokens, slot_weight, w_in, w_out, cotangent):
-    torus = ("x", "z", "exp")
-    swap = [(0, 1), (1, 0)]
-    at = jnp.stack([lax.axis_index("exp"), lax.axis_index("core")]).astype(jnp.int32)
-    peers = lax.axis_size(torus)
+    every = ("x", "z", "core", "exp")
+    x, z, core, y = (lax.axis_index(axis) for axis in every)
+    at = jnp.stack([y, (core + x + z + y) % 2]).astype(jnp.int32)
+    peers = lax.axis_size(every) // 2
+    swap = lambda array: lax.ppermute(array, "core", [(0, 1), (1, 0)])
+    trade = lambda array: lax.all_to_all(
+        array, every, 0, 0, axis_index_groups=groups_of(), tiled=True
+    )
     kept, given, columns, weight, rows, cot = opening(at, tokens, slot_weight, cotangent)
-    taken = lax.ppermute(given, "core", swap)
+    taken = swap(given)
     kept_grad, given_grad = grads_of(columns, cot)
-    taken_grad = lax.ppermute(given_grad, "core", swap)
+    taken_grad = swap(given_grad)
     logits, combine = combining(rows, weight)
     sent = merge_grads(
         merge_slots(kept, taken, cotangent.shape[1], peers), kept_grad, taken_grad
     )
-    got = lax.all_to_all(sent, torus, split_axis=0, concat_axis=0, tiled=True)
+    got = trade(sent)
     told = expert(got, w_in, w_out)
-    told = lax.all_to_all(told, torus, split_axis=0, concat_axis=0, tiled=True)
-    pair = lax.ppermute(told, "core", swap)
+    told = trade(told)
+    pair = swap(told)
     return tuple(closing(told, pair, rows, cot, combine, logits, weight))
 
 

time: 64.2 us -> 65.7 us (1.023)
  blocking collectives: 42.4 us -> 46.7 us
  starting transfers between devices: 4.75 us -> 1.6 us
    all_to_all x2, blocking collectives: 42.4 us -> 46.7 us  [shards(): lax.all_to_all(array, every, 0, 0, axis_index_groups=groups_of(), tiled=T...]
    ppermute x3, starting transfers between devices: 4.75 us -> 1.6 us  [shards(): swap = lambda array: lax.ppermute(array, 'core', [(0, 1), (1, 0)])]
where the time goes in v9:
time: 65.7 us; the launch traced here: 65.5 us
  blocking collectives  46.7 us (71%)
  Pallas kernels  13.7 us (21%)
  waiting for transfers between devices  2.68 us (4%)
  starting transfers between devices  1.6 us (2%)
  between operations  0.72 us (1%)
    all_to_all x2, blocking collectives, shards(): lax.all_to_all(array, every, 0, 0, axis_index_groups=groups_of(), tiled=T...  46.7 us
    pallas_call x6, Pallas kernels, call(): pl.pallas_call(kernel, in_specs=specs, out_specs=out_specs, out_shape=out...  13.6 us
    ppermute x3, waiting for transfers between devices, shards(): swap = lambda array: lax.ppermute(array, 'core', [(0, 1), (1, 0)])  2.68 us
    ppermute x3, starting transfers between devices, shards(): swap = lambda array: lax.ppermute(array, 'core', [(0, 1), (1, 0)])  1.6 us
  transfers between devices with their start and end apart: 3, of which 3 were waited for; matrix products, arithmetic and copies ran while one was open for 0% of the time, Pallas kernels for 3%

profile of v9, /device:TPU:1, one launch (start us, length us, event | category | flops | bytes accessed | tf_op | source)
XLA Modules:
  0.0 65.5 jit_solution(7981606130375588978)
XLA Ops:
  0.6 0.1 pad_add_fusion.at_ref
  0.7 3.4 %opening.1 = (bf16[128,1408]{1,0:T(8,128)(2,1)S(1)}, bf16[128,1408]{1,0:T(8,128)(2,1)S(1)}, f32[256,512]{1,0:T(8,128)S(1)}, bf16[256,1280]{1,0:T(8,128)(2,1)S(1)...) custom-call(s32[2]{0:T(128)S(1)} %pad_add_fusion.at_ref, bf16[2048,1280]{1,0:T(8,128)(2,1)} %tok_hbm.1, ...), custom_call_target="tpu_custom_call" | custom-call | tf_op jit(solution)/shard_map/opening/pallas_call | solution.py:57
  4.1 1.5 %collective-permute-start = (bf16[128,1408]{1,0:T(8,128)(2,1)S(1)}, bf16[128,1408]{1,0:T(8,128)(2,1)S(1)}, u32[]{:S(2)}, u32[]{:S(2)}) collective-permute-start(bf16[128,1408]{1,0:T(8,128)(2,1)S(1)} %get-tuple-element.13), channel_id=1, source_target_pairs={{0,4},{4,0},{1,5},{5,1},{2,6},{6,2},{3,7},{7,3},{8,12},{12,8},{9,1... | collective-permute-start | bytes 1081352 | tf_op jit(solution)/shard_map/ppermute | solution.py:361
  5.6 0.6 grads.1
  6.3 0.1 collective-permute-start.1
  6.4 0.6 collective-permute-done.taken_ref
  6.9 0.0 slice-start
  6.9 0.0 slice-start.2
  6.9 0.3 merge_slots.1.sent_ref
  7.3 0.7 %collective-permute-done.1.taken_ref = bf16[128,1280]{1,0:T(8,128)(2,1)S(1)} collective-permute-done((bf16[128,1280]{1,0:T(8,128)(2,1)S(1)}, bf16[128,1280]{1,0:T(8,128)(2,1)S(1)}, u32[]{:S(2)}, u32[]{:S(2)}) %collective-permute-start.1) | collective-permute-done | bytes 327712 | tf_op jit(solution)/shard_map/ppermute | solution.py:361
  8.0 0.0 slice-start.1
  8.0 0.0 slice-start.3
  8.0 0.1 merge_grads.1
  8.1 26.8 %all_to_all.10.got_ref = bf16[64,2,2688]{2,1,0:T(2,128)(2,1)S(1)} all-to-all(bf16[64,2,2688]{2,1,0:T(2,128)(2,1)S(1)} %merge_grads.1), channel_id=1, replica_groups={{0,5,2,7,12,9,14,11,16,21,18,23,28,25,30,27,36,33,38,35,40,45,42,47,52,..., dimensions={0} | all-to-all | bytes 1376256 | tf_op jit(solution)/shard_map/all_to_all | solution.py:362
  34.9 0.0 slice-done
  34.9 0.0 slice-done.2
  34.9 0.0 slice-done.1
  34.9 0.0 slice-done.3
  34.9 5.6 %expert.1 = bf16[64,2,2688]{2,1,0:T(2,128)(2,1)S(1)} custom-call(bf16[64,2,2688]{2,1,0:T(2,128)(2,1)S(1)} %all_to_all.10.got_ref, bf16[1,1280,2560]{2,1,0:T(8,128)(2,1)S(1)} %bitcast.3, bf16[1,2560,1280]{2,1,0:T(8,128)(2,1)S(1)} %bitcast.5), custom_call_target="tpu_custom_call" | custom-call | tf_op jit(solution)/shard_map/expert/pallas_call | solution.py:57
  40.6 19.9 %all_to_all.11.mine_ref = bf16[64,2,2688]{2,1,0:T(2,128)(2,1)S(1)} all-to-all(bf16[64,2,2688]{2,1,0:T(2,128)(2,1)S(1)} %expert.1), channel_id=1, replica_groups={{0,5,2,7,12,9,14,11,16,21,18,23,28,25,30,27,36,33,38,35,40,45,42,47,52,..., dimensions={0} | all-to-all | bytes 1376256 | tf_op jit(solution)/shard_map/all_to_all | solution.py:362
  60.5 0.0 collective-permute-start.2
  60.5 0.7 %combining.1 = (f32[512,256]{1,0:T(8,128)S(1)}, f32[512,256]{1,0:T(8,128)S(1)}) custom-call(bf16[512,1280]{1,0:T(8,128)(2,1)S(1)} %get-tuple-element.18.rows_ref.tok_ref, bf16[256,1280]{1,0:T(8,128)(2,1)S(1)} %get-tuple-element.19.order_ref), custom_call_target="tpu_custom_call" | custom-call | flops 1000000000 | bytes 4000000 | tf_op jit(solution)/shard_map/combining/pallas_call | solution.py:57
  61.2 1.4 %collective-permute-done.2.pair_ref = bf16[64,2,2688]{2,1,0:T(2,128)(2,1)S(1)} collective-permute-done((bf16[64,2,2688]{2,1,0:T(2,128)(2,1)S(1)}, bf16[64,2,2688]{2,1,0:T(2,128)(2,1)S(1)}, u32[]{:S(2)}, u32[]{:S(2)}) %collective-permute-start.2) | collective-permute-done | bytes 688160 | tf_op jit(solution)/shard_map/ppermute | solution.py:361
  62.6 2.9 %closing.1 = (bf16[512,1280]{1,0:T(8,128)(2,1)}, bf16[512,1280]{1,0:T(8,128)(2,1)}) custom-call(bf16[64,2,2688]{2,1,0:T(2,128)(2,1)S(1)} %all_to_all.11.mine_ref, bf16[64,2,2688]{2,1,0:T(2,128)(2,1)S(1)} %collective-permute-done.2.pair_ref, bf16[512,1280]{1,0:T(8,128)(2,1)S(1)} %get-tuple-element.18.rows_ref.tok_ref, ...), custom_call_target="tpu_custom_call" | custom-call | tf_op jit(solution)/shard_map/closing/pallas_call | solution.py:57
  (2 shorter events, 0.0 us)
Async XLA Ops:
  4.1 2.8 %collective-permute-start = (bf16[128,1408]{1,0:T(8,128)(2,1)S(1)}, bf16[128,1408]{1,0:T(8,128)(2,1)S(1)}, u32[]{:S(2)}, u32[]{:S(2)}) collective-permute-start(bf16[128,1408]{1,0:T(8,128)(2,1)S(1)} %get-tuple-element.13), channel_id=1, source_target_pairs={{0,4},{4,0},{1,5},{5,1},{2,6},{6,2},{3,7},{7,3},{8,12},{12,8},{9,1... | collective-permute-start | bytes 1081352 | tf_op jit(solution)/shard_map/ppermute | solution.py:361
  6.3 1.7 %collective-permute-start.1 = (bf16[128,1280]{1,0:T(8,128)(2,1)S(1)}, bf16[128,1280]{1,0:T(8,128)(2,1)S(1)}, u32[]{:S(2)}, u32[]{:S(2)}) collective-permute-start(bf16[128,1280]{1,0:T(8,128)(2,1)S(1)} %get-tuple-element.17), channel_id=1, source_target_pairs={{0,4},{4,0},{1,5},{5,1},{2,6},{6,2},{3,7},{7,3},{8,12},{12,8},{9,1... | collective-permute-start | bytes 983048 | tf_op jit(solution)/shard_map/ppermute | solution.py:361
  6.9 28.0 %slice-start = ((s8[6553600]{0:T(1024)(128)(4,1)}), s8[4194304]{0:T(1024)(128)(4,1)S(1)}, s32[]{:S(2)}) async-start(s8[6553600]{0:T(1024)(128)(4,1)} %bitcast.2), calls=%async_computation.2 | async-start | bytes 8388608
  6.9 28.0 %slice-start.2 = ((s8[6553600]{0:T(1024)(128)(4,1)}), s8[2359296]{0:T(1024)(128)(4,1)S(1)}, s32[]{:S(2)}) async-start(s8[6553600]{0:T(1024)(128)(4,1)} %bitcast.4), calls=%async_computation.4 | async-start | bytes 4718592
  8.0 26.9 %slice-start.1 = ((s8[6553600]{0:T(1024)(128)(4,1)}), s8[2359296]{0:T(1024)(128)(4,1)S(1)}, s32[]{:S(2)}) async-start(s8[6553600]{0:T(1024)(128)(4,1)} %bitcast.2), calls=%async_computation.3 | async-start | bytes 4718592
  8.0 26.9 %slice-start.3 = ((s8[6553600]{0:T(1024)(128)(4,1)}), s8[4194304]{0:T(1024)(128)(4,1)S(1)}, s32[]{:S(2)}) async-start(s8[6553600]{0:T(1024)(128)(4,1)} %bitcast.4), calls=%async_computation.5 | async-start | bytes 8388608
  60.5 2.1 %collective-permute-start.2 = (bf16[64,2,2688]{2,1,0:T(2,128)(2,1)S(1)}, bf16[64,2,2688]{2,1,0:T(2,128)(2,1)S(1)}, u32[]{:S(2)}, u32[]{:S(2)}) collective-permute-start(bf16[64,2,2688]{2,1,0:T(2,128)(2,1)S(1)} %all_to_all.11.mine_ref), channel_id=1, source_target_pairs={{0,4},{4,0},{1,5},{5,1},{2,6},{6,2},{3,7},{7,3},{8,12},{12,8},{9,1... | collective-permute-start | bytes 2064392 | tf_op jit(solution)/shard_map/ppermute | solution.py:361

commit v10 on v7

--- a/solution.py
+++ b/solution.py
@@ -76,15 +76,9 @@
     return (source == wanted).astype(WIDE).astype(LOW)
 
 
-def halves(value, outs, columns):
-    half = outs[0].shape[0]
-    for at, out in enumerate(outs):
-        out[:, columns] = value[at * half : (at + 1) * half].astype(LOW)
-
-
 def opening_kernel(
     at_ref, tok_hbm, weight_hbm, cot_hbm,
-    kept_ref, given_ref, logit_ref, order_ref, rows_ref, cot_ref,
+    given_ref, shift_ref, piece_ref, logit_ref, order_ref, rows_ref, cot_ref,
     weight_ref, sems,
 ):
     slots = weight_ref.shape[1]
@@ -97,7 +91,7 @@
         source = tok_hbm.at[pl.ds(start + at * block, block)]
         loads.append(pltpu.make_async_copy(source, rows_ref.at[part], sems.at[1 + at]))
     loads.append(pltpu.make_async_copy(cot_hbm, cot_ref, sems.at[5]))
-    for copy in loads[:5]:
+    for copy in loads:
         copy.start()
     order = ordering(at_ref[1], slots)
     loads[0].wait()
@@ -105,25 +99,28 @@
     order_ref[...] = weight
     for copy in loads[1:5]:
         copy.wait()
-    loads[5].start()
     rows = rows_ref[...]
     logits = product(weight, rows, 1, 1)
     logit_ref[...] = logits
     slot_max = jnp.max(logits, axis=1, keepdims=True)
     shifted = jnp.exp(logits - slot_max)
     slot_sum = jnp.sum(shifted, axis=1, keepdims=True)
-    outs = (kept_ref, given_ref)
-    halves(product(shifted.astype(LOW), rows, 1, 0), outs, slice(0, width))
+    half = slots // 2
+    shifted = shifted.astype(LOW)
+    given_ref[:, :width] = product(shifted[half:], rows, 1, 0).astype(LOW)
+    shift_ref[...] = shifted[:half]
     pieces = place(split3(slot_max) + split3(slot_sum), (slots, EXTRA), 1)
-    halves(pieces, outs, slice(width, width + EXTRA))
+    given_ref[:, width:] = pieces[half:].astype(LOW)
+    piece_ref[...] = pieces[:half]
     loads[5].wait()
 
 
 def opening(at, tokens, slot_weight, cotangent):
     rows, width = cotangent.shape
     slots = slot_weight.shape[1]
-    shapes = [((slots // 2, width + EXTRA), LOW)] * 2 + [((slots, rows), WIDE)]
-    shapes += [((slots, width), LOW)] + [((rows, width), LOW)] * 2
+    half = slots // 2
+    shapes = [((half, width + EXTRA), LOW), ((half, rows), LOW), ((half, EXTRA), WIDE)]
+    shapes += [((slots, rows), WIDE), ((slots, width), LOW)] + [((rows, width), LOW)] * 2
     return call(
         opening_kernel,
         "opening",
@@ -135,21 +132,23 @@
     )
 
 
-def grads_kernel(logit_ref, cot_ref, kept_ref, given_ref):
+def grads_kernel(logit_ref, cot_ref, given_ref, comb_ref):
     logits = logit_ref[...]
     raised = jnp.exp(logits - jnp.max(logits, axis=0, keepdims=True))
-    combine = raised * (1.0 / jnp.sum(raised, axis=0, keepdims=True))
-    grad_part = product(combine.astype(LOW), cot_ref[...], 1, 0)
-    halves(grad_part, (kept_ref, given_ref), slice(0, grad_part.shape[1]))
+    combine = (raised * (1.0 / jnp.sum(raised, axis=0, keepdims=True))).astype(LOW)
+    half = given_ref.shape[0]
+    given_ref[...] = product(combine[half:], cot_ref[...], 1, 0).astype(LOW)
+    comb_ref[...] = combine[:half]
 
 
 SIDE = pl.CostEstimate(flops=1_000_000_000, bytes_accessed=4_000_000, transcendentals=131_072)
 
 
 def grads_of(logits, cotangent):
-    shape = jax.ShapeDtypeStruct((logits.shape[0] // 2, cotangent.shape[1]), LOW)
+    half, rows = logits.shape[0] // 2, logits.shape[1]
+    shapes = [jax.ShapeDtypeStruct((half, wide), LOW) for wide in (cotangent.shape[1], rows)]
     args = (logits, cotangent)
-    return call(grads_kernel, "grads", args, [IN_VMEM] * 2, [IN_VMEM] * 2, [shape] * 2, (), SIDE)
+    return call(grads_kernel, "grads", args, [IN_VMEM] * 2, [IN_VMEM] * 2, shapes, (), SIDE)
 
 
 def combine_kernel(rows_ref, order_ref, logit_ref, comb_ref):
@@ -167,33 +166,41 @@
     )
 
 
-def merge_slots_kernel(kept_ref, taken_ref, out_ref):
+def merge_slots_kernel(
+    shift_ref, piece_ref, comb_ref, rows_ref, cot_ref, taken_ref, out_ref, grad_ref
+):
     peers, own, wide = out_ref.shape
-    width = kept_ref.shape[1] - EXTRA
-    kept, taken = kept_ref[:, width:].astype(WIDE), taken_ref[:, width:].astype(WIDE)
+    width = rows_ref.shape[1]
+    kept, taken = piece_ref[...], taken_ref[:, width:].astype(WIDE)
     kept_max, taken_max = lanes(kept, 0), lanes(taken, 0)
     top = jnp.maximum(kept_max, taken_max)
     kept_scale, taken_scale = jnp.exp(kept_max - top), jnp.exp(taken_max - top)
     total = kept_scale * lanes(kept, 3) + taken_scale * lanes(taken, 3)
-    slots = kept_scale * kept_ref[:, :width].astype(WIDE) + taken_scale * taken_ref[
-        :, :width
-    ].astype(WIDE)
+    slots = kept_scale * product(shift_ref[...], rows_ref[...], 1, 0)
+    slots += taken_scale * taken_ref[:, :width].astype(WIDE)
     pieces = place(split3(top) + split3(total), kept.shape, 1)
     out_ref[:, :, :width] = slots.astype(LOW).reshape(peers, own, width)
     out_ref[:, :, wide - EXTRA :] = pieces.astype(LOW).reshape(peers, own, EXTRA)
+    grad_ref[...] = product(comb_ref[...], cot_ref[...], 1, 0)
 
 
 def merge_grads_kernel(sent_ref, kept_ref, taken_ref, out_ref):
     peers, own = out_ref.shape[:2]
     width = kept_ref.shape[1]
-    grads = kept_ref[...].astype(WIDE) + taken_ref[...].astype(WIDE)
+    grads = kept_ref[...] + taken_ref[...].astype(WIDE)
     out_ref[:, :, width : 2 * width] = grads.astype(LOW).reshape(peers, own, width)
 
 
-def merge_slots(kept, taken, width, peers):
-    shape = jax.ShapeDtypeStruct((peers, kept.shape[0] // peers, kept.shape[1] + width), LOW)
-    args = (kept, taken)
-    return call(merge_slots_kernel, "merge_slots", args, [IN_VMEM] * 2, IN_VMEM, shape, (), SIDE)
+def merge_slots(shifted, pieces, combine, rows, cotangent, taken, peers):
+    half, width = shifted.shape[0], rows.shape[1]
+    args = (shifted, pieces, combine, rows, cotangent, taken)
+    shapes = [
+        jax.ShapeDtypeStruct((peers, half // peers, taken.shape[1] + width), LOW),
+        jax.ShapeDtypeStruct((half, width), WIDE),
+    ]
+    return call(
+        merge_slots_kernel, "merge_slots", args, [IN_VMEM] * 6, [IN_VMEM] * 2, shapes, (), SIDE
+    )
 
 
 def merge_grads(sent, kept, taken):
@@ -346,14 +353,15 @@
     swap = [(0, 1), (1, 0)]
     at = jnp.stack([lax.axis_index("exp"), lax.axis_index("core")]).astype(jnp.int32)
     peers = lax.axis_size(torus)
-    kept, given, columns, weight, rows, cot = opening(at, tokens, slot_weight, cotangent)
+    given, shifted, pieces, columns, weight, rows, cot = opening(
+        at, tokens, slot_weight, cotangent
+    )
     taken = lax.ppermute(given, "core", swap)
-    kept_grad, given_grad = grads_of(columns, cot)
+    given_grad, kept_combine = grads_of(columns, cot)
     taken_grad = lax.ppermute(given_grad, "core", swap)
     logits, combine = combining(rows, weight)
-    sent = merge_grads(
-        merge_slots(kept, taken, cotangent.shape[1], peers), kept_grad, taken_grad
-    )
+    sent, kept_grad = merge_slots(shifted, pieces, kept_combine, rows, cot, taken, peers)
+    sent = merge_grads(sent, kept_grad, taken_grad)
     got = lax.all_to_all(sent, torus, split_axis=0, concat_axis=0, tiled=True)
     told = expert(got, w_in, w_out)
     told = lax.all_to_all(told, torus, split_axis=0, concat_axis=0, tiled=True)

time: 64.2 us -> 63.7 us (level)
  no operation moved by 1% of the time
where the time goes in v10:
time: 63.7 us; the launch traced here: 63.5 us
  blocking collectives  42.4 us (67%)
  Pallas kernels  13.4 us (21%)
  starting transfers between devices  4.76 us (7%)
  waiting for transfers between devices  2.12 us (3%)
  between operations  0.7 us (1%)
    all_to_all x1, blocking collectives, shards(): got = lax.all_to_all(sent, torus, split_axis=0, concat_axis=0, tiled=True)  25.2 us
    all_to_all x1, blocking collectives, shards(): told = lax.all_to_all(told, torus, split_axis=0, concat_axis=0, tiled=True)  17.3 us
    pallas_call x6, Pallas kernels, call(): pl.pallas_call(kernel, in_specs=specs, out_specs=out_specs, out_shape=out...  13.3 us
    ppermute x1, starting transfers between devices, shards(): pair = lax.ppermute(told, 'core', swap)  3.16 us
    ppermute x1, starting transfers between devices, shards(): taken = lax.ppermute(given, 'core', swap)  1.5 us
  transfers between devices with their start and end apart: 3, of which 3 were waited for; matrix products, arithmetic and copies ran while one was open for 0% of the time, Pallas kernels for 3%

profile of v10, /device:TPU:1, one launch (start us, length us, event | category | flops | bytes accessed | tf_op | source)
XLA Modules:
  0.0 63.5 jit_solution(3798081311967985416)
XLA Ops:
  0.6 0.1 pad_add_fusion.at_ref
  0.7 3.1 %opening.1 = (bf16[128,1408]{1,0:T(8,128)(2,1)S(1)}, bf16[128,512]{1,0:T(8,128)(2,1)S(1)}, f32[128,128]{1,0:T(8,128)S(1)}, f32[256,512]{1,0:T(8,128)S(1)}, bf16[...) custom-call(s32[2]{0:T(128)S(1)} %pad_add_fusion.at_ref, ...), custom_call_target="tpu_custom_call" | custom-call | tf_op jit(solution)/shard_map/opening/pallas_call | solution.py:57
  3.8 1.5 %collective-permute-start = (bf16[128,1408]{1,0:T(8,128)(2,1)S(1)}, bf16[128,1408]{1,0:T(8,128)(2,1)S(1)}, u32[]{:S(2)}, u32[]{:S(2)}) collective-permute-start(bf16[128,1408]{1,0:T(8,128)(2,1)S(1)} %get-tuple-element.21), channel_id=1, source_target_pairs={{0,4},{4,0},{1,5},{5,1},{2,6},{6,2},{3,7},{7,3},{8,12},{12,8},{9,1... | collective-permute-start | bytes 1081352 | tf_op jit(solution)/shard_map/ppermute | solution.py:359
  5.3 0.5 grads.1
  5.8 0.1 collective-permute-start.1
  5.9 0.7 %collective-permute-done.taken_ref = bf16[128,1408]{1,0:T(8,128)(2,1)S(1)} collective-permute-done((bf16[128,1408]{1,0:T(8,128)(2,1)S(1)}, bf16[128,1408]{1,0:T(8,128)(2,1)S(1)}, u32[]{:S(2)}, u32[]{:S(2)}) %collective-permute-start) | collective-permute-done | bytes 360480 | tf_op jit(solution)/shard_map/ppermute | solution.py:359
  6.6 0.0 slice-start
  6.6 0.0 slice-start.2
  6.6 0.5 merge_slots.1
  7.2 0.3 collective-permute-done.1.taken_ref
  7.5 0.0 slice-start.1
  7.5 0.0 slice-start.3
  7.5 0.1 merge_grads.1
  7.6 25.2 %all_to_all.10.got_ref = bf16[64,2,2688]{2,1,0:T(2,128)(2,1)S(1)} all-to-all(bf16[64,2,2688]{2,1,0:T(2,128)(2,1)S(1)} %merge_grads.1), channel_id=1, replica_groups=mesh['x'=4,'z'=4,'core'=2,'exp'=4] {'x','z','exp'}, dimensions={0} | all-to-all | bytes 1376256 | tf_op jit(solution)/shard_map/all_to_all | solution.py:365
  32.8 0.0 slice-done
  32.8 0.0 slice-done.2
  32.8 0.0 slice-done.1
  32.8 0.0 slice-done.3
  32.8 5.6 %expert.1 = bf16[64,2,2688]{2,1,0:T(2,128)(2,1)S(1)} custom-call(bf16[64,2,2688]{2,1,0:T(2,128)(2,1)S(1)} %all_to_all.10.got_ref, bf16[1,1280,2560]{2,1,0:T(8,128)(2,1)S(1)} %bitcast.3, bf16[1,2560,1280]{2,1,0:T(8,128)(2,1)S(1)} %bitcast.5), custom_call_target="tpu_custom_call" | custom-call | tf_op jit(solution)/shard_map/expert/pallas_call | solution.py:57
  38.4 17.3 %all_to_all.11.mine_ref = bf16[64,2,2688]{2,1,0:T(2,128)(2,1)S(1)} all-to-all(bf16[64,2,2688]{2,1,0:T(2,128)(2,1)S(1)} %expert.1), channel_id=1, replica_groups=mesh['x'=4,'z'=4,'core'=2,'exp'=4] {'x','z','exp'}, dimensions={0} | all-to-all | bytes 1376256 | tf_op jit(solution)/shard_map/all_to_all | solution.py:367
  55.7 3.2 %collective-permute-start.2 = (bf16[64,2,2688]{2,1,0:T(2,128)(2,1)S(1)}, bf16[64,2,2688]{2,1,0:T(2,128)(2,1)S(1)}, u32[]{:S(2)}, u32[]{:S(2)}) collective-permute-start(bf16[64,2,2688]{2,1,0:T(2,128)(2,1)S(1)} %all_to_all.11.mine_ref), channel_id=1, source_target_pairs={{0,4},{4,0},{1,5},{5,1},{2,6},{6,2},{3,7},{7,3},{8,12},{12,8},{9,1... | collective-permute-start | bytes 2064392 | tf_op jit(solution)/shard_map/ppermute | solution.py:368
  58.9 0.7 %combining.1 = (f32[512,256]{1,0:T(8,128)S(1)}, f32[512,256]{1,0:T(8,128)S(1)}) custom-call(bf16[512,1280]{1,0:T(8,128)(2,1)S(1)} %get-tuple-element.20.rows_ref.tok_ref, bf16[256,1280]{1,0:T(8,128)(2,1)S(1)} %get-tuple-element.25.order_ref), custom_call_target="tpu_custom_call" | custom-call | flops 1000000000 | bytes 4000000 | tf_op jit(solution)/shard_map/combining/pallas_call | solution.py:57
  59.6 1.1 %collective-permute-done.2.pair_ref = bf16[64,2,2688]{2,1,0:T(2,128)(2,1)S(1)} collective-permute-done((bf16[64,2,2688]{2,1,0:T(2,128)(2,1)S(1)}, bf16[64,2,2688]{2,1,0:T(2,128)(2,1)S(1)}, u32[]{:S(2)}, u32[]{:S(2)}) %collective-permute-start.2) | collective-permute-done | bytes 688160 | tf_op jit(solution)/shard_map/ppermute | solution.py:368
  60.6 2.9 %closing.1 = (bf16[512,1280]{1,0:T(8,128)(2,1)}, bf16[512,1280]{1,0:T(8,128)(2,1)}) custom-call(bf16[64,2,2688]{2,1,0:T(2,128)(2,1)S(1)} %all_to_all.11.mine_ref, bf16[64,2,2688]{2,1,0:T(2,128)(2,1)S(1)} %collective-permute-done.2.pair_ref, bf16[512,1280]{1,0:T(8,128)(2,1)S(1)} %get-tuple-element.20.rows_ref.tok_ref, ...), custom_call_target="tpu_custom_call" | custom-call | tf_op jit(solution)/shard_map/closing/pallas_call | solution.py:57
  (2 shorter events, 0.0 us)
Async XLA Ops:
  3.8 2.8 %collective-permute-start = (bf16[128,1408]{1,0:T(8,128)(2,1)S(1)}, bf16[128,1408]{1,0:T(8,128)(2,1)S(1)}, u32[]{:S(2)}, u32[]{:S(2)}) collective-permute-start(bf16[128,1408]{1,0:T(8,128)(2,1)S(1)} %get-tuple-element.21), channel_id=1, source_target_pairs={{0,4},{4,0},{1,5},{5,1},{2,6},{6,2},{3,7},{7,3},{8,12},{12,8},{9,1... | collective-permute-start | bytes 1081352 | tf_op jit(solution)/shard_map/ppermute | solution.py:359
  5.8 1.7 %collective-permute-start.1 = (bf16[128,1280]{1,0:T(8,128)(2,1)S(1)}, bf16[128,1280]{1,0:T(8,128)(2,1)S(1)}, u32[]{:S(2)}, u32[]{:S(2)}) collective-permute-start(bf16[128,1280]{1,0:T(8,128)(2,1)S(1)} %get-tuple-element.24), channel_id=1, source_target_pairs={{0,4},{4,0},{1,5},{5,1},{2,6},{6,2},{3,7},{7,3},{8,12},{12,8},{9,1... | collective-permute-start | bytes 983048 | tf_op jit(solution)/shard_map/ppermute | solution.py:361
  6.6 26.2 %slice-start = ((s8[6553600]{0:T(1024)(128)(4,1)}), s8[4194304]{0:T(1024)(128)(4,1)S(1)}, s32[]{:S(2)}) async-start(s8[6553600]{0:T(1024)(128)(4,1)} %bitcast.2), calls=%async_computation.2 | async-start | bytes 8388608
  6.6 26.2 %slice-start.2 = ((s8[6553600]{0:T(1024)(128)(4,1)}), s8[2359296]{0:T(1024)(128)(4,1)S(1)}, s32[]{:S(2)}) async-start(s8[6553600]{0:T(1024)(128)(4,1)} %bitcast.4), calls=%async_computation.4 | async-start | bytes 4718592
  7.5 25.3 %slice-start.1 = ((s8[6553600]{0:T(1024)(128)(4,1)}), s8[2359296]{0:T(1024)(128)(4,1)S(1)}, s32[]{:S(2)}) async-start(s8[6553600]{0:T(1024)(128)(4,1)} %bitcast.2), calls=%async_computation.3 | async-start | bytes 4718592
  7.5 25.3 %slice-start.3 = ((s8[6553600]{0:T(1024)(128)(4,1)}), s8[4194304]{0:T(1024)(128)(4,1)S(1)}, s32[]{:S(2)}) async-start(s8[6553600]{0:T(1024)(128)(4,1)} %bitcast.4), calls=%async_computation.5 | async-start | bytes 8388608
  55.7 4.9 %collective-permute-start.2 = (bf16[64,2,2688]{2,1,0:T(2,128)(2,1)S(1)}, bf16[64,2,2688]{2,1,0:T(2,128)(2,1)S(1)}, u32[]{:S(2)}, u32[]{:S(2)}) collective-permute-start(bf16[64,2,2688]{2,1,0:T(2,128)(2,1)S(1)} %all_to_all.11.mine_ref), channel_id=1, source_target_pairs={{0,4},{4,0},{1,5},{5,1},{2,6},{6,2},{3,7},{7,3},{8,12},{12,8},{9,1... | collective-permute-start | bytes 2064392 | tf_op jit(solution)/shard_map/ppermute | solution.py:368

commit v11 on v10

--- a/solution.py
+++ b/solution.py
@@ -91,10 +91,11 @@
         source = tok_hbm.at[pl.ds(start + at * block, block)]
         loads.append(pltpu.make_async_copy(source, rows_ref.at[part], sems.at[1 + at]))
     loads.append(pltpu.make_async_copy(cot_hbm, cot_ref, sems.at[5]))
-    for copy in loads:
+    for copy in loads[:5]:
         copy.start()
     order = ordering(at_ref[1], slots)
     loads[0].wait()
+    loads[5].start()
     weight = product(order, weight_ref[...], 1, 1).astype(LOW)
     order_ref[...] = weight
     for copy in loads[1:5]:

time: 63.7 us -> 63.7 us (level)
  no operation moved by 1% of the time
where the time goes in v11:
time: 63.7 us; the launch traced here: 63.5 us
  blocking collectives  42.4 us (67%)
  Pallas kernels  13.4 us (21%)
  starting transfers between devices  4.76 us (7%)
  waiting for transfers between devices  2.11 us (3%)
  between operations  0.7 us (1%)
    all_to_all x1, blocking collectives, shards(): got = lax.all_to_all(sent, torus, split_axis=0, concat_axis=0, tiled=True)  25.2 us
    all_to_all x1, blocking collectives, shards(): told = lax.all_to_all(told, torus, split_axis=0, concat_axis=0, tiled=True)  17.3 us
    pallas_call x6, Pallas kernels, call(): pl.pallas_call(kernel, in_specs=specs, out_specs=out_specs, out_shape=out...  13.3 us
    ppermute x1, starting transfers between devices, shards(): pair = lax.ppermute(told, 'core', swap)  3.16 us
    ppermute x1, starting transfers between devices, shards(): taken = lax.ppermute(given, 'core', swap)  1.5 us
  transfers between devices with their start and end apart: 3, of which 3 were waited for; matrix products, arithmetic and copies ran while one was open for 0% of the time, Pallas kernels for 3%

profile of v11, /device:TPU:1, one launch (start us, length us, event | category | flops | bytes accessed | tf_op | source)
XLA Modules:
  0.0 63.5 jit_solution(14321001624525097942)
XLA Ops:
  0.6 0.1 pad_add_fusion.at_ref
  0.7 3.1 %opening.1 = (bf16[128,1408]{1,0:T(8,128)(2,1)S(1)}, bf16[128,512]{1,0:T(8,128)(2,1)S(1)}, f32[128,128]{1,0:T(8,128)S(1)}, f32[256,512]{1,0:T(8,128)S(1)}, bf16[...) custom-call(s32[2]{0:T(128)S(1)} %pad_add_fusion.at_ref, ...), custom_call_target="tpu_custom_call" | custom-call | tf_op jit(solution)/shard_map/opening/pallas_call | solution.py:57
  3.8 1.5 %collective-permute-start = (bf16[128,1408]{1,0:T(8,128)(2,1)S(1)}, bf16[128,1408]{1,0:T(8,128)(2,1)S(1)}, u32[]{:S(2)}, u32[]{:S(2)}) collective-permute-start(bf16[128,1408]{1,0:T(8,128)(2,1)S(1)} %get-tuple-element.21), channel_id=1, source_target_pairs={{0,4},{4,0},{1,5},{5,1},{2,6},{6,2},{3,7},{7,3},{8,12},{12,8},{9,1... | collective-permute-start | bytes 1081352 | tf_op jit(solution)/shard_map/ppermute | solution.py:360
  5.3 0.5 grads.1
  5.8 0.1 collective-permute-start.1
  5.9 0.7 %collective-permute-done.taken_ref = bf16[128,1408]{1,0:T(8,128)(2,1)S(1)} collective-permute-done((bf16[128,1408]{1,0:T(8,128)(2,1)S(1)}, bf16[128,1408]{1,0:T(8,128)(2,1)S(1)}, u32[]{:S(2)}, u32[]{:S(2)}) %collective-permute-start) | collective-permute-done | bytes 360480 | tf_op jit(solution)/shard_map/ppermute | solution.py:360
  6.6 0.0 slice-start
  6.6 0.0 slice-start.2
  6.6 0.5 merge_slots.1
  7.2 0.3 collective-permute-done.1.taken_ref
  7.5 0.0 slice-start.1
  7.5 0.0 slice-start.3
  7.5 0.1 merge_grads.1
  7.6 25.2 %all_to_all.10.got_ref = bf16[64,2,2688]{2,1,0:T(2,128)(2,1)S(1)} all-to-all(bf16[64,2,2688]{2,1,0:T(2,128)(2,1)S(1)} %merge_grads.1), channel_id=1, replica_groups=mesh['x'=4,'z'=4,'core'=2,'exp'=4] {'x','z','exp'}, dimensions={0} | all-to-all | bytes 1376256 | tf_op jit(solution)/shard_map/all_to_all | solution.py:366
  32.8 0.0 slice-done
  32.8 0.0 slice-done.2
  32.8 0.0 slice-done.1
  32.8 0.0 slice-done.3
  32.8 5.6 %expert.1 = bf16[64,2,2688]{2,1,0:T(2,128)(2,1)S(1)} custom-call(bf16[64,2,2688]{2,1,0:T(2,128)(2,1)S(1)} %all_to_all.10.got_ref, bf16[1,1280,2560]{2,1,0:T(8,128)(2,1)S(1)} %bitcast.3, bf16[1,2560,1280]{2,1,0:T(8,128)(2,1)S(1)} %bitcast.5), custom_call_target="tpu_custom_call" | custom-call | tf_op jit(solution)/shard_map/expert/pallas_call | solution.py:57
  38.4 17.3 %all_to_all.11.mine_ref = bf16[64,2,2688]{2,1,0:T(2,128)(2,1)S(1)} all-to-all(bf16[64,2,2688]{2,1,0:T(2,128)(2,1)S(1)} %expert.1), channel_id=1, replica_groups=mesh['x'=4,'z'=4,'core'=2,'exp'=4] {'x','z','exp'}, dimensions={0} | all-to-all | bytes 1376256 | tf_op jit(solution)/shard_map/all_to_all | solution.py:368
  55.7 3.2 %collective-permute-start.2 = (bf16[64,2,2688]{2,1,0:T(2,128)(2,1)S(1)}, bf16[64,2,2688]{2,1,0:T(2,128)(2,1)S(1)}, u32[]{:S(2)}, u32[]{:S(2)}) collective-permute-start(bf16[64,2,2688]{2,1,0:T(2,128)(2,1)S(1)} %all_to_all.11.mine_ref), channel_id=1, source_target_pairs={{0,4},{4,0},{1,5},{5,1},{2,6},{6,2},{3,7},{7,3},{8,12},{12,8},{9,1... | collective-permute-start | bytes 2064392 | tf_op jit(solution)/shard_map/ppermute | solution.py:369
  58.9 0.7 %combining.1 = (f32[512,256]{1,0:T(8,128)S(1)}, f32[512,256]{1,0:T(8,128)S(1)}) custom-call(bf16[512,1280]{1,0:T(8,128)(2,1)S(1)} %get-tuple-element.20.rows_ref.tok_ref, bf16[256,1280]{1,0:T(8,128)(2,1)S(1)} %get-tuple-element.25.order_ref), custom_call_target="tpu_custom_call" | custom-call | flops 1000000000 | bytes 4000000 | tf_op jit(solution)/shard_map/combining/pallas_call | solution.py:57
  59.6 1.1 %collective-permute-done.2.pair_ref = bf16[64,2,2688]{2,1,0:T(2,128)(2,1)S(1)} collective-permute-done((bf16[64,2,2688]{2,1,0:T(2,128)(2,1)S(1)}, bf16[64,2,2688]{2,1,0:T(2,128)(2,1)S(1)}, u32[]{:S(2)}, u32[]{:S(2)}) %collective-permute-start.2) | collective-permute-done | bytes 688160 | tf_op jit(solution)/shard_map/ppermute | solution.py:369
  60.6 2.9 %closing.1 = (bf16[512,1280]{1,0:T(8,128)(2,1)}, bf16[512,1280]{1,0:T(8,128)(2,1)}) custom-call(bf16[64,2,2688]{2,1,0:T(2,128)(2,1)S(1)} %all_to_all.11.mine_ref, bf16[64,2,2688]{2,1,0:T(2,128)(2,1)S(1)} %collective-permute-done.2.pair_ref, bf16[512,1280]{1,0:T(8,128)(2,1)S(1)} %get-tuple-element.20.rows_ref.tok_ref, ...), custom_call_target="tpu_custom_call" | custom-call | tf_op jit(solution)/shard_map/closing/pallas_call | solution.py:57
  (2 shorter events, 0.0 us)
Async XLA Ops:
  3.8 2.8 %collective-permute-start = (bf16[128,1408]{1,0:T(8,128)(2,1)S(1)}, bf16[128,1408]{1,0:T(8,128)(2,1)S(1)}, u32[]{:S(2)}, u32[]{:S(2)}) collective-permute-start(bf16[128,1408]{1,0:T(8,128)(2,1)S(1)} %get-tuple-element.21), channel_id=1, source_target_pairs={{0,4},{4,0},{1,5},{5,1},{2,6},{6,2},{3,7},{7,3},{8,12},{12,8},{9,1... | collective-permute-start | bytes 1081352 | tf_op jit(solution)/shard_map/ppermute | solution.py:360
  5.8 1.7 %collective-permute-start.1 = (bf16[128,1280]{1,0:T(8,128)(2,1)S(1)}, bf16[128,1280]{1,0:T(8,128)(2,1)S(1)}, u32[]{:S(2)}, u32[]{:S(2)}) collective-permute-start(bf16[128,1280]{1,0:T(8,128)(2,1)S(1)} %get-tuple-element.24), channel_id=1, source_target_pairs={{0,4},{4,0},{1,5},{5,1},{2,6},{6,2},{3,7},{7,3},{8,12},{12,8},{9,1... | collective-permute-start | bytes 983048 | tf_op jit(solution)/shard_map/ppermute | solution.py:362
  6.6 26.2 %slice-start = ((s8[6553600]{0:T(1024)(128)(4,1)}), s8[4194304]{0:T(1024)(128)(4,1)S(1)}, s32[]{:S(2)}) async-start(s8[6553600]{0:T(1024)(128)(4,1)} %bitcast.2), calls=%async_computation.2 | async-start | bytes 8388608
  6.6 26.2 %slice-start.2 = ((s8[6553600]{0:T(1024)(128)(4,1)}), s8[2359296]{0:T(1024)(128)(4,1)S(1)}, s32[]{:S(2)}) async-start(s8[6553600]{0:T(1024)(128)(4,1)} %bitcast.4), calls=%async_computation.4 | async-start | bytes 4718592
  7.5 25.3 %slice-start.1 = ((s8[6553600]{0:T(1024)(128)(4,1)}), s8[2359296]{0:T(1024)(128)(4,1)S(1)}, s32[]{:S(2)}) async-start(s8[6553600]{0:T(1024)(128)(4,1)} %bitcast.2), calls=%async_computation.3 | async-start | bytes 4718592
  7.5 25.3 %slice-start.3 = ((s8[6553600]{0:T(1024)(128)(4,1)}), s8[4194304]{0:T(1024)(128)(4,1)S(1)}, s32[]{:S(2)}) async-start(s8[6553600]{0:T(1024)(128)(4,1)} %bitcast.4), calls=%async_computation.5 | async-start | bytes 8388608
  55.7 4.9 %collective-permute-start.2 = (bf16[64,2,2688]{2,1,0:T(2,128)(2,1)S(1)}, bf16[64,2,2688]{2,1,0:T(2,128)(2,1)S(1)}, u32[]{:S(2)}, u32[]{:S(2)}) collective-permute-start(bf16[64,2,2688]{2,1,0:T(2,128)(2,1)S(1)} %all_to_all.11.mine_ref), channel_id=1, source_target_pairs={{0,4},{4,0},{1,5},{5,1},{2,6},{6,2},{3,7},{7,3},{8,12},{12,8},{9,1... | collective-permute-start | bytes 2064392 | tf_op jit(solution)/shard_map/ppermute | solution.py:369

commit v12 on v11

--- a/solution.py
+++ b/solution.py
@@ -167,22 +167,29 @@
     )
 
 
-def merge_slots_kernel(
-    shift_ref, piece_ref, comb_ref, rows_ref, cot_ref, taken_ref, out_ref, grad_ref
-):
+def kept_kernel(shift_ref, comb_ref, rows_ref, cot_ref, slot_ref, grad_ref):
+    slot_ref[...] = product(shift_ref[...], rows_ref[...], 1, 0)
+    grad_ref[...] = product(comb_ref[...], cot_ref[...], 1, 0)
+
+
+def kept_sums(shifted, combine, rows, cotangent):
+    shape = jax.ShapeDtypeStruct((shifted.shape[0], rows.shape[1]), WIDE)
+    args = (shifted, combine, rows, cotangent)
+    return call(kept_kernel, "kept", args, [IN_VMEM] * 4, [IN_VMEM] * 2, [shape] * 2, (), SIDE)
+
+
+def merge_slots_kernel(kept_ref, piece_ref, taken_ref, out_ref):
     peers, own, wide = out_ref.shape
-    width = rows_ref.shape[1]
+    width = kept_ref.shape[1]
     kept, taken = piece_ref[...], taken_ref[:, width:].astype(WIDE)
     kept_max, taken_max = lanes(kept, 0), lanes(taken, 0)
     top = jnp.maximum(kept_max, taken_max)
     kept_scale, taken_scale = jnp.exp(kept_max - top), jnp.exp(taken_max - top)
     total = kept_scale * lanes(kept, 3) + taken_scale * lanes(taken, 3)
-    slots = kept_scale * product(shift_ref[...], rows_ref[...], 1, 0)
-    slots += taken_scale * taken_ref[:, :width].astype(WIDE)
+    slots = kept_scale * kept_ref[...] + taken_scale * taken_ref[:, :width].astype(WIDE)
     pieces = place(split3(top) + split3(total), kept.shape, 1)
     out_ref[:, :, :width] = slots.astype(LOW).reshape(peers, own, width)
     out_ref[:, :, wide - EXTRA :] = pieces.astype(LOW).reshape(peers, own, EXTRA)
-    grad_ref[...] = product(comb_ref[...], cot_ref[...], 1, 0)
 
 
 def merge_grads_kernel(sent_ref, kept_ref, taken_ref, out_ref):
@@ -192,16 +199,11 @@
     out_ref[:, :, width : 2 * width] = grads.astype(LOW).reshape(peers, own, width)
 
 
-def merge_slots(shifted, pieces, combine, rows, cotangent, taken, peers):
-    half, width = shifted.shape[0], rows.shape[1]
-    args = (shifted, pieces, combine, rows, cotangent, taken)
-    shapes = [
-        jax.ShapeDtypeStruct((peers, half // peers, taken.shape[1] + width), LOW),
-        jax.ShapeDtypeStruct((half, width), WIDE),
-    ]
-    return call(
-        merge_slots_kernel, "merge_slots", args, [IN_VMEM] * 6, [IN_VMEM] * 2, shapes, (), SIDE
-    )
+def merge_slots(kept, pieces, taken, peers):
+    half, width = kept.shape
+    shape = jax.ShapeDtypeStruct((peers, half // peers, taken.shape[1] + width), LOW)
+    args = (kept, pieces, taken)
+    return call(merge_slots_kernel, "merge_slots", args, [IN_VMEM] * 3, IN_VMEM, shape, (), SIDE)
 
 
 def merge_grads(sent, kept, taken):
@@ -361,8 +363,8 @@
     given_grad, kept_combine = grads_of(columns, cot)
     taken_grad = lax.ppermute(given_grad, "core", swap)
     logits, combine = combining(rows, weight)
-    sent, kept_grad = merge_slots(shifted, pieces, kept_combine, rows, cot, taken, peers)
-    sent = merge_grads(sent, kept_grad, taken_grad)
+    kept, kept_grad = kept_sums(shifted, kept_combine, rows, cot)
+    sent = merge_grads(merge_slots(kept, pieces, taken, peers), kept_grad, taken_grad)
     got = lax.all_to_all(sent, torus, split_axis=0, concat_axis=0, tiled=True)
     told = expert(got, w_in, w_out)
     told = lax.all_to_all(told, torus, split_axis=0, concat_axis=0, tiled=True)

time: 63.7 us -> 63.7 us (level)
    pallas_call x6 -> x7, Pallas kernels: 13.3 us -> 13.6 us  [call(): pl.pallas_call(kernel, in_specs=specs, out_specs=out_specs, out_shape=out...]
where the time goes in v12:
time: 63.7 us; the launch traced here: 63.5 us
  blocking collectives  42.4 us (67%)
  Pallas kernels  13.7 us (22%)
  starting transfers between devices  4.76 us (7%)
  waiting for transfers between devices  1.83 us (3%)
  between operations  0.71 us (1%)
    all_to_all x1, blocking collectives, shards(): got = lax.all_to_all(sent, torus, split_axis=0, concat_axis=0, tiled=True)  25.2 us
    all_to_all x1, blocking collectives, shards(): told = lax.all_to_all(told, torus, split_axis=0, concat_axis=0, tiled=True)  17.3 us
    pallas_call x7, Pallas kernels, call(): pl.pallas_call(kernel, in_specs=specs, out_specs=out_specs, out_shape=out...  13.6 us
    ppermute x1, starting transfers between devices, shards(): pair = lax.ppermute(told, 'core', swap)  3.16 us
    ppermute x1, starting transfers between devices, shards(): taken = lax.ppermute(given, 'core', swap)  1.5 us
  transfers between devices with their start and end apart: 3, of which 3 were waited for; matrix products, arithmetic and copies ran while one was open for 0% of the time, Pallas kernels for 3%

profile of v12, /device:TPU:1, one launch (start us, length us, event | category | flops | bytes accessed | tf_op | source)
XLA Modules:
  0.0 63.5 jit_solution(1680610108006522927)
XLA Ops:
  0.6 0.1 pad_add_fusion.at_ref
  0.7 3.1 %opening.1 = (bf16[128,1408]{1,0:T(8,128)(2,1)S(1)}, bf16[128,512]{1,0:T(8,128)(2,1)S(1)}, f32[128,128]{1,0:T(8,128)S(1)}, f32[256,512]{1,0:T(8,128)S(1)}, bf16[...) custom-call(s32[2]{0:T(128)S(1)} %pad_add_fusion.at_ref, ...), custom_call_target="tpu_custom_call" | custom-call | tf_op jit(solution)/shard_map/opening/pallas_call | solution.py:57
  3.8 1.5 %collective-permute-start = (bf16[128,1408]{1,0:T(8,128)(2,1)S(1)}, bf16[128,1408]{1,0:T(8,128)(2,1)S(1)}, u32[]{:S(2)}, u32[]{:S(2)}) collective-permute-start(bf16[128,1408]{1,0:T(8,128)(2,1)S(1)} %get-tuple-element.22), channel_id=1, source_target_pairs={{0,4},{4,0},{1,5},{5,1},{2,6},{6,2},{3,7},{7,3},{8,12},{12,8},{9,1... | collective-permute-start | bytes 1081352 | tf_op jit(solution)/shard_map/ppermute | solution.py:362
  5.3 0.5 grads.1
  5.8 0.1 collective-permute-start.1
  5.9 0.5 kept.1
  6.4 0.2 collective-permute-done.taken_ref
  6.6 0.0 slice-start
  6.6 0.0 slice-start.2
  6.6 0.3 merge_slots.1.sent_ref
  6.9 0.5 collective-permute-done.1.taken_ref
  7.5 0.0 slice-start.3
  7.5 0.1 merge_grads.1
  7.6 25.2 %all_to_all.10.got_ref = bf16[64,2,2688]{2,1,0:T(2,128)(2,1)S(1)} all-to-all(bf16[64,2,2688]{2,1,0:T(2,128)(2,1)S(1)} %merge_grads.1), channel_id=1, replica_groups=mesh['x'=4,'z'=4,'core'=2,'exp'=4] {'x','z','exp'}, dimensions={0} | all-to-all | bytes 1376256 | tf_op jit(solution)/shard_map/all_to_all | solution.py:368
  32.8 0.0 slice-done
  32.8 0.0 slice-done.2
  32.8 0.0 slice-done.1
  32.8 0.0 slice-done.3
  32.8 5.6 %expert.1 = bf16[64,2,2688]{2,1,0:T(2,128)(2,1)S(1)} custom-call(bf16[64,2,2688]{2,1,0:T(2,128)(2,1)S(1)} %all_to_all.10.got_ref, bf16[1,1280,2560]{2,1,0:T(8,128)(2,1)S(1)} %bitcast.3, bf16[1,2560,1280]{2,1,0:T(8,128)(2,1)S(1)} %bitcast.5), custom_call_target="tpu_custom_call" | custom-call | tf_op jit(solution)/shard_map/expert/pallas_call | solution.py:57
  38.4 17.3 %all_to_all.11.mine_ref = bf16[64,2,2688]{2,1,0:T(2,128)(2,1)S(1)} all-to-all(bf16[64,2,2688]{2,1,0:T(2,128)(2,1)S(1)} %expert.1), channel_id=1, replica_groups=mesh['x'=4,'z'=4,'core'=2,'exp'=4] {'x','z','exp'}, dimensions={0} | all-to-all | bytes 1376256 | tf_op jit(solution)/shard_map/all_to_all | solution.py:370
  55.7 3.2 %collective-permute-start.2 = (bf16[64,2,2688]{2,1,0:T(2,128)(2,1)S(1)}, bf16[64,2,2688]{2,1,0:T(2,128)(2,1)S(1)}, u32[]{:S(2)}, u32[]{:S(2)}) collective-permute-start(bf16[64,2,2688]{2,1,0:T(2,128)(2,1)S(1)} %all_to_all.11.mine_ref), channel_id=1, source_target_pairs={{0,4},{4,0},{1,5},{5,1},{2,6},{6,2},{3,7},{7,3},{8,12},{12,8},{9,1... | collective-permute-start | bytes 2064392 | tf_op jit(solution)/shard_map/ppermute | solution.py:371
  58.9 0.7 %combining.1 = (f32[512,256]{1,0:T(8,128)S(1)}, f32[512,256]{1,0:T(8,128)S(1)}) custom-call(bf16[512,1280]{1,0:T(8,128)(2,1)S(1)} %get-tuple-element.19.rows_ref.tok_ref, bf16[256,1280]{1,0:T(8,128)(2,1)S(1)} %get-tuple-element.25.order_ref), custom_call_target="tpu_custom_call" | custom-call | flops 1000000000 | bytes 4000000 | tf_op jit(solution)/shard_map/combining/pallas_call | solution.py:57
  59.6 1.1 %collective-permute-done.2.pair_ref = bf16[64,2,2688]{2,1,0:T(2,128)(2,1)S(1)} collective-permute-done((bf16[64,2,2688]{2,1,0:T(2,128)(2,1)S(1)}, bf16[64,2,2688]{2,1,0:T(2,128)(2,1)S(1)}, u32[]{:S(2)}, u32[]{:S(2)}) %collective-permute-start.2) | collective-permute-done | bytes 688160 | tf_op jit(solution)/shard_map/ppermute | solution.py:371
  60.6 2.9 %closing.1 = (bf16[512,1280]{1,0:T(8,128)(2,1)}, bf16[512,1280]{1,0:T(8,128)(2,1)}) custom-call(bf16[64,2,2688]{2,1,0:T(2,128)(2,1)S(1)} %all_to_all.11.mine_ref, bf16[64,2,2688]{2,1,0:T(2,128)(2,1)S(1)} %collective-permute-done.2.pair_ref, bf16[512,1280]{1,0:T(8,128)(2,1)S(1)} %get-tuple-element.19.rows_ref.tok_ref, ...), custom_call_target="tpu_custom_call" | custom-call | tf_op jit(solution)/shard_map/closing/pallas_call | solution.py:57
  (3 shorter events, 0.0 us)
Async XLA Ops:
  3.8 2.8 %collective-permute-start = (bf16[128,1408]{1,0:T(8,128)(2,1)S(1)}, bf16[128,1408]{1,0:T(8,128)(2,1)S(1)}, u32[]{:S(2)}, u32[]{:S(2)}) collective-permute-start(bf16[128,1408]{1,0:T(8,128)(2,1)S(1)} %get-tuple-element.22), channel_id=1, source_target_pairs={{0,4},{4,0},{1,5},{5,1},{2,6},{6,2},{3,7},{7,3},{8,12},{12,8},{9,1... | collective-permute-start | bytes 1081352 | tf_op jit(solution)/shard_map/ppermute | solution.py:362
  5.8 1.7 %collective-permute-start.1 = (bf16[128,1280]{1,0:T(8,128)(2,1)S(1)}, bf16[128,1280]{1,0:T(8,128)(2,1)S(1)}, u32[]{:S(2)}, u32[]{:S(2)}) collective-permute-start(bf16[128,1280]{1,0:T(8,128)(2,1)S(1)} %get-tuple-element.24), channel_id=1, source_target_pairs={{0,4},{4,0},{1,5},{5,1},{2,6},{6,2},{3,7},{7,3},{8,12},{12,8},{9,1... | collective-permute-start | bytes 983048 | tf_op jit(solution)/shard_map/ppermute | solution.py:364
  6.6 26.2 %slice-start = ((s8[6553600]{0:T(1024)(128)(4,1)}), s8[4194304]{0:T(1024)(128)(4,1)S(1)}, s32[]{:S(2)}) async-start(s8[6553600]{0:T(1024)(128)(4,1)} %bitcast.2), calls=%async_computation.2 | async-start | bytes 8388608
  6.6 26.2 %slice-start.2 = ((s8[6553600]{0:T(1024)(128)(4,1)}), s8[2359296]{0:T(1024)(128)(4,1)S(1)}, s32[]{:S(2)}) async-start(s8[6553600]{0:T(1024)(128)(4,1)} %bitcast.4), calls=%async_computation.4 | async-start | bytes 4718592
  7.5 25.3 %slice-start.1 = ((s8[6553600]{0:T(1024)(128)(4,1)}), s8[2359296]{0:T(1024)(128)(4,1)S(1)}, s32[]{:S(2)}) async-start(s8[6553600]{0:T(1024)(128)(4,1)} %bitcast.2), calls=%async_computation.3 | async-start | bytes 4718592
  7.5 25.3 %slice-start.3 = ((s8[6553600]{0:T(1024)(128)(4,1)}), s8[4194304]{0:T(1024)(128)(4,1)S(1)}, s32[]{:S(2)}) async-start(s8[6553600]{0:T(1024)(128)(4,1)} %bitcast.4), calls=%async_computation.5 | async-start | bytes 8388608
  55.7 4.9 %collective-permute-start.2 = (bf16[64,2,2688]{2,1,0:T(2,128)(2,1)S(1)}, bf16[64,2,2688]{2,1,0:T(2,128)(2,1)S(1)}, u32[]{:S(2)}, u32[]{:S(2)}) collective-permute-start(bf16[64,2,2688]{2,1,0:T(2,128)(2,1)S(1)} %all_to_all.11.mine_ref), channel_id=1, source_target_pairs={{0,4},{4,0},{1,5},{5,1},{2,6},{6,2},{3,7},{7,3},{8,12},{12,8},{9,1... | collective-permute-start | bytes 2064392 | tf_op jit(solution)/shard_map/ppermute | solution.py:371
